TPU v7x, 32 devices: a whole 2x2x4 slice. The times are simulated.
32 devices in a mesh: blk: 8 (over z, x), ulysses: 4 (over y, core).
Axes of the slice: x: 2, y: 2, z: 4, core: 2. Of those that a mesh axis runs over, the one named last changes fastest.
Arguments:
- tokens: bfloat16 [2, 2048, 2048], P(None, ('blk', 'ulysses')), may hold values from -6 to 6
- attn_gain: bfloat16 [2048], P('blk'), may hold values from 0.25 to 1.75
- w_query: bfloat16 [2048, 3072], P('blk', 'ulysses'), may hold values from -0.125 to 0.125
- w_latent: bfloat16 [2048, 576], P('blk'), may hold values from -0.125 to 0.125
- latent_gain: bfloat16 [512], P('blk'), may hold values from 0.25 to 1.75
- w_expand: bfloat16 [512, 4096], P('blk', 'ulysses'), may hold values from -0.25 to 0.25
- w_output: bfloat16 [2048, 2048], P('ulysses', 'blk'), may hold values from -2 to 2
- ffn_gain: bfloat16 [2048], P('blk'), may hold values from 0.25 to 1.75
- w_router: bfloat16 [2048, 64], P('blk'), may hold values from -0.0625 to 0.0625
- w_shared_gate: bfloat16 [2048, 2816], P('blk', 'ulysses'), may hold values from -0.125 to 0.125
- w_shared_up: bfloat16 [2048, 2816], P('blk', 'ulysses'), may hold values from -0.125 to 0.125
- w_shared_down: bfloat16 [2816, 2048], P('ulysses', 'blk'), may hold values from -0.15625 to 0.15625
- w_gate: bfloat16 [64, 2048, 1408], P(('blk', 'ulysses')), may hold values from -0.125 to 0.125
- w_up: bfloat16 [64, 2048, 1408], P(('blk', 'ulysses')), may hold values from -0.125 to 0.125
- w_down: bfloat16 [64, 1408, 2048], P(('blk', 'ulysses')), may hold values from -0.3125 to 0.3125
- routes: int32 [2048, 2, 6], P(('blk', 'ulysses')), may hold values from 0 to 63, all different within a row; in each aligned block of 128 rows (0 to 127, 128 to 255, ..., all dimensions but the last counted through in order) at most 14 rows name the same one
- clip_limit: float32 [1], replicated, may hold values from 1 to 2
- out_grad: bfloat16 [2, 2048, 2048], P(None, ('blk', 'ulysses')), may hold values from -6 to 6
Outputs:
- block_out: bfloat16 [2, 2048, 2048], P(None, ('blk', 'ulysses'))
- tokens_grad: bfloat16 [2, 2048, 2048], P(None, ('blk', 'ulysses'))
- attn_gain_grad: float32 [2048], P('blk')
- w_query_grad: float32 [2048, 3072], P('blk', 'ulysses')
- w_latent_grad: float32 [2048, 576], P('blk')
- latent_gain_grad: float32 [512], P('blk')
- w_expand_grad: float32 [512, 4096], P('blk', 'ulysses')
- w_output_grad: float32 [2048, 2048], P('ulysses', 'blk')
- ffn_gain_grad: float32 [2048], P('blk')
- w_router_grad: float32 [2048, 64], P('blk')
- w_shared_gate_grad: float32 [2048, 2816], P('blk', 'ulysses')
- w_shared_up_grad: float32 [2048, 2816], P('blk', 'ulysses')
- w_shared_down_grad: float32 [2816, 2048], P('ulysses', 'blk')
- w_gate_grad: float32 [64, 2048, 1408], P(('blk', 'ulysses'))
- w_up_grad: float32 [64, 2048, 1408], P(('blk', 'ulysses'))
- w_down_grad: float32 [64, 1408, 2048], P(('blk', 'ulysses'))
- clip_factor: float32 [16], P('ulysses')
Inputs may be any that keep to these rules, and one draw needn't show every extreme that they name: `routes`: among the rows of one device no expert is named more than 14 times, a bound that some block reaches; the 6 experts of a row differ.
All inputs are finite; a program needn't handle non-finite values.
Results may differ from a plain program's by a relative error of at most 0.017.
Values may be sent and summed in bfloat16 or wider, within the bound.
A program may use at most 448 MiB of HBM per device.

v0:
```python
import jax
import jax.numpy as jnp
from jax import lax
from jax.sharding import PartitionSpec as P

H = 16
NOPE = 128
RD = 64
VH = 128
KVR = 512
EXPERTS = 64
TOP = 6
CAP = 14


epsilon = 1e-06
rope_base = 10000.0
wide_type = jnp.float32
narrow_type = jnp.bfloat16


def norm_rows(values, gain):
    inverse = lax.rsqrt(jnp.mean(values * values, axis=-1, keepdims=True) + epsilon)
    normed = values * inverse
    return (normed * gain, normed, inverse)


def norm_input_back(grad_out, normed, inverse, gain):
    scaled = grad_out * gain
    return inverse * (scaled - normed * jnp.mean(scaled * normed, axis=-1, keepdims=True))


def rotary_tables(positions):
    half_width = RD // 2
    frequency = rope_base ** (-2.0 * jnp.arange(half_width).astype(jnp.float32) / RD)
    angles = positions.astype(jnp.float32)[:, None] * frequency[None, :]
    return (jnp.cos(angles), jnp.sin(angles))


def rotate(values, cosine, sine_table):
    half_width = RD // 2
    first_half = values[..., :half_width]
    second_half = values[..., half_width:]
    return jnp.concatenate(
        [
            first_half * cosine - second_half * sine_table,
            second_half * cosine + first_half * sine_table,
        ],
        axis=-1,
    )


def unrotate(gradient, cosine, sine_table):
    half_width = RD // 2
    first_half = gradient[..., :half_width]
    second_half = gradient[..., half_width:]
    return jnp.concatenate(
        [
            first_half * cosine + second_half * sine_table,
            second_half * cosine - first_half * sine_table,
        ],
        axis=-1,
    )


def silu_slope(values):
    sigmoid_value = jax.nn.sigmoid(values)
    return sigmoid_value * (1.0 + values * (1.0 - sigmoid_value))


def slot_tables(route_rows):
    flat_routes = route_rows.reshape(-1)
    onehot = (flat_routes[:, None] == jnp.arange(EXPERTS, dtype=jnp.int32)[None, :]).astype(
        jnp.int32
    )
    slot_rank = jnp.sum((jnp.cumsum(onehot, axis=0) - 1) * onehot, axis=1)
    position = flat_routes * CAP + slot_rank
    entries = flat_routes.shape[0]
    slot_pick = (
        jnp.full((EXPERTS * CAP,), entries, jnp.int32)
        .at[position]
        .set(jnp.arange(entries, dtype=jnp.int32))
    )
    return (position, slot_pick)


def spread_units(slot_values, unit_split, features):
    shaped = slot_values.reshape(EXPERTS, 1, CAP, features)
    return jnp.broadcast_to(shaped, (EXPERTS, unit_split, CAP, features)).reshape(
        EXPERTS * unit_split, CAP, features
    )


def join_units(unit_values, unit_split, features):
    return jnp.sum(unit_values.reshape(EXPERTS, unit_split, CAP, features), axis=1).reshape(
        EXPERTS * CAP, features
    )


def to_units(values):
    return lax.all_to_all(values, ("blk", "ulysses"), split_axis=0, concat_axis=1, tiled=True)


def from_units(values):
    return lax.all_to_all(values, ("blk", "ulysses"), split_axis=1, concat_axis=0, tiled=True)


def per_device(
    tokens,
    attn_gain,
    w_query,
    w_latent,
    latent_gain,
    w_expand,
    w_output,
    ffn_gain,
    w_router,
    w_shared_gate,
    w_shared_up,
    w_shared_down,
    w_gate,
    w_up,
    w_down,
    routes,
    clip_limit,
    out_grad,
):
    seq_count, local_len, features = tokens.shape
    row_count = seq_count * local_len
    qk_width = NOPE + RD
    kv_width = qk_width + VH
    ulysses_size = lax.axis_size("ulysses")
    blk_size = lax.axis_size("blk")
    heads_here = H // ulysses_size
    group_rows = ulysses_size * local_len
    group_count = seq_count * group_rows
    device_count = lax.axis_size(("blk", "ulysses"))
    unit_split = w_gate.shape[0] * device_count // EXPERTS
    score_scale = qk_width ** (-0.5)
    full_len = group_rows * blk_size
    block_number = lax.axis_index("blk")
    own_start = lax.axis_index("ulysses") * local_len

    def own_rows(values):
        width = values.shape[-1]
        shaped = values.reshape(seq_count, group_rows, width)
        return lax.dynamic_slice_in_dim(shaped, own_start, local_len, 1).reshape(row_count, width)

    gathered = (
        lax.all_gather(attn_gain, "blk", axis=0, tiled=True),
        lax.all_gather(w_query, "blk", axis=0, tiled=True),
        lax.all_gather(w_latent, "blk", axis=0, tiled=True),
        lax.all_gather(latent_gain, "blk", axis=0, tiled=True),
        lax.all_gather(w_expand, "blk", axis=0, tiled=True),
        lax.all_gather(w_output, "blk", axis=1, tiled=True),
        lax.all_gather(ffn_gain, "blk", axis=0, tiled=True),
        lax.all_gather(w_router, "blk", axis=0, tiled=True),
        lax.all_gather(w_shared_gate, "blk", axis=0, tiled=True),
        lax.all_gather(w_shared_up, "blk", axis=0, tiled=True),
        lax.all_gather(w_shared_down, "blk", axis=1, tiled=True),
    )
    (
        gain_attn_raw,
        part_query,
        whole_latent,
        gain_latent_raw,
        part_expand,
        part_output,
        gain_ffn_raw,
        whole_router,
        part_gate,
        part_up,
        part_down,
    ) = gathered
    gain_attn = gain_attn_raw.astype(wide_type)
    gain_latent = gain_latent_raw.astype(wide_type)
    gain_ffn = gain_ffn_raw.astype(wide_type)
    group_pos = jnp.tile(
        block_number * group_rows + jnp.arange(group_rows, dtype=jnp.int32), seq_count
    )
    local_pos = jnp.tile(
        block_number * group_rows + own_start + jnp.arange(local_len, dtype=jnp.int32), seq_count
    )
    cosine_group, sine_group = rotary_tables(group_pos)
    cosine_local, sine_local = rotary_tables(local_pos)
    inputs = tokens.astype(wide_type).reshape(row_count, features)
    scaled_in, normed_in, inverse_in = norm_rows(inputs, gain_attn)
    hidden_local = scaled_in.astype(narrow_type)
    latent_all = jnp.dot(hidden_local, whole_latent, preferred_element_type=wide_type)
    scaled_lat, normed_lat, inverse_lat = norm_rows(latent_all[:, :KVR], gain_latent)
    latent_local = scaled_lat.astype(narrow_type)
    rope_local = rotate(latent_all[:, KVR:], cosine_local, sine_local).astype(narrow_type)
    tokens_group, grad_group, latent_group, rope_group = (
        lax.all_gather(tokens, "ulysses", axis=1, tiled=True),
        lax.all_gather(out_grad, "ulysses", axis=1, tiled=True),
        lax.all_gather(
            latent_local.reshape(seq_count, local_len, KVR), "ulysses", axis=1, tiled=True
        ),
        lax.all_gather(rope_local.reshape(seq_count, local_len, RD), "ulysses", axis=1, tiled=True),
    )
    inputs_group = tokens_group.astype(wide_type).reshape(group_count, features)
    hidden_group = norm_rows(inputs_group, gain_attn)[0].astype(narrow_type)
    latent_rows = latent_group.reshape(group_count, KVR)
    rope_rows = rope_group.reshape(group_count, RD)
    query_lin = jnp.dot(hidden_group, part_query, preferred_element_type=wide_type).reshape(
        group_count, heads_here, qk_width
    )
    query_rows = jnp.concatenate(
        [
            query_lin[..., :NOPE],
            rotate(query_lin[..., NOPE:], cosine_group[:, None, :], sine_group[:, None, :]),
        ],
        axis=-1,
    ).astype(narrow_type)
    expanded = jnp.dot(latent_rows, part_expand, preferred_element_type=wide_type).reshape(
        group_count, heads_here, NOPE + VH
    )
    rope_wide = jnp.broadcast_to(
        rope_rows.astype(wide_type)[:, None, :], (group_count, heads_here, RD)
    )
    packed_rows = jnp.concatenate(
        [expanded[..., :NOPE], rope_wide, expanded[..., NOPE:]], axis=-1
    ).astype(narrow_type)
    query_four = query_rows.reshape(seq_count, group_rows, heads_here, qk_width)
    packed_head = packed_rows.reshape(seq_count, group_rows, heads_here * kv_width)
    all_keys = lax.all_gather(packed_head, "blk", axis=1, tiled=True)
    query_pos = block_number * group_rows + jnp.arange(group_rows, dtype=jnp.int32)
    last_query = block_number * group_rows + group_rows - 1

    def raw_scores(key_block, offset):
        scores = (
            jnp.einsum("sqhc,skhc->shqk", query_four, key_block, preferred_element_type=wide_type)
            * score_scale
        )
        allowed = (offset + jnp.arange(group_rows, dtype=jnp.int32))[None, :] <= query_pos[:, None]
        return (scores, allowed)

    def guarded(update, running, pieces, offset):
        return lax.cond(
            offset > last_query, lambda: running, lambda: update(running, pieces, offset)
        )

    def over_keys(update, carried):

        def visit_block(counter, running):
            offset = counter * group_rows
            pieces = lax.dynamic_slice_in_dim(all_keys, offset, group_rows, 1)
            return guarded(update, running, pieces, offset)

        return lax.fori_loop(0, blk_size, visit_block, carried)

    def stats_update(running, pieces, offset):
        maxima, totals = running
        packed_four = pieces.reshape(seq_count, group_rows, heads_here, kv_width)
        scores, allowed = raw_scores(packed_four[..., :qk_width], offset)
        masked = jnp.where(allowed, scores, -jnp.inf)
        new_max = jnp.maximum(maxima, jnp.max(masked, axis=-1))
        totals = totals * jnp.exp(maxima - new_max) + jnp.sum(
            jnp.where(allowed, jnp.exp(masked - new_max[..., None]), 0.0), axis=-1
        )
        return (new_max, totals)

    start_max = jnp.full((seq_count, heads_here, group_rows), -1e30, wide_type)
    maxima, totals = over_keys(stats_update, (start_max, jnp.zeros_like(start_max)))
    log_sum = maxima + jnp.log(totals)
    head_top = lax.pmax(jnp.max(maxima, axis=(0, 2)), "blk")
    clip_value = clip_limit[0]
    clip_factor = clip_value / jnp.maximum(head_top, clip_value)

    def value_update(running, pieces, offset):
        packed_four = pieces.reshape(seq_count, group_rows, heads_here, kv_width)
        scores, allowed = raw_scores(packed_four[..., :qk_width], offset)
        probability = jnp.where(allowed, jnp.exp(scores - log_sum[..., None]), 0.0).astype(
            narrow_type
        )
        return running + jnp.einsum(
            "shqk,skhd->shqd",
            probability,
            packed_four[..., qk_width:],
            preferred_element_type=wide_type,
        )

    attention = over_keys(
        value_update, jnp.zeros((seq_count, heads_here, group_rows, VH), wide_type)
    )
    attended = (
        jnp.swapaxes(attention, 1, 2).reshape(group_count, heads_here * VH).astype(narrow_type)
    )
    attn_partial = jnp.dot(attended, part_output, preferred_element_type=wide_type)
    attn_total = lax.psum(attn_partial, "ulysses")
    residual_group = inputs_group + attn_total
    scaled_mid_group, normed_mid_group, inverse_mid_group = norm_rows(residual_group, gain_ffn)
    hidden_mid_group = scaled_mid_group.astype(narrow_type)
    hidden_mid = own_rows(hidden_mid_group)
    residual_local = own_rows(residual_group)
    logits = jnp.dot(hidden_mid, whole_router, preferred_element_type=wide_type)
    route_rows = jnp.swapaxes(routes, 0, 1).reshape(row_count, TOP)
    choose = (route_rows[..., None] == jnp.arange(EXPERTS, dtype=jnp.int32)).astype(wide_type)
    gate_weights = jax.nn.softmax(jnp.sum(choose * logits[:, None, :], axis=-1), axis=-1)
    shared_gate = jnp.dot(hidden_mid_group, part_gate, preferred_element_type=wide_type)
    shared_up = jnp.dot(hidden_mid_group, part_up, preferred_element_type=wide_type)
    shared_act = (jax.nn.silu(shared_gate) * shared_up).astype(narrow_type)
    shared_partial = jnp.dot(shared_act, part_down, preferred_element_type=wide_type)
    shared_local = lax.psum_scatter(
        shared_partial.reshape(seq_count, group_rows, features),
        "ulysses",
        scatter_dimension=1,
        tiled=True,
    ).reshape(row_count, features)
    position, slot_pick = slot_tables(route_rows)
    slot_rows = slot_pick // TOP
    padded_mid = jnp.concatenate([hidden_mid, jnp.zeros((1, features), narrow_type)], axis=0)
    received = to_units(spread_units(padded_mid[slot_rows], unit_split, features))
    unit_gate = jnp.einsum("umd,udf->umf", received, w_gate, preferred_element_type=wide_type)
    unit_up = jnp.einsum("umd,udf->umf", received, w_up, preferred_element_type=wide_type)
    unit_act = (jax.nn.silu(unit_gate) * unit_up).astype(narrow_type)
    unit_out = jnp.einsum("umf,ufd->umd", unit_act, w_down, preferred_element_type=wide_type)
    expert_rows = join_units(from_units(unit_out), unit_split, features)[position].reshape(
        row_count, TOP, features
    )
    routed = jnp.sum(gate_weights[..., None] * expert_rows, axis=1)
    block_out = (
        (residual_local + shared_local + routed)
        .astype(narrow_type)
        .reshape(seq_count, local_len, features)
    )
    grad_narrow = out_grad.reshape(row_count, features)
    grad_wide = grad_narrow.astype(wide_type)
    gate_grad = jnp.sum(expert_rows * grad_wide[:, None, :], axis=-1)
    chosen_grad = gate_weights * (
        gate_grad - jnp.sum(gate_weights * gate_grad, axis=-1, keepdims=True)
    )
    logit_grad = jnp.sum(choose * chosen_grad[..., None], axis=1).astype(narrow_type)
    router_wgrad = jnp.einsum("rd,re->de", hidden_mid, logit_grad, preferred_element_type=wide_type)
    mid_local = jnp.einsum("re,de->rd", logit_grad, whole_router, preferred_element_type=wide_type)
    grad_rows = grad_group.reshape(group_count, features)
    shared_act_grad = jnp.einsum(
        "rd,fd->rf", grad_rows, part_down, preferred_element_type=wide_type
    )
    shared_down_wgrad = jnp.einsum(
        "rf,rd->fd", shared_act, grad_rows, preferred_element_type=wide_type
    )
    shared_gate_grad = (shared_act_grad * shared_up * silu_slope(shared_gate)).astype(narrow_type)
    shared_up_grad = (shared_act_grad * jax.nn.silu(shared_gate)).astype(narrow_type)
    shared_gate_wgrad = jnp.einsum(
        "rd,rf->df", hidden_mid_group, shared_gate_grad, preferred_element_type=wide_type
    )
    shared_up_wgrad = jnp.einsum(
        "rd,rf->df", hidden_mid_group, shared_up_grad, preferred_element_type=wide_type
    )
    mid_shared = jnp.einsum(
        "rf,df->rd", shared_gate_grad, part_gate, preferred_element_type=wide_type
    ) + jnp.einsum("rf,df->rd", shared_up_grad, part_up, preferred_element_type=wide_type)
    route_grad = (
        (gate_weights[..., None] * grad_wide[:, None, :])
        .astype(narrow_type)
        .reshape(row_count * TOP, features)
    )
    padded_grad = jnp.concatenate([route_grad, jnp.zeros((1, features), narrow_type)], axis=0)
    unit_grad = to_units(spread_units(padded_grad[slot_pick], unit_split, features))
    act_grad = jnp.einsum("umd,ufd->umf", unit_grad, w_down, preferred_element_type=wide_type)
    down_wgrad = jnp.einsum("umf,umd->ufd", unit_act, unit_grad, preferred_element_type=wide_type)
    lin_gate_grad = (act_grad * unit_up * silu_slope(unit_gate)).astype(narrow_type)
    lin_up_grad = (act_grad * jax.nn.silu(unit_gate)).astype(narrow_type)
    gate_wgrad = jnp.einsum(
        "umd,umf->udf", received, lin_gate_grad, preferred_element_type=wide_type
    )
    up_wgrad = jnp.einsum("umd,umf->udf", received, lin_up_grad, preferred_element_type=wide_type)
    unit_in_grad = jnp.einsum(
        "umf,udf->umd", lin_gate_grad, w_gate, preferred_element_type=wide_type
    ) + jnp.einsum("umf,udf->umd", lin_up_grad, w_up, preferred_element_type=wide_type)
    returned = join_units(from_units(unit_in_grad), unit_split, features)
    mid_local = (
        mid_local
        + jnp.zeros((row_count + 1, features), wide_type).at[slot_rows].add(returned)[:row_count]
    )
    width = mid_local.shape[-1]
    empty = jnp.zeros((seq_count, group_rows, width), mid_local.dtype)
    mid_group = lax.psum(
        mid_shared
        + lax.dynamic_update_slice_in_dim(
            empty, mid_local.reshape(seq_count, local_len, width), own_start, 1
        ).reshape(group_count, width),
        "ulysses",
    )
    mid_in_grad = norm_input_back(mid_group, normed_mid_group, inverse_mid_group, gain_ffn)
    ffn_gain_grad = jnp.sum(own_rows(mid_group) * own_rows(normed_mid_group), axis=0)
    residual_grad_group = grad_rows.astype(wide_type) + mid_in_grad
    attn_grad = residual_grad_group.astype(narrow_type)
    output_wgrad = jnp.einsum("ro,rd->od", attended, attn_grad, preferred_element_type=wide_type)
    attended_grad = jnp.einsum(
        "rd,od->ro", attn_grad, part_output, preferred_element_type=wide_type
    ).astype(narrow_type)
    grad_four = attended_grad.reshape(seq_count, group_rows, heads_here, VH)
    row_delta = jnp.einsum("sqhd,shqd->shq", grad_four, attention, preferred_element_type=wide_type)

    def grad_update(running, pieces, offset):
        query_acc, key_acc = running
        packed_four = pieces.reshape(seq_count, group_rows, heads_here, kv_width)
        scores, allowed = raw_scores(packed_four[..., :qk_width], offset)
        probability = jnp.where(allowed, jnp.exp(scores - log_sum[..., None]), 0.0)
        prob_narrow = probability.astype(narrow_type)
        prob_grad = jnp.einsum(
            "sqhd,skhd->shqk",
            grad_four,
            packed_four[..., qk_width:],
            preferred_element_type=wide_type,
        )
        score_grad = (probability * (prob_grad - row_delta[..., None]) * score_scale).astype(
            narrow_type
        )
        query_acc = query_acc + jnp.einsum(
            "shqk,skhc->sqhc",
            score_grad,
            packed_four[..., :qk_width],
            preferred_element_type=wide_type,
        )
        key_part = jnp.einsum(
            "shqk,sqhc->skhc", score_grad, query_four, preferred_element_type=wide_type
        )
        value_part = jnp.einsum(
            "shqk,sqhd->skhd", prob_narrow, grad_four, preferred_element_type=wide_type
        )
        block_grad = jnp.concatenate([key_part, value_part], axis=-1).reshape(
            seq_count, group_rows, heads_here * kv_width
        )
        key_acc = lax.dynamic_update_slice_in_dim(key_acc, block_grad, offset, 1)
        return (query_acc, key_acc)

    start_grads = (
        jnp.zeros((seq_count, group_rows, heads_here, qk_width), wide_type),
        jnp.zeros((seq_count, full_len, heads_here * kv_width), wide_type),
    )
    query_acc, key_acc = over_keys(grad_update, start_grads)
    key_sums = lax.psum_scatter(key_acc, "blk", scatter_dimension=1, tiled=True).astype(narrow_type)
    query_back = (
        query_acc.astype(narrow_type).astype(wide_type).reshape(group_count, heads_here, qk_width)
    )
    query_lin_grad = (
        jnp.concatenate(
            [
                query_back[..., :NOPE],
                unrotate(query_back[..., NOPE:], cosine_group[:, None, :], sine_group[:, None, :]),
            ],
            axis=-1,
        )
        .reshape(group_count, heads_here * qk_width)
        .astype(narrow_type)
    )
    packed_back = key_sums.reshape(group_count, heads_here, kv_width)
    rope_partial = jnp.sum(packed_back[..., NOPE:qk_width].astype(wide_type), axis=1)
    expand_grad = jnp.concatenate(
        [packed_back[..., :NOPE], packed_back[..., qk_width:]], axis=-1
    ).reshape(group_count, heads_here * (NOPE + VH))
    expand_wgrad = jnp.einsum(
        "rk,re->ke", latent_rows, expand_grad, preferred_element_type=wide_type
    )
    query_wgrad = jnp.einsum(
        "rd,rq->dq", hidden_group, query_lin_grad, preferred_element_type=wide_type
    )
    latent_partial = jnp.einsum(
        "re,ke->rk", expand_grad, part_expand, preferred_element_type=wide_type
    )
    hidden_partial = jnp.einsum(
        "rq,dq->rd", query_lin_grad, part_query, preferred_element_type=wide_type
    )
    hidden_sum, latent_sum, rope_sum = (
        lax.psum_scatter(
            hidden_partial.reshape(seq_count, group_rows, features),
            "ulysses",
            scatter_dimension=1,
            tiled=True,
        ),
        lax.psum_scatter(
            latent_partial.reshape(seq_count, group_rows, KVR),
            "ulysses",
            scatter_dimension=1,
            tiled=True,
        ),
        lax.psum_scatter(
            rope_partial.reshape(seq_count, group_rows, RD),
            "ulysses",
            scatter_dimension=1,
            tiled=True,
        ),
    )
    latent_grad = latent_sum.reshape(row_count, KVR)
    key_rope_grad = unrotate(rope_sum.reshape(row_count, RD), cosine_local, sine_local)
    latent_in_grad = norm_input_back(latent_grad, normed_lat, inverse_lat, gain_latent)
    latent_gain_grad = jnp.sum(latent_grad * normed_lat, axis=0)
    latent_all_grad = jnp.concatenate([latent_in_grad, key_rope_grad], axis=-1).astype(narrow_type)
    latent_wgrad = jnp.einsum(
        "rd,rk->dk", hidden_local, latent_all_grad, preferred_element_type=wide_type
    )
    hidden_grad = hidden_sum.reshape(row_count, features) + jnp.einsum(
        "rk,dk->rd", latent_all_grad, whole_latent, preferred_element_type=wide_type
    )
    input_grad = norm_input_back(hidden_grad, normed_in, inverse_in, gain_attn)
    attn_gain_grad = jnp.sum(hidden_grad * normed_in, axis=0)
    tokens_grad = (
        (own_rows(residual_grad_group) + input_grad)
        .astype(narrow_type)
        .reshape(seq_count, local_len, features)
    )
    small_total = lax.psum(
        (attn_gain_grad, latent_wgrad, latent_gain_grad, ffn_gain_grad, router_wgrad), "ulysses"
    )
    summed = (
        lax.psum_scatter(small_total[0], "blk", scatter_dimension=0, tiled=True),
        lax.psum_scatter(query_wgrad, "blk", scatter_dimension=0, tiled=True),
        lax.psum_scatter(small_total[1], "blk", scatter_dimension=0, tiled=True),
        lax.psum_scatter(small_total[2], "blk", scatter_dimension=0, tiled=True),
        lax.psum_scatter(expand_wgrad, "blk", scatter_dimension=0, tiled=True),
        lax.psum_scatter(output_wgrad, "blk", scatter_dimension=1, tiled=True),
        lax.psum_scatter(small_total[3], "blk", scatter_dimension=0, tiled=True),
        lax.psum_scatter(small_total[4], "blk", scatter_dimension=0, tiled=True),
        lax.psum_scatter(shared_gate_wgrad, "blk", scatter_dimension=0, tiled=True),
        lax.psum_scatter(shared_up_wgrad, "blk", scatter_dimension=0, tiled=True),
        lax.psum_scatter(shared_down_wgrad, "blk", scatter_dimension=1, tiled=True),
    )
    return (
        block_out,
        tokens_grad,
        summed[0],
        summed[1],
        summed[2],
        summed[3],
        summed[4],
        summed[5],
        summed[6],
        summed[7],
        summed[8],
        summed[9],
        summed[10],
        gate_wgrad,
        up_wgrad,
        down_wgrad,
        clip_factor,
    )


def solution(mesh):
    return jax.shard_map(
        per_device,
        mesh=mesh,
        in_specs=(
            P(None, ("blk", "ulysses"), None),
            P("blk"),
            P("blk", "ulysses"),
            P("blk", None),
            P("blk"),
            P("blk", "ulysses"),
            P("ulysses", "blk"),
            P("blk"),
            P("blk", None),
            P("blk", "ulysses"),
            P("blk", "ulysses"),
            P("ulysses", "blk"),
            P(("blk", "ulysses"), None, None),
            P(("blk", "ulysses"), None, None),
            P(("blk", "ulysses"), None, None),
            P(("blk", "ulysses"), None, None),
            P(),
            P(None, ("blk", "ulysses"), None),
        ),
        out_specs=(
            P(None, ("blk", "ulysses"), None),
            P(None, ("blk", "ulysses"), None),
            P("blk"),
            P("blk", "ulysses"),
            P("blk", None),
            P("blk"),
            P("blk", "ulysses"),
            P("ulysses", "blk"),
            P("blk"),
            P("blk", None),
            P("blk", "ulysses"),
            P("blk", "ulysses"),
            P("ulysses", "blk"),
            P(("blk", "ulysses"), None, None),
            P(("blk", "ulysses"), None, None),
            P(("blk", "ulysses"), None, None),
            P("ulysses"),
        ),
        check_vma=False,
    )
```

profile of v0, /device:TPU:0, one launch (start us, length us, event | category | flops | bytes accessed | tf_op | source)
XLA Modules:
  0.0 2818.1 jit_solution(7913898590772205291)
XLA Ops:
  10.7 22.2 all-gather
  37.1 17.3 all-reduce.2
  57.5 50.3 %all-gather.15.cloned.1.call-done = bf16[2048,576]{0,1:T(8,128)(2,1)} async-done(((bf16[256,576]{0,1:T(8,128)(2,1)}), bf16[2048,576]{0,1:T(8,128)(2,1)}) %all-gather.15.cloned.1.call-update) | async-done | bytes 2359312 | tf_op jit(solution)/shard_map/all_gather | solution.py:152
  111.9 5.4 all_gather.54
  117.5 10.6 all_gather.52
  135.9 59.7 %all-gather.21.cloned.1.call-done = bf16[2048,768]{1,0:T(8,128)(2,1)} async-done(((bf16[256,768]{1,0:T(8,128)(2,1)}), bf16[2048,768]{1,0:T(8,128)(2,1)}) %all-gather.21.cloned.1.call-update) | async-done | bytes 3145744 | tf_op jit(solution)/shard_map/all_gather | solution.py:151
  204.2 143.5 %all-gather.19.cloned.1.call-done = bf16[2,2048,1280]{1,2,0:T(8,128)(2,1)} async-done(((bf16[2,256,1280]{1,2,0:T(8,128)(2,1)}), bf16[2,2048,1280]{1,2,0:T(8,128)(2,1)}) %all-gather.19.cloned.1.call-update) | async-done | bytes 10485776 | tf_op jit(solution)/shard_map/all_gather | solution.py:226
  355.6 43.2 %all-gather.23.cloned.1.call-done = bf16[512,2048]{1,0:T(8,128)(2,1)} async-done(((bf16[512,256]{1,0:T(8,128)(2,1)}), bf16[512,2048]{1,0:T(8,128)(2,1)}) %all-gather.23.cloned.1.call-update) | async-done | bytes 2097168 | tf_op jit(solution)/shard_map/all_gather | solution.py:155
  404.9 17.7 all-gather.1
  428.8 58.8 %all-reduce.13.cloned.1.call-done = f32[512,2048]{1,0:T(8,128)} async-done(((f32[512,2048]{1,0:T(8,128)}), f32[512,2048]{1,0:T(8,128)}) %all-reduce.13.cloned.1.call-update) | async-done | bytes 4194320 | tf_op jit(solution)/shard_map/psum | solution.py:290
  500.1 6.0 reshape_reshape.7
  515.5 8.3 mul.525
  523.7 101.5 %all_gather.62 = bf16[2048,64]{0,1:T(8,128)(2,1)S(1)} all-gather(bf16[256,64]{0,1:T(8,128)(2,1)S(1)} %copy-done.65), channel_id=1, replica_groups=mesh['blk'=8,'ulysses'=4] {'blk'}, dimensions={0}, use_global_device_ids=true | all-gather | bytes 294912 | tf_op jit(solution)/shard_map/all_gather | solution.py:157
  636.2 6.0 reshape_reshape.8
  646.6 6.0 copy.298
  652.6 12.3 fusion.40
  665.0 11.5 fusion.38
  676.4 64.5 %all-to-all-done.2 = bf16[64,14,2048]{2,1,0:T(8,128)(2,1)} async-done(((bf16[64,14,2048]{2,1,0:T(8,128)(2,1)}), bf16[64,14,2048]{2,1,0:T(8,128)(2,1)}, u32[]{:S(2)}, u32[]{:S(2)}) %all-to-all-start.2) | async-done | bytes 3670048 | tf_op jit(solution)/shard_map/all_to_all | solution.py:101
  741.0 7.8 copy.300
  748.8 17.8 multiply_convert_fusion.1
  766.6 12.3 fusion.99
  778.9 11.8 copy.266
  797.2 9.0 fusion.101
  806.2 11.7 convolution_add_fusion
  817.9 11.8 copy.274
  829.6 197.6 %all-to-all-done.1 = f32[2,448,2048]{2,0,1:T(2,128)} async-done(((f32[2,448,2048]{2,0,1:T(2,128)}), f32[2,448,2048]{2,0,1:T(2,128)}, u32[]{:S(2)}, u32[]{:S(2)}) %all-to-all-start.1) | async-done | bytes 7340064 | tf_op jit(solution)/shard_map/all_to_all | solution.py:105
  1042.3 49.6 %all-gather.31.cloned.1.call-done = bf16[2,256,2048]{2,1,0:T(8,128)(2,1)} async-done(((bf16[2,64,2048]{2,1,0:T(8,128)(2,1)}), bf16[2,256,2048]{2,1,0:T(8,128)(2,1)}) %all-gather.31.cloned.1.call-update) | async-done | bytes 2097168 | tf_op jit(solution)/shard_map/all_gather | solution.py:195
  1091.9 110.0 %all-gather.29.cloned.1.call-done = bf16[704,2048]{1,0:T(8,128)(2,1)} async-done(((bf16[704,256]{1,0:T(8,128)(2,1)}), bf16[704,2048]{1,0:T(8,128)(2,1)}) %all-gather.29.cloned.1.call-update) | async-done | bytes 2883600 | tf_op jit(solution)/shard_map/all_gather | solution.py:160
  1201.9 6.1 multiply_convert_fusion.6
  1211.8 13.2 copy.267
  1224.9 8.1 reshape.541
  1233.0 10.3 gather_fusion.1
  1243.3 7.8 reshape.542
  1251.1 13.0 copy.275
  1264.2 8.2 reshape.600
  1272.3 15.2 scatter_custom_fusion.1
  1287.6 7.3 multiply_reduce_fusion
  1302.7 87.9 %all-reduce.15.cloned.1.call-done = f32[512,2048]{1,0:T(8,128)} async-done(((f32[512,2048]{1,0:T(8,128)}), f32[512,2048]{1,0:T(8,128)}) %all-reduce.15.cloned.1.call-update) | async-done | bytes 4194320 | tf_op jit(solution)/shard_map/psum | solution.py:379
  1402.5 10.2 broadcast_in_dim.130
  1412.7 6.4 while.51
  1412.7 6.1 conditional.11
  1419.3 387.0 %reduce-scatter.20.cloned.1.call-done = f32[2,256,1280]{1,2,0:T(8,128)} async-done(((f32[2,2048,1280]{1,2,0:T(8,128)}), f32[2,256,1280]{1,2,0:T(8,128)}) %reduce-scatter.20.cloned.1.call-update) | async-done | bytes 2621456 | tf_op jit(solution)/shard_map/reduce_scatter | solution.py:435
  1808.2 9.1 copy.279
  1821.9 7.5 copy.302
  1829.4 7.5 reshape.626
  1842.8 5.9 fusion.97
  1850.3 5.7 fusion.32
  1862.5 21.3 reduce-scatter.22.cloned.1.call-done
  1890.9 5.8 fusion.105
  1909.9 5.4 fusion.47
  1923.5 21.2 pmax.7
  1948.8 17.7 fusion.36
  1966.6 13.0 fusion.34
  1979.6 12.1 fusion.28
  2001.4 33.1 %all-reduce.6 = (f32[2048]{0:T(1024)S(1)}, f32[512]{0:T(512)S(1)}, f32[2048]{0:T(1024)S(1)}) all-reduce(f32[2048]{0:T(1024)S(1)} %get-tuple-element.828, f32[512]{0:T(512)S(1)} %get-tuple-element.830, f32[2048]{0:T(1024)S(1)} %multiply_reduce_fusion.6), channel_id=7, replica_groups=mesh['blk'=8,'ulysses'=4] {'blk'}, use_global_device_ids=true, to_apply=%region_43.44.clone | all-reduce | flops 4608 | bytes 36864
  2034.7 6.6 all-reduce.7
  2044.0 98.8 %reduce-scatter.36.cloned.1.call-done = f32[256,576]{0,1:T(8,128)} async-done(((f32[2048,576]{0,1:T(8,128)}), f32[256,576]{0,1:T(8,128)}) %reduce-scatter.36.cloned.1.call-update) | async-done | bytes 589840 | tf_op jit(solution)/shard_map/reduce_scatter | solution.py:511
  2145.5 111.9 %reduce-scatter.30.cloned.1.call-done = f32[256,704]{0,1:T(8,128)} async-done(((f32[2048,704]{0,1:T(8,128)}), f32[256,704]{0,1:T(8,128)}) %reduce-scatter.30.cloned.1.call-update) | async-done | bytes 720912 | tf_op jit(solution)/shard_map/reduce_scatter | solution.py:517
  2257.5 114.9 %reduce-scatter.32.cloned.1.call-done = f32[256,704]{0,1:T(8,128)} async-done(((f32[2048,704]{0,1:T(8,128)}), f32[256,704]{0,1:T(8,128)}) %reduce-scatter.32.cloned.1.call-update) | async-done | bytes 720912 | tf_op jit(solution)/shard_map/reduce_scatter | solution.py:518
  2372.3 114.9 %reduce-scatter.34.cloned.1.call-done = f32[704,256]{1,0:T(8,128)} async-done(((f32[704,2048]{1,0:T(8,128)}), f32[704,256]{1,0:T(8,128)}) %reduce-scatter.34.cloned.1.call-update) | async-done | bytes 720912 | tf_op jit(solution)/shard_map/reduce_scatter | solution.py:519
  2487.2 92.9 %reduce-scatter.28.cloned.1.call-done = f32[512,256]{1,0:T(8,128)} async-done(((f32[512,2048]{1,0:T(8,128)}), f32[512,256]{1,0:T(8,128)}) %reduce-scatter.28.cloned.1.call-update) | async-done | bytes 524304 | tf_op jit(solution)/shard_map/reduce_scatter | solution.py:514
  2580.1 121.7 %reduce-scatter.24.cloned.1.call-done = f32[256,768]{1,0:T(8,128)} async-done(((f32[2048,768]{1,0:T(8,128)}), f32[256,768]{1,0:T(8,128)}) %reduce-scatter.24.cloned.1.call-update) | async-done | bytes 786448 | tf_op jit(solution)/shard_map/reduce_scatter | solution.py:510
  2701.8 70.9 %reduce-scatter.26.cloned.1.call-done = f32[64,1024]{1,0:T(8,128)} async-done(((f32[512,1024]{1,0:T(8,128)}), f32[64,1024]{1,0:T(8,128)}) %reduce-scatter.26.cloned.1.call-update) | async-done | bytes 262160 | tf_op jit(solution)/shard_map/reduce_scatter | solution.py:513
  2772.7 35.3 %all-reduce.17.cloned.1.call-done = (f32[256,576]{0,1:T(8,128)}, f32[256,64]{0,1:T(8,128)}) async-done(((f32[256,576]{0,1:T(8,128)}, f32[256,64]{0,1:T(8,128)}), (f32[256,576]{0,1:T(8,128)}, f32[256,64]{0,1:T(8,128)})) %all-reduce.17.cloned.1.call-update) | async-done | bytes 655376 | tf_op jit(solution)/shard_map/psum | solution.py:505
  (476 shorter events, 219.0 us)
Async XLA Ops:
  7.2 48.7 %all-gather.17.cloned.1.call-start = ((), (), s32[]{:S(2)}) async-start(), calls=%async_computation.19 | async-start | bytes 1179648 | tf_op jit(solution)/shard_map/all_gather | solution.py:154
  7.9 100.0 %all-gather.15.cloned.1.call-start = ((), (), s32[]{:S(2)}) async-start(), calls=%async_computation.18 | async-start | bytes 2654208 | tf_op jit(solution)/shard_map/all_gather | solution.py:152
  8.7 124.4 %all-gather.13.cloned.1.call-start = ((), (), s32[]{:S(2)}) async-start(), calls=%async_computation.17 | async-start | bytes 2621440 | tf_op jit(solution)/shard_map/all_gather | solution.py:194
  9.4 186.2 %all-gather.21.cloned.1.call-start = ((), (), s32[]{:S(2)}) async-start(), calls=%async_computation.21 | async-start | bytes 3538944 | tf_op jit(solution)/shard_map/all_gather | solution.py:151
  10.0 337.7 %all-gather.19.cloned.1.call-start = ((), (), s32[]{:S(2)}) async-start(), calls=%async_computation.20 | async-start | bytes 11796480 | tf_op jit(solution)/shard_map/all_gather | solution.py:226
  33.0 102.4 %copy-start.54 = (f32[8,1,256]{2,1,0:T(1,128)}, f32[8,1,256]{2,1,0:T(1,128)S(1)}, u32[]{:S(2)}) copy-start(f32[8,1,256]{2,1,0:T(1,128)S(1)} %convert_element_type.252) | copy-start | bytes 24580
  34.3 23.2 copy-start.75
  54.5 56.0 %copy-start.63 = (f32[512]{0:T(512)}, f32[512]{0:T(512)S(1)}, u32[]{:S(2)}) copy-start(f32[512]{0:T(512)S(1)} %convert_element_type.213) | copy-start | bytes 6148
  54.6 56.7 %copy-start.81 = (f32[128]{0:T(128)}, f32[128]{0:T(128)S(1)}, u32[]{:S(2)}) copy-start(f32[128]{0:T(128)S(1)} %convert_element_type.216) | copy-start | bytes 1540
  54.6 77.0 %copy-start.77 = (f32[32]{0:T(128)}, f32[32]{0:T(128)S(1)}, u32[]{:S(2)}) copy-start(f32[32]{0:T(128)S(1)} %multiply_power_fusion) | copy-start | bytes 388
  55.8 55.3 %copy-start.33 = (bf16[128,2048]{1,0:T(8,128)(2,1)}, bf16[128,2048]{1,0:T(8,128)(2,1)S(1)}, u32[]{:S(2)}) copy-start(bf16[128,2048]{1,0:T(8,128)(2,1)S(1)} %multiply_convert_fusion.9) | copy-start | bytes 1572868
  110.3 18.6 copy-start.26
  130.7 268.2 %all-gather.23.cloned.1.call-start = ((), (), s32[]{:S(2)}) async-start(), calls=%async_computation.22 | async-start | bytes 2359296 | tf_op jit(solution)/shard_map/all_gather | solution.py:155
  131.3 356.4 %all-reduce.13.cloned.1.call-start = ((), (), s32[]{:S(2)}) async-start(), calls=%async_computation.23 | async-start | bytes 8388608 | tf_op jit(solution)/shard_map/psum | solution.py:290
  131.9 72.1 %copy-start.48 = (f32[512,32]{0,1:T(8,128)}, f32[512,32]{0,1:T(8,128)S(1)}, u32[]{:S(2)}) copy-start(f32[512,32]{0,1:T(8,128)S(1)} %get-tuple-element.922) | copy-start | bytes 196612
  131.9 72.1 %copy-start.50 = (f32[512,32]{0,1:T(8,128)}, f32[512,32]{0,1:T(8,128)S(1)}, u32[]{:S(2)}) copy-start(f32[512,32]{0,1:T(8,128)S(1)} %get-tuple-element.923) | copy-start | bytes 196612
  135.9 64.3 %copy-start.16 = (bf16[2,256,2048]{2,1,0:T(8,128)(2,1)}, bf16[2,256,2048]{2,1,0:T(8,128)(2,1)S(1)}, u32[]{:S(2)}) copy-start(bf16[2,256,2048]{2,1,0:T(8,128)(2,1)S(1)} %multiply_convert_fusion.5) | copy-start | bytes 6291460
  355.1 48.7 %copy-start.2 = (bf16[2,256,4,192]{1,3,2,0:T(8,128)(2,1)}, bf16[2,256,4,192]{1,3,2,0:T(8,128)(2,1)S(1)}, u32[]{:S(2)}) copy-start(bf16[2,256,4,192]{1,3,2,0:T(8,128)(2,1)S(1)} %get-tuple-element.1250) | copy-start | bytes 2359300
  355.1 48.6 %copy-start.19 = (f32[2,4,256,128]{3,2,1,0:T(8,128)}, f32[2,4,256,128]{3,2,1,0:T(8,128)S(1)}, u32[]{:S(2)}) copy-start(f32[2,4,256,128]{3,2,1,0:T(8,128)S(1)} %get-tuple-element.679) | copy-start | bytes 3145732
  355.1 48.6 %copy-start.73 = (f32[2,4,256]{2,1,0:T(4,128)}, f32[2,4,256]{2,1,0:T(4,128)S(1)}, u32[]{:S(2)}) copy-start(f32[2,4,256]{2,1,0:T(4,128)S(1)} %get-tuple-element.1319) | copy-start | bytes 24580
  355.6 48.1 %copy-start.28 = (bf16[2,256,4,128]{3,2,1,0:T(4,128)(2,1)}, bf16[2,256,4,128]{3,2,1,0:T(4,128)(2,1)S(1)}, u32[]{:S(2)}) copy-start(bf16[2,256,4,128]{3,2,1,0:T(4,128)(2,1)S(1)} %copy.256) | copy-start | bytes 1572868
  403.8 83.9 %copy-start.11 = (bf16[2,256,2048]{2,1,0:T(8,128)(2,1)S(1)}, bf16[2,256,2048]{2,1,0:T(8,128)(2,1)}, u32[]{:S(2)}) copy-start(bf16[2,256,2048]{2,1,0:T(8,128)(2,1)} %all-gather.13.cloned.1.call-done) | copy-start | bytes 6291460
  422.6 67.9 %copy-start.58 = (f32[8,1,256]{2,1,0:T(1,128)}, f32[8,1,256]{2,1,0:T(1,128)S(1)}, u32[]{:S(2)}) copy-start(f32[8,1,256]{2,1,0:T(1,128)S(1)} %convert_element_type.253) | copy-start | bytes 24580
  428.8 61.7 %copy-start.68 = (s32[896]{0:T(1024)}, s32[896]{0:T(1024)S(1)}, u32[]{:S(2)}) copy-start(s32[896]{0:T(1024)S(1)} %get-tuple-element.921) | copy-start | bytes 10756
  495.1 130.2 %copy-start.22 = (bf16[2,64,2048]{2,1,0:T(8,128)(2,1)}, bf16[2,64,2048]{2,1,0:T(8,128)(2,1)S(1)}, u32[]{:S(2)}) copy-start(bf16[2,64,2048]{2,1,0:T(8,128)(2,1)S(1)} %constant_dynamic-slice_fusion.4) | copy-start | bytes 1572868
  506.1 136.2 %all-to-all-start = ((bf16[64,14,2048]{2,1,0:T(8,128)(2,1)}), bf16[64,14,2048]{2,1,0:T(8,128)(2,1)}, u32[]{:S(2)}, u32[]{:S(2)}) async-start(bf16[64,14,2048]{2,1,0:T(8,128)(2,1)} %reshape_reshape.7), calls=%async_computation.1 | async-start | bytes 8388608 | tf_op jit(solution)/shard_map/all_to_all | solution.py:101
  511.0 114.5 %copy-start.61 = (s32[128,6]{0,1:T(8,128)}, s32[128,6]{0,1:T(8,128)S(1)}, u32[]{:S(2)}) copy-start(s32[128,6]{0,1:T(8,128)S(1)} %eq.40) | copy-start | bytes 9220
  642.2 98.7 %all-to-all-start.2 = ((bf16[64,14,2048]{2,1,0:T(8,128)(2,1)}), bf16[64,14,2048]{2,1,0:T(8,128)(2,1)}, u32[]{:S(2)}, u32[]{:S(2)}) async-start(bf16[64,14,2048]{2,1,0:T(8,128)(2,1)} %reshape_reshape.8), calls=%async_computation.3 | async-start | bytes 8388608 | tf_op jit(solution)/shard_map/all_to_all | solution.py:101
  766.6 30.6 %copy-start.12 = (bf16[2,448,1408]{2,1,0:T(8,128)(2,1)}, bf16[2,448,1408]{2,1,0:T(8,128)(2,1)S(1)}, u32[]{:S(2)}) copy-start(bf16[2,448,1408]{2,1,0:T(8,128)(2,1)S(1)} %get-tuple-element.901) | copy-start | bytes 7569412
  790.7 236.5 %all-to-all-start.1 = ((f32[2,448,2048]{2,0,1:T(2,128)}), f32[2,448,2048]{2,0,1:T(2,128)}, u32[]{:S(2)}, u32[]{:S(2)}) async-start(f32[2,448,2048]{2,0,1:T(2,128)} %copy.266), calls=%async_computation.2 | async-start | bytes 14680064 | tf_op jit(solution)/shard_map/all_to_all | solution.py:105
  795.7 238.5 %all-gather.25.cloned.1.call-start = ((), (), s32[]{:S(2)}) async-start(), calls=%async_computation.24 | async-start | bytes 3244032 | tf_op jit(solution)/shard_map/all_gather | solution.py:158
  796.5 241.2 %all-gather.27.cloned.1.call-start = ((), (), s32[]{:S(2)}) async-start(), calls=%async_computation.25 | async-start | bytes 3244032 | tf_op jit(solution)/shard_map/all_gather | solution.py:159
  829.6 203.4 %copy-start.32 = (bf16[2,64,2048]{2,1,0:T(8,128)(2,1)S(1)}, bf16[2,64,2048]{2,1,0:T(8,128)(2,1)}, u32[]{:S(2)}) copy-start(bf16[2,64,2048]{2,1,0:T(8,128)(2,1)} %param.47) | copy-start | bytes 1572868
  829.6 204.5 %copy-start.5 = (bf16[512,2048]{1,0:T(8,128)(2,1)S(1)}, bf16[512,2048]{1,0:T(8,128)(2,1)}, u32[]{:S(2)}) copy-start(bf16[512,2048]{1,0:T(8,128)(2,1)} %copy-done.4) | copy-start | bytes 6291460
  1027.2 223.9 %all-to-all-start.3 = ((f32[2,448,2048]{2,0,1:T(2,128)}), f32[2,448,2048]{2,0,1:T(2,128)}, u32[]{:S(2)}, u32[]{:S(2)}) async-start(f32[2,448,2048]{2,0,1:T(2,128)} %copy.274), calls=%async_computation.4 | async-start | bytes 14680064 | tf_op jit(solution)/shard_map/all_to_all | solution.py:105
  1031.3 60.6 %all-gather.31.cloned.1.call-start = ((), (), s32[]{:S(2)}) async-start(), calls=%async_computation.28 | async-start | bytes 2621440 | tf_op jit(solution)/shard_map/all_gather | solution.py:195
  1031.9 170.0 %all-gather.29.cloned.1.call-start = ((), (), s32[]{:S(2)}) async-start(), calls=%async_computation.26 | async-start | bytes 3244032 | tf_op jit(solution)/shard_map/all_gather | solution.py:160
  1032.6 357.9 %all-reduce.15.cloned.1.call-start = ((), (), s32[]{:S(2)}) async-start(), calls=%async_computation.29 | async-start | bytes 8388608 | tf_op jit(solution)/shard_map/psum | solution.py:379
  1207.9 88.2 %copy-start.30 = (bf16[512,704]{0,1:T(8,128)(2,1)}, bf16[512,704]{0,1:T(8,128)(2,1)S(1)}, u32[]{:S(2)}) copy-start(bf16[512,704]{0,1:T(8,128)(2,1)S(1)} %get-tuple-element.903) | copy-start | bytes 2162692
  1264.1 23.4 copy-start.34
  1264.1 23.4 copy-start.53
  1302.2 88.4 %copy-start.59 = (f32[8,1,256]{2,1,0:T(1,128)S(1)}, f32[8,1,256]{2,1,0:T(1,128)}, u32[]{:S(2)}) copy-start(f32[8,1,256]{2,1,0:T(1,128)} %copy-done.58) | copy-start | bytes 24580
  1302.2 92.5 %copy-start.24 = (bf16[2,256,2048]{2,1,0:T(8,128)(2,1)S(1)}, bf16[2,256,2048]{2,1,0:T(8,128)(2,1)}, u32[]{:S(2)}) copy-start(bf16[2,256,2048]{2,1,0:T(8,128)(2,1)} %all-gather.31.cloned.1.call-done) | copy-start | bytes 6291460
  1302.2 504.1 %reduce-scatter.20.cloned.1.call-start = ((), (), s32[]{:S(2)}) async-start(), calls=%async_computation.31 | async-start | bytes 23592960 | tf_op jit(solution)/shard_map/reduce_scatter | solution.py:435
  1419.1 439.1 %reduce-scatter.40.cloned.1.call-start = ((), (), s32[]{:S(2)}) async-start(), calls=%async_computation.41 | async-start | bytes 163840
  1836.9 46.9 %reduce-scatter.22.cloned.1.call-start = ((), (), s32[]{:S(2)}) async-start(), calls=%async_computation.32 | async-start | bytes 1310720 | tf_op jit(solution)/shard_map/reduce_scatter | solution.py:474
  1842.7 148.9 %reduce-scatter.16.cloned.1.call-start = ((), (), s32[]{:S(2)}) async-start(), calls=%async_computation.27 | async-start | bytes 5242880 | tf_op jit(solution)/shard_map/reduce_scatter | solution.py:304
  1848.7 149.6 %reduce-scatter.18.cloned.1.call-start = ((), (), s32[]{:S(2)}) async-start(), calls=%async_computation.30 | async-start | bytes 5242880 | tf_op jit(solution)/shard_map/reduce_scatter | solution.py:468
  1856.1 187.9 %reduce-scatter.38.cloned.1.call-start = ((), (), s32[]{:S(2)}) async-start(), calls=%async_computation.40 | async-start | bytes 589824 | tf_op jit(solution)/shard_map/reduce_scatter | solution.py:516
  1858.1 26.8 copy-start.27
  1858.1 26.9 copy-start.64
  1858.1 26.9 copy-start.80
  1858.1 284.7 %reduce-scatter.36.cloned.1.call-start = ((), (), s32[]{:S(2)}) async-start(), calls=%async_computation.39 | async-start | bytes 5308416 | tf_op jit(solution)/shard_map/reduce_scatter | solution.py:511
  1889.3 368.2 %reduce-scatter.30.cloned.1.call-start = ((), (), s32[]{:S(2)}) async-start(), calls=%async_computation.36 | async-start | bytes 6488064 | tf_op jit(solution)/shard_map/reduce_scatter | solution.py:517
  1896.7 475.6 %reduce-scatter.32.cloned.1.call-start = ((), (), s32[]{:S(2)}) async-start(), calls=%async_computation.37 | async-start | bytes 6488064 | tf_op jit(solution)/shard_map/reduce_scatter | solution.py:518
  1902.1 585.1 %reduce-scatter.34.cloned.1.call-start = ((), (), s32[]{:S(2)}) async-start(), calls=%async_computation.38 | async-start | bytes 6488064 | tf_op jit(solution)/shard_map/reduce_scatter | solution.py:519
  1908.9 671.2 %reduce-scatter.28.cloned.1.call-start = ((), (), s32[]{:S(2)}) async-start(), calls=%async_computation.35 | async-start | bytes 4718592 | tf_op jit(solution)/shard_map/reduce_scatter | solution.py:514
  1915.4 786.5 %reduce-scatter.24.cloned.1.call-start = ((), (), s32[]{:S(2)}) async-start(), calls=%async_computation.33 | async-start | bytes 7077888 | tf_op jit(solution)/shard_map/reduce_scatter | solution.py:510
  1921.5 23.8 copy-start.45
  1921.5 851.2 %reduce-scatter.26.cloned.1.call-start = ((), (), s32[]{:S(2)}) async-start(), calls=%async_computation.34 | async-start | bytes 2359296 | tf_op jit(solution)/shard_map/reduce_scatter | solution.py:513
  1948.7 859.3 %all-reduce.17.cloned.1.call-start = ((), (), s32[]{:S(2)}) async-start(), calls=%async_computation.42 | async-start | bytes 1310720 | tf_op jit(solution)/shard_map/psum | solution.py:505
  1948.8 17.8 copy-start.37
  1948.8 17.8 copy-start.85
  1966.5 13.1 copy-start.15
  (52 other events, 217.5 us)
Sparse Core Ops, SparseCore 0:
  10.1 43.1 all-gather.16
  55.4 52.4 all-gather.14
  109.5 23.5 all-gather.12
  135.1 60.4 all-gather.20
  198.1 149.5 all-gather.18
  349.6 49.2 all-gather.22
  403.9 83.6 all-reduce.12
  798.8 127.2 all-gather.24
  928.3 86.2 all-gather.26
  1033.5 58.4 all-gather.30
  1094.2 107.6 all-gather.28
  1302.3 88.1 all-reduce.14
  1419.2 387.0 reduce-scatter.19
  1837.0 18.7 reduce-scatter.39
  1858.9 24.8 reduce-scatter.21
  1886.2 44.4 reduce-scatter.15
  1933.3 44.4 reduce-scatter.17
  1981.6 62.3 reduce-scatter.37
  2048.1 94.6 reduce-scatter.35
  2147.3 110.0 reduce-scatter.29
  2262.2 110.1 reduce-scatter.31
  2377.0 110.1 reduce-scatter.33
  2491.8 88.2 reduce-scatter.27
  2584.1 117.6 reduce-scatter.23
  2705.9 66.7 reduce-scatter.25
  2775.1 32.9 all-reduce.16
where the time goes:
time: 2830 us; the launch traced here: 2820 us
  waiting for transfers between devices  2040 us (72%)
  blocking collectives  236 us (8%)
  local copies, waits for them, and re-layouts  227 us (8%)
  matrix products  210 us (7%)
  other arithmetic  59.6 us (2%)
    reduce_scatter x1, waiting for transfers between devices, per_device(): lax.psum_scatter(key_acc, 'blk', scatter_dimension=1, tiled=True)  387 us
    all_to_all x2, waiting for transfers between devices, from_units(): lax.all_to_all(values, ('blk', 'ulysses'), split_axis=1, concat_axis=0, t...  198 us
    all_gather x1, waiting for transfers between devices, per_device(): all_keys = lax.all_gather(packed_head, 'blk', axis=1, tiled=True)  143 us
    reduce_scatter x1, waiting for transfers between devices, per_device(): lax.psum_scatter(query_wgrad, 'blk', scatter_dimension=0, tiled=True)  122 us
    reduce_scatter x1, waiting for transfers between devices, per_device(): lax.psum_scatter(shared_down_wgrad, 'blk', scatter_dimension=1, tiled=True)  115 us
    reduce_scatter x1, waiting for transfers between devices, per_device(): lax.psum_scatter(shared_up_wgrad, 'blk', scatter_dimension=0, tiled=True)  115 us
    reduce_scatter x1, waiting for transfers between devices, per_device(): lax.psum_scatter(shared_gate_wgrad, 'blk', scatter_dimension=0, tiled=True)  112 us
    all_gather x1, waiting for transfers between devices, per_device(): lax.all_gather(w_shared_down, 'blk', axis=1, tiled=True)  110 us
  transfers between devices with their start and end apart: 30, of which 22 were waited for; matrix products, arithmetic and copies ran while one was open for 11% of the time, Pallas kernels for 0%

commit v1 on v0

v1 whole, which is shorter than its diff:
```python
import jax
import jax.numpy as jnp
from jax import lax
from jax.sharding import Mesh
from jax.sharding import PartitionSpec as P

H = 16
NOPE = 128
RD = 64
VH = 128
KVR = 512
EXPERTS = 64
TOP = 6
CAP = 14
Z_SIZE = 4
CORES = 2

epsilon = 1e-06
rope_base = 10000.0
wide = jnp.float32
narrow = jnp.bfloat16


def dot(a, b, out=wide):
    return jnp.dot(a, b, preferred_element_type=out)


def dot_tn(a, b, out=wide):
    return lax.dot_general(a, b, (((0,), (0,)), ((), ())), preferred_element_type=out)


def dot_nt(a, b, out=wide):
    return lax.dot_general(a, b, (((1,), (1,)), ((), ())), preferred_element_type=out)


def norm_rows(values, gain):
    inverse = lax.rsqrt(jnp.mean(values * values, axis=-1, keepdims=True) + epsilon)
    normed = values * inverse
    return (normed * gain, normed, inverse)


def norm_input_back(grad_out, normed, inverse, gain):
    scaled = grad_out * gain
    return inverse * (scaled - normed * jnp.mean(scaled * normed, axis=-1, keepdims=True))


def rotary_tables(positions):
    half_width = RD // 2
    frequency = rope_base ** (-2.0 * jnp.arange(half_width).astype(wide) / RD)
    angles = positions.astype(wide)[:, None] * frequency[None, :]
    return (jnp.cos(angles), jnp.sin(angles))


def rotate(values, cosine, sine):
    half = RD // 2
    a, b = values[..., :half], values[..., half:]
    return jnp.concatenate([a * cosine - b * sine, b * cosine + a * sine], axis=-1)


def unrotate(values, cosine, sine):
    half = RD // 2
    a, b = values[..., :half], values[..., half:]
    return jnp.concatenate([a * cosine + b * sine, b * cosine - a * sine], axis=-1)


def silu_slope(values):
    s = jax.nn.sigmoid(values)
    return s * (1.0 + values * (1.0 - s))


def hop(value, axis):
    n = lax.axis_size(axis)
    return lax.ppermute(value, axis, [(i, (i + 1) % n) for i in range(n)])


def ring(value, axis):
    items = [value]
    for _ in range(lax.axis_size(axis) - 1):
        items.append(hop(items[-1], axis))
    return items


def ring_sum(blocks, axis):
    n = lax.axis_size(axis)
    if n == 1:
        return blocks[0].astype(wide)
    running = hop(blocks[1].astype(narrow), axis)
    for s in range(2, n):
        running = hop((running.astype(wide) + blocks[s].astype(wide)).astype(narrow), axis)
    return running.astype(wide) + blocks[0].astype(wide)


def flat_ring(value, axes):
    items = [value]
    for axis in axes:
        items = [piece for item in items for piece in ring(item, axis)]
    return items


def tree_sum(blocks, axes):
    for axis in reversed(axes):
        n = lax.axis_size(axis)
        blocks = [ring_sum(blocks[i : i + n], axis) for i in range(0, len(blocks), n)]
    return blocks[0]


def per_device(
    tokens, attn_gain, w_query, w_latent, latent_gain, w_expand, w_output, ffn_gain, w_router,
    w_shared_gate, w_shared_up, w_shared_down, w_gate, w_up, w_down, routes, clip_limit, out_grad,
):
    seqs, local_len, features = tokens.shape
    rows = seqs * local_len
    qk = NOPE + RD
    nz, nx, ny, nc = (lax.axis_size(a) for a in ("z", "x", "y", "core"))
    zi, xi, yi, ci = (lax.axis_index(a) for a in ("z", "x", "y", "core"))
    nb, nu = nz * nx, ny * nc
    layer = nx * nu
    heads = H // nu
    group = nu * rows
    all_rows = nb * group
    upd = w_gate.shape[0]
    split = upd * nz * layer // EXPERTS
    scale = qk ** (-0.5)
    GROUP = ("y", "core")
    ALL = ("z", "x", "y", "core")
    LAYER = ("x", "y", "core")

    def gather_blk(shard, dim):
        size = shard.shape[dim]
        shape = list(shard.shape)
        shape[dim] = size * nb
        whole = jnp.zeros(tuple(shape), shard.dtype)
        for sz, behind in enumerate(ring(shard, "z")):
            for sx, piece in enumerate(ring(behind, "x")):
                owner = ((zi + nz - sz) % nz) * nx + (xi + nx - sx) % nx
                whole = lax.dynamic_update_slice_in_dim(whole, piece, owner * size, dim)
        return whole

    def scatter_blk(whole, dim):
        size = whole.shape[dim] // nb
        blocks = []
        for sz in range(nz):
            for sx in range(nx):
                owner = ((zi + nz - sz) % nz) * nx + (xi + nx - sx) % nx
                blocks.append(lax.dynamic_slice_in_dim(whole, owner * size, size, dim))
        return tree_sum(blocks, ("z", "x"))

    def group_gather(value):
        return jnp.concatenate(flat_ring(value, GROUP), axis=0)

    def group_scatter(value):
        return tree_sum([value[i * rows : (i + 1) * rows] for i in range(nu)], GROUP)

    def group_sum(value):
        for axis in GROUP:
            items = ring(value, axis)
            value = sum(item.astype(wide) for item in items)
        return value

    def device_positions(blk, u):
        return (blk * nu + u) * local_len + jnp.arange(local_len, dtype=jnp.int32)

    local_pos = device_positions(zi * nx + xi, yi * nc + ci)
    group_pos = jnp.concatenate(
        [
            device_positions(zi * nx + xi, (yi + ny - sy) % ny * nc + (ci + nc - sc) % nc)
            for sy in range(ny)
            for sc in range(nc)
        ]
    )
    key_pos = jnp.concatenate(
        [
            device_positions(
                (zi + nz - sz) % nz * nx + (xi + nx - sx) % nx,
                (yi + ny - sy) % ny * nc + (ci + nc - sc) % nc,
            )
            for sz in range(nz)
            for sx in range(nx)
            for sy in range(ny)
            for sc in range(nc)
        ]
    )

    small = jnp.concatenate(
        [
            w_latent,
            w_router,
            attn_gain[:, None],
            ffn_gain[:, None],
            jnp.pad(latent_gain, (0, attn_gain.shape[0] - latent_gain.shape[0]))[:, None],
        ],
        axis=1,
    )
    small_whole = gather_blk(small, 0)
    tokens_local = tokens.reshape(rows, features)
    grad_narrow = out_grad.reshape(rows, features)
    tokens_group = group_gather(tokens_local)
    latent_w = small_whole[:, : KVR + RD]
    router_w = small_whole[:, KVR + RD : KVR + RD + EXPERTS]
    gain_attn = small_whole[:, KVR + RD + EXPERTS].astype(wide)
    gain_ffn = small_whole[:, KVR + RD + EXPERTS + 1].astype(wide)
    gain_latent = (
        small_whole[:, KVR + RD + EXPERTS + 2]
        .reshape(nb, -1)[:, : latent_gain.shape[0]]
        .reshape(-1)
        .astype(wide)
    )
    query_w = gather_blk(w_query, 0)
    expand_w = gather_blk(w_expand, 0)
    output_w = gather_blk(w_output, 1)

    inputs = tokens_local.astype(wide)
    scaled_in, normed_in, inverse_in = norm_rows(inputs, gain_attn)
    hidden_local = scaled_in.astype(narrow)
    latent_all = dot(hidden_local, latent_w)
    scaled_lat, normed_lat, inverse_lat = norm_rows(latent_all[:, :KVR], gain_latent)
    cos_local, sin_local = rotary_tables(jnp.tile(local_pos, seqs))
    latent_pack = jnp.concatenate(
        [scaled_lat, rotate(latent_all[:, KVR:], cos_local, sin_local)], axis=-1
    ).astype(narrow)
    latent_keys = jnp.concatenate(
        [p.reshape(seqs, local_len, KVR + RD) for p in flat_ring(latent_pack, ALL)], axis=1
    )
    length = latent_keys.shape[1]
    latent_rows = latent_keys[..., :KVR].reshape(all_rows, KVR)
    rope_keys = latent_keys[..., KVR:]

    grad_group = group_gather(grad_narrow)

    route_line = jnp.concatenate(
        ring(jnp.swapaxes(routes, 0, 1).reshape(rows, TOP), "z"), axis=0
    ).reshape(nz, rows, TOP)
    member = jnp.any(
        route_line[..., None] == jnp.arange(EXPERTS, dtype=jnp.int32), axis=2
    )
    earlier = (
        jnp.arange(rows, dtype=jnp.int32)[None, :] < jnp.arange(rows, dtype=jnp.int32)[:, None]
    ).astype(narrow)
    rank = jnp.einsum(
        "tq,zqe->zte", earlier, member.astype(narrow), preferred_element_type=wide
    ).astype(jnp.int32)
    here = EXPERTS // nz
    rank = jnp.where(member, rank, -1)
    rank_layer = lax.dynamic_slice_in_dim(rank, zi * here, here, 2)
    picks = []
    for a in range(upd):
        experts = [(d * upd + a) // split for d in range(layer)]
        chosen = jnp.stack([rank_layer[..., e] for e in experts], axis=-1)
        hit = chosen[..., None] == jnp.arange(CAP, dtype=jnp.int32)
        own = jnp.eye(nz, dtype=jnp.bool_)
        pick = hit[:, :, :, None, :] & own[:, None, None, :, None]
        picks.append(pick.astype(narrow).reshape(nz * rows, layer * nz * CAP))

    def to_experts(line):
        return [
            lax.all_to_all(
                dot_tn(pick, line, narrow).reshape(layer, nz * CAP, -1),
                LAYER, split_axis=0, concat_axis=0, tiled=True,
            ).reshape(layer * nz * CAP, -1)
            for pick in picks
        ]

    def from_experts(parts):
        back = [
            lax.all_to_all(
                part.reshape(layer, nz * CAP, -1), LAYER, split_axis=0, concat_axis=0, tiled=True
            ).reshape(layer * nz * CAP, -1)
            for part in parts
        ]
        line = sum(dot(pick, rows_back) for pick, rows_back in zip(picks, back))
        return ring_sum([line[i * rows : (i + 1) * rows] for i in range(nz)], "z")

    grad_line = jnp.concatenate(ring(grad_narrow, "z"), axis=0)
    expert_grads = to_experts(grad_line)
    down_back = [dot_nt(expert_grads[a], w_down[a]) for a in range(upd)]

    gate_w = gather_blk(w_shared_gate, 0)
    up_w = gather_blk(w_shared_up, 0)
    down_w = gather_blk(w_shared_down, 1)

    hidden_group = norm_rows(tokens_group.astype(wide), gain_attn)[0].astype(narrow)
    cos_group, sin_group = rotary_tables(
        jnp.repeat(group_pos.reshape(nu, 1, local_len), seqs, 1).reshape(-1)
    )
    query_lin = dot(hidden_group, query_w).reshape(group, heads, qk)
    query_rows = jnp.concatenate(
        [
            query_lin[..., :NOPE],
            rotate(query_lin[..., NOPE:], cos_group[:, None, :], sin_group[:, None, :]),
        ],
        axis=-1,
    ).astype(narrow)

    def by_seq(values):
        tail = values.shape[1:]
        return jnp.swapaxes(values.reshape((nu, seqs, local_len) + tail), 0, 1).reshape(
            (seqs, nu * local_len) + tail
        )

    def from_seq(values):
        tail = values.shape[2:]
        return jnp.swapaxes(values.reshape((seqs, nu, local_len) + tail), 0, 1).reshape(
            (group,) + tail
        )

    query_four = by_seq(query_rows)
    expanded = dot(latent_rows, expand_w, narrow).reshape(seqs, length, heads, NOPE + VH)
    rope_wide = jnp.broadcast_to(rope_keys[:, :, None, :], (seqs, length, heads, RD))
    key_four = jnp.concatenate([expanded[..., :NOPE], rope_wide], axis=-1)
    value_four = expanded[..., NOPE:]
    allowed = key_pos[None, :] <= group_pos[:, None]
    scores = (
        jnp.einsum("sqhc,skhc->shqk", query_four, key_four, preferred_element_type=wide) * scale
    )
    masked = jnp.where(allowed, scores, -jnp.inf)
    maxima = jnp.max(masked, axis=-1)
    totals = jnp.sum(jnp.exp(masked - maxima[..., None]), axis=-1)
    log_sum = maxima + jnp.log(totals)
    probability = jnp.exp(masked - log_sum[..., None])
    prob_narrow = probability.astype(narrow)
    attention = jnp.einsum(
        "shqk,skhd->sqhd", prob_narrow, value_four, preferred_element_type=wide
    )
    attended = from_seq(attention).reshape(group, heads * VH).astype(narrow)

    top = jnp.max(maxima, axis=(0, 2))
    for axis in ("z", "x"):
        items = ring(top, axis)
        for item in items[1:]:
            top = jnp.maximum(top, item)
    clip_value = clip_limit[0]
    clip_factor = clip_value / jnp.maximum(top, clip_value)

    residual = inputs + group_scatter(dot(attended, output_w, narrow))
    scaled_mid, normed_mid, inverse_mid = norm_rows(residual, gain_ffn)
    hidden_mid = scaled_mid.astype(narrow)

    logits = dot(hidden_mid, router_w)
    own_member = member[0]
    chosen_logits = jnp.where(own_member, logits, -jnp.inf)
    raised = jnp.exp(chosen_logits - jnp.max(chosen_logits, axis=-1, keepdims=True))
    gates = raised / jnp.sum(raised, axis=-1, keepdims=True)

    def halves(values):
        high = values.astype(narrow)
        return [high, (values - high.astype(wide)).astype(narrow)]

    dispatch_line = jnp.concatenate(
        ring(jnp.concatenate([hidden_mid] + halves(gates), axis=1), "z"), axis=0
    )
    expert_rows = to_experts(dispatch_line)
    hidden_mid_group = group_gather(hidden_mid)

    shared_gate = dot(hidden_mid_group, gate_w)
    shared_up = dot(hidden_mid_group, up_w)
    shared_act = (jax.nn.silu(shared_gate) * shared_up).astype(narrow)
    shared_partial = dot(shared_act, down_w, narrow)
    shared_act_grad = dot_nt(grad_group, down_w)
    shared_gate_grad = (shared_act_grad * shared_up * silu_slope(shared_gate)).astype(narrow)
    shared_up_grad = (shared_act_grad * jax.nn.silu(shared_gate)).astype(narrow)
    mid_shared = dot_nt(shared_gate_grad, gate_w) + dot_nt(shared_up_grad, up_w)
    mid_shared_local = group_scatter(mid_shared.astype(narrow))
    shared_local = group_scatter(shared_partial)

    first_unit = ((zi * nx + xi) * nu + yi * nc + ci) * upd
    returned, outputs, gate_wgrad, up_wgrad, down_wgrad = [], [], [], [], []
    for a in range(upd):
        expert = (first_unit + a) // split
        lane = jnp.arange(EXPERTS, dtype=jnp.int32)[None, :] == expert
        picked = expert_rows[a][:, :features]
        gate_lanes = expert_rows[a][:, features:].astype(wide)
        weight = jnp.sum(
            jnp.where(lane, gate_lanes[:, :EXPERTS] + gate_lanes[:, EXPERTS:], 0.0),
            axis=1, keepdims=True,
        )
        unit_gate = dot(picked, w_gate[a])
        unit_up = dot(picked, w_up[a])
        unit_act = (jax.nn.silu(unit_gate) * unit_up).astype(narrow)
        unit_out = dot(unit_act, w_down[a])
        grad_rows = expert_grads[a].astype(wide)
        gate_grad = jnp.sum(unit_out * grad_rows, axis=1, keepdims=True)
        act_grad = down_back[a] * weight
        lin_gate_grad = (act_grad * unit_up * silu_slope(unit_gate)).astype(narrow)
        lin_up_grad = (act_grad * jax.nn.silu(unit_gate)).astype(narrow)
        unit_in_grad = dot_nt(lin_gate_grad, w_gate[a]) + dot_nt(lin_up_grad, w_up[a])
        returned.append(
            jnp.concatenate(
                [unit_in_grad.astype(narrow)]
                + [jnp.where(lane, half, jnp.zeros((), narrow)) for half in halves(gate_grad)],
                axis=1,
            )
        )
        outputs.append((unit_out * weight).astype(narrow))
        route_grad = (grad_rows * weight).astype(narrow)
        gate_wgrad.append(dot_tn(picked, lin_gate_grad))
        up_wgrad.append(dot_tn(picked, lin_up_grad))
        down_wgrad.append(dot_tn(unit_act, route_grad))
    gate_wgrad, up_wgrad, down_wgrad = (
        jnp.stack(items) for items in (gate_wgrad, up_wgrad, down_wgrad)
    )

    back = from_experts(returned)
    routed = from_experts(outputs)
    block_out = (residual + shared_local + routed).astype(narrow).reshape(tokens.shape)

    shared_gate_wgrad = scatter_blk(dot_tn(hidden_mid_group, shared_gate_grad, narrow), 0)
    shared_up_wgrad = scatter_blk(dot_tn(hidden_mid_group, shared_up_grad, narrow), 0)
    shared_down_wgrad = scatter_blk(dot_tn(shared_act, grad_group, narrow), 1)

    grad_wide = grad_narrow.astype(wide)
    gate_grads = back[:, features : features + EXPERTS] + back[:, features + EXPERTS :]
    logit_grad = (
        gates * (gate_grads - jnp.sum(gates * gate_grads, axis=-1, keepdims=True))
    ).astype(narrow)
    mid_grad = back[:, :features] + mid_shared_local + dot_nt(logit_grad, router_w)
    residual_grad = grad_wide + norm_input_back(mid_grad, normed_mid, inverse_mid, gain_ffn)
    ffn_gain_grad = jnp.sum(mid_grad * normed_mid, axis=0)
    router_wgrad = dot_tn(hidden_mid, logit_grad)
    mid_small = group_sum(
        scatter_blk(
            jnp.concatenate([router_wgrad, ffn_gain_grad[:, None]], axis=1).astype(narrow), 0
        )
    )

    attn_grad = group_gather(residual_grad.astype(narrow))
    attended_grad = dot_nt(attn_grad, output_w, narrow)
    output_wgrad = scatter_blk(dot_tn(attended, attn_grad, narrow), 1)

    grad_four = by_seq(attended_grad.reshape(group, heads, VH))
    prob_grad = jnp.einsum("sqhd,skhd->shqk", grad_four, value_four, preferred_element_type=wide)
    row_delta = jnp.einsum("sqhd,sqhd->shq", grad_four, attention, preferred_element_type=wide)
    score_grad = (probability * (prob_grad - row_delta[..., None]) * scale).astype(narrow)
    query_acc = jnp.einsum("shqk,skhc->sqhc", score_grad, key_four, preferred_element_type=wide)
    key_grad = jnp.einsum("shqk,sqhc->skhc", score_grad, query_four, preferred_element_type=wide)
    value_grad = jnp.einsum("shqk,sqhd->skhd", prob_narrow, grad_four, preferred_element_type=wide)

    query_back = from_seq(query_acc)
    query_lin_grad = (
        jnp.concatenate(
            [
                query_back[..., :NOPE],
                unrotate(query_back[..., NOPE:], cos_group[:, None, :], sin_group[:, None, :]),
            ],
            axis=-1,
        )
        .reshape(group, heads * qk)
        .astype(narrow)
    )
    hidden_sum = group_scatter(dot_nt(query_lin_grad, query_w, narrow))
    expand_grad = (
        jnp.concatenate([key_grad[..., :NOPE], value_grad], axis=-1)
        .astype(narrow)
        .reshape(all_rows, heads * (NOPE + VH))
    )
    rope_partial = jnp.sum(key_grad[..., NOPE:], axis=2)
    latent_partial = jnp.concatenate(
        [dot_nt(expand_grad, expand_w).reshape(seqs, length, KVR), rope_partial], axis=-1
    ).astype(narrow)
    latent_sum = tree_sum(
        [
            latent_partial[:, i * local_len : (i + 1) * local_len].reshape(rows, KVR + RD)
            for i in range(nb * nu)
        ],
        ALL,
    )
    query_wgrad = scatter_blk(dot_tn(hidden_group, query_lin_grad, narrow), 0)
    expand_wgrad = scatter_blk(dot_tn(latent_rows, expand_grad, narrow), 0)

    latent_grad = latent_sum[:, :KVR]
    key_rope_grad = unrotate(latent_sum[:, KVR:], cos_local, sin_local)
    latent_in_grad = norm_input_back(latent_grad, normed_lat, inverse_lat, gain_latent)
    latent_gain_grad = jnp.sum(latent_grad * normed_lat, axis=0)
    latent_all_grad = jnp.concatenate([latent_in_grad, key_rope_grad], axis=-1).astype(narrow)
    hidden_grad = hidden_sum + dot_nt(latent_all_grad, latent_w)
    input_grad = norm_input_back(hidden_grad, normed_in, inverse_in, gain_attn)
    attn_gain_grad = jnp.sum(hidden_grad * normed_in, axis=0)
    tokens_grad = (residual_grad + input_grad).astype(narrow).reshape(tokens.shape)
    latent_wgrad = dot_tn(hidden_local, latent_all_grad)
    lat_len = latent_gain.shape[0]
    latent_gain_column = jnp.pad(
        latent_gain_grad.reshape(nb, lat_len), ((0, 0), (0, attn_gain.shape[0] - lat_len))
    ).reshape(-1)
    in_small = group_sum(
        scatter_blk(
            jnp.concatenate(
                [latent_wgrad, attn_gain_grad[:, None], latent_gain_column[:, None]], axis=1
            ).astype(narrow),
            0,
        )
    )
    width = KVR + RD
    return (
        block_out,
        tokens_grad,
        in_small[:, width],
        query_wgrad,
        in_small[:, :width],
        in_small[:lat_len, width + 1],
        expand_wgrad,
        output_wgrad,
        mid_small[:, EXPERTS],
        mid_small[:, :EXPERTS],
        shared_gate_wgrad,
        shared_up_wgrad,
        shared_down_wgrad,
        gate_wgrad,
        up_wgrad,
        down_wgrad,
        clip_factor,
    )


def solution(mesh):
    blocks, group = mesh.shape["blk"], mesh.shape["ulysses"]
    chips = Mesh(
        mesh.devices.reshape(Z_SIZE, blocks // Z_SIZE, group // CORES, CORES),
        ("z", "x", "y", "core"),
    )
    blk, uly, every = ("z", "x"), ("y", "core"), ("z", "x", "y", "core")
    rows = P(None, every, None)
    unit = P(every, None, None)
    return jax.shard_map(
        per_device,
        mesh=chips,
        in_specs=(
            rows, P(blk), P(blk, uly), P(blk, None), P(blk), P(blk, uly), P(uly, blk), P(blk),
            P(blk, None), P(blk, uly), P(blk, uly), P(uly, blk), unit, unit, unit, unit, P(), rows,
        ),
        out_specs=(
            rows, rows, P(blk), P(blk, uly), P(blk, None), P(blk), P(blk, uly), P(uly, blk), P(blk),
            P(blk, None), P(blk, uly), P(blk, uly), P(uly, blk), unit, unit, unit, P(uly),
        ),
        check_vma=False,
    )
```

time: 2830 us -> 1290 us (0.46)
  waiting for transfers between devices: 2040 us -> 362 us
  blocking collectives: 236 us -> 0 us
  starting transfers between devices: 21.1 us -> 187 us
  matrix products: 210 us -> 294 us
  other arithmetic: 59.6 us -> 139 us
  local copies, waits for them, and re-layouts: 227 us -> 291 us
    reduce_scatter x12 -> x0, waiting for transfers between devices: 1140 us -> none  [the longest x1 387 us: per_device(): lax.psum_scatter(key_acc, 'blk', scatter_dimension=1, tiled=True)]
    all_gather x10 -> x0, waiting for transfers between devices: 458 us -> none  [the longest x1 143 us: per_device(): all_keys = lax.all_gather(packed_head, 'blk', axis=1, tiled=True)]
    ppermute x0 -> x214, waiting for transfers between devices: none -> 338 us  [hop(): return lax.ppermute(value, axis, [(i, (i + 1) % n) for i in range(n)])]
    all_to_all x4 -> x8, waiting for transfers between devices: 262 us -> 24 us  [the longest x4 13 us: to_experts(): lax.all_to_all(dot_tn(pick, line, narrow).reshape(layer, nz * CAP, -1), L...]
    psum x3 -> x0, waiting for transfers between devices: 182 us -> none  [the longest x1 87.9 us: per_device(): lax.psum(mid_shared + lax.dynamic_update_slice_in_dim(empty, mid_local.re...]
    all_gather x5 -> x0, blocking collectives: 157 us -> none  [the longest x1 101 us: per_device(): lax.all_gather(w_router, 'blk', axis=0, tiled=True)]
    ppermute x0 -> x214, starting transfers between devices: none -> 154 us  [hop(): return lax.ppermute(value, axis, [(i, (i + 1) % n) for i in range(n)])]
    dot_general x40 -> x57, matrix products: 210 us -> 294 us  [the longest x18 88.5 us: dot(): return jnp.dot(a, b, preferred_element_type=out)]
  transfers between devices with their start and end apart: 30 -> 222, of which waited for: 22 -> 84; matrix products, arithmetic and copies ran while one was open for 11% -> 48% of each run, Pallas kernels for 0% -> 0%
where the time goes in v1:
time: 1290 us; the launch traced here: 1280 us
  waiting for transfers between devices  362 us (28%)
  matrix products  294 us (23%)
  local copies, waits for them, and re-layouts  291 us (23%)
  starting transfers between devices  187 us (14%)
  other arithmetic  139 us (11%)
    ppermute x214, waiting for transfers between devices, hop(): return lax.ppermute(value, axis, [(i, (i + 1) % n) for i in range(n)])  338 us
    ppermute x214, starting transfers between devices, hop(): return lax.ppermute(value, axis, [(i, (i + 1) % n) for i in range(n)])  154 us
    dot_general x18, matrix products, dot(): return jnp.dot(a, b, preferred_element_type=out)  88.5 us
    dot_general x18, matrix products, dot_tn(): lax.dot_general(a, b, (((0,), (0,)), ((), ())), preferred_element_type=out)  84.2 us
    unnamed x467, local copies, waits for them, and re-layouts  74.3 us
    dot_general x14, matrix products, dot_nt(): lax.dot_general(a, b, (((1,), (1,)), ((), ())), preferred_element_type=out)  67.8 us
    dynamic_update_slice x56, local copies, waits for them, and re-layouts, gather_blk(): whole = lax.dynamic_update_slice_in_dim(whole, piece, owner * size, dim)  52.8 us
    ppermute x31, local copies, waits for them, and re-layouts, hop(): return lax.ppermute(value, axis, [(i, (i + 1) % n) for i in range(n)])  49.6 us
  transfers between devices with their start and end apart: 222, of which 84 were waited for; matrix products, arithmetic and copies ran while one was open for 48% of the time, Pallas kernels for 0%

profile of v1, /device:TPU:0, one launch (start us, length us, event | category | flops | bytes accessed | tf_op | source)
XLA Modules:
  0.0 1279.9 jit_solution(4075875253753257233)
XLA Ops:
  37.1 5.3 collective-permute-done.93
  75.6 6.9 collective-permute-done.76
  172.4 14.0 %collective-permute-done.61 = bf16[512,256]{1,0:T(8,128)(2,1)S(1)} collective-permute-done((bf16[512,256]{1,0:T(8,128)(2,1)S(1)}, bf16[512,256]{1,0:T(8,128)(2,1)S(1)}, u32[]{:S(2)}, u32[]{:S(2)}) %collective-permute-start.61) | collective-permute-done | bytes 262176 | tf_op jit(solution)/shard_map/ppermute | solution.py:73
  248.2 5.8 fusion.116
  376.3 7.0 fusion.44
  389.5 6.0 fusion.2
  395.5 6.1 fusion.1
  401.7 10.6 bitcast_convert_fusion
  419.2 5.1 fusion.126
  431.9 7.0 collective-permute-done.63
  445.5 8.4 collective-permute-done.66
  462.7 5.1 collective-permute-done.210
  467.8 5.3 collective-permute-done.211
  473.1 5.3 collective-permute-done.212
  519.6 5.9 collective-permute-done.196
  527.8 4.9 collective-permute-done.97
  554.2 6.5 collective-permute-done.204
  562.7 10.7 collective-permute-done.198
  582.9 6.0 collective-permute-done.207
  593.2 24.2 %collective-permute-done.200 = bf16[256,704]{0,1:T(8,128)(2,1)S(1)} collective-permute-done((bf16[256,704]{0,1:T(8,128)(2,1)}, bf16[256,704]{0,1:T(8,128)(2,1)S(1)}, u32[]{:S(2)}, u32[]{:S(2)}) %collective-permute-start.200) | collective-permute-done | bytes 360480 | tf_op jit(solution)/shard_map/ppermute | solution.py:73
  618.7 6.4 collective-permute-done.193
  626.2 6.6 collective-permute-done.209
  635.0 5.6 collective-permute-done.202
  652.9 7.7 fusion.9
  660.6 13.0 %all-to-all-done.6 = bf16[8,56,2048]{2,1,0:T(8,128)(2,1)} async-done(((bf16[8,56,2048]{2,1,0:T(8,128)(2,1)}), bf16[8,56,2048]{2,1,0:T(8,128)(2,1)}, u32[]{:S(2)}, u32[]{:S(2)}) %all-to-all-start.6) | async-done | bytes 1835040 | tf_op jit(solution)/shard_map/all_to_all | solution.py:256
  677.4 6.1 fusion.56
  683.6 8.8 multiply_convert_fusion.4
  692.4 6.3 fusion.51
  698.8 6.0 fusion.21
  704.8 7.8 fusion.53
  712.6 8.0 multiply_convert_fusion.6
  720.8 4.9 fusion.49
  728.9 5.7 add_convert_fusion.2
  740.9 5.5 fusion.7
  746.6 7.5 add_convert_fusion.1
  758.1 7.9 convolution_bitcast_fusion.4
  766.1 6.2 convolution_bitcast_fusion.1
  772.3 9.2 convolution_bitcast_fusion
  787.2 7.8 convolution_bitcast_fusion.5
  795.1 13.5 %pad_maximum_fusion.2 = f32[2,1408,2048]{2,1,0:T(8,128)} fusion(f32[1,1408,2048]{2,1,0:T(8,128)} %convolution_bitcast_fusion, f32[1,1408,2048]{2,1,0:T(8,128)S(1)} %copy-done.8), kind=kLoop, calls=%fused_computation.33 | loop fusion | flops 5767168 | bytes 46137344 | tf_op jit(solution)/shard_map/stack | solution.py:399
  820.4 17.8 %pad_maximum_fusion = f32[2,2048,1408]{2,1,0:T(8,128)} fusion(f32[1,2048,1408]{2,1,0:T(8,128)} %convolution_bitcast_fusion.4, f32[1,2048,1408]{2,1,0:T(8,128)} %convolution_bitcast_fusion.5), kind=kLoop, calls=%fused_computation.31 | loop fusion | flops 5767168 | bytes 46137344 | tf_op jit(solution)/shard_map/stack | solution.py:399
  838.5 7.9 convolution_bitcast_fusion.2
  846.3 8.9 collective-permute-done.105
  856.1 7.6 convolution_bitcast_fusion.3
  867.8 4.9 fusion.213
  880.1 10.9 all-to-all-done.3
  900.7 10.1 collective-permute-done.181
  917.1 5.9 collective-permute-done.185
  924.7 13.4 %pad_maximum_fusion.1 = f32[2,2048,1408]{2,1,0:T(8,128)} fusion(f32[1,2048,1408]{2,1,0:T(8,128)S(1)} %bitcast.365, f32[1,2048,1408]{2,1,0:T(8,128)} %convolution_bitcast_fusion.3), kind=kLoop, calls=%fused_computation.32 | loop fusion | flops 5767168 | bytes 46137344 | tf_op jit(solution)/shard_map/stack | solution.py:399
  946.2 12.7 convolution_bitcast_fusion.7
  959.0 13.7 %multiply_convert_fusion = bf16[2,4,256,2048]{3,2,1,0:T(8,128)(2,1)} fusion(f32[2,4,256,2048]{3,2,1,0:T(8,128)} %copy-done.5, f32[2,4,256]{2,1,0:T(4,128)S(1)} %fusion.106, f32[2,4,256]{2,1,0:T(4,128)S(1)} %bitcast.478, pred[256,2048]{1,0:T(8,128)(4,1)S(1)} %copy-done.27, bf16[2,256,4,128]{3,1,2,0:T(8,128)(2,1)S(1)} %bitcast.381, ...), kind=kOutput, calls=%fused_computation.35 | convolution fusion | flops 1103101952 | bytes 30425088 | tf_op jit(solution)/shard_map/sqhd,skhd->shqk/dot_general | solution.py:430
  972.8 8.7 fusion.77
  994.9 8.4 maximum_convert_fusion
  1003.3 8.2 convolution_convert_fusion
  1015.9 13.8 %copy.821 = bf16[2,2048,4,256]{3,2,1,0:T(4,128)(2,1)} copy(bf16[2,2048,4,256]{1,3,2,0:T(8,128)(2,1)} %maximum_convert_fusion) | data formatting | bytes 16777216 | tf_op jit(solution)/shard_map/convert_element_type | solution.py:452
  1072.2 9.4 copy.850
  1081.6 9.7 fusion.230
  1114.3 4.6 collective-permute-done.128
  1161.2 8.0 collective-permute-done.117
  1179.0 5.8 collective-permute-done.150
  1205.0 5.4 collective-permute-done.169
  1213.9 6.5 collective-permute-done.153
  1232.1 5.1 collective-permute-done.155
  1245.1 14.7 %collective-permute-done.162 = bf16[256,768]{1,0:T(8,128)(2,1)S(1)} collective-permute-done((bf16[256,768]{1,0:T(8,128)(2,1)S(1)}, bf16[256,768]{1,0:T(8,128)(2,1)S(1)}, u32[]{:S(2)}, u32[]{:S(2)}) %collective-permute-start.162) | collective-permute-done | bytes 393248 | tf_op jit(solution)/shard_map/ppermute | solution.py:73
  (1274 shorter events, 745.5 us)
Async XLA Ops:
  0.7 50.7 %collective-permute-start.39 = (bf16[64,1024]{1,0:T(8,128)(2,1)}, bf16[64,1024]{1,0:T(8,128)(2,1)S(1)}, u32[]{:S(2)}, u32[]{:S(2)}) collective-permute-start(bf16[64,1024]{1,0:T(8,128)(2,1)} %param.23), channel_id=1, source_target_pairs={{0,8},{8,16},{16,24},{24,0},{1,9},{9,17},{17,25},{25,1},{2,10},{10... | collective-permute-start | bytes 393224 | tf_op jit(solution)/shard_map/ppermute | solution.py:73
  3.8 49.1 %collective-permute-start.38 = (bf16[64,1024]{1,0:T(8,128)(2,1)}, bf16[64,1024]{1,0:T(8,128)(2,1)}, u32[]{:S(2)}, u32[]{:S(2)}) collective-permute-start(bf16[64,1024]{1,0:T(8,128)(2,1)} %param.23), channel_id=1, source_target_pairs={{0,4},{4,0},{1,5},{5,1},{2,6},{6,2},{3,7},{7,3},{8,12},{12,8},{9,1... | collective-permute-start | bytes 393224 | tf_op jit(solution)/shard_map/ppermute | solution.py:73
  5.3 60.7 %collective-permute-start.56 = (bf16[512,256]{1,0:T(8,128)(2,1)}, bf16[512,256]{1,0:T(8,128)(2,1)}, u32[]{:S(2)}, u32[]{:S(2)}) collective-permute-start(bf16[512,256]{1,0:T(8,128)(2,1)} %param.24), channel_id=1, source_target_pairs={{0,8},{8,16},{16,24},{24,0},{1,9},{9,17},{17,25},{25,1},{2,10},{10... | collective-permute-start | bytes 786440 | tf_op jit(solution)/shard_map/ppermute | solution.py:73
  6.8 48.8 %collective-permute-start.55 = (bf16[512,256]{1,0:T(8,128)(2,1)}, bf16[512,256]{1,0:T(8,128)(2,1)}, u32[]{:S(2)}, u32[]{:S(2)}) collective-permute-start(bf16[512,256]{1,0:T(8,128)(2,1)} %param.24), channel_id=1, source_target_pairs={{0,4},{4,0},{1,5},{5,1},{2,6},{6,2},{3,7},{7,3},{8,12},{12,8},{9,1... | collective-permute-start | bytes 786440 | tf_op jit(solution)/shard_map/ppermute | solution.py:73
  8.1 28.8 %collective-permute-start.92 = (s32[128,6]{0,1:T(8,128)S(1)}, s32[128,6]{0,1:T(8,128)S(1)}, u32[]{:S(2)}, u32[]{:S(2)}) collective-permute-start(s32[128,6]{0,1:T(8,128)S(1)} %reshape.655), channel_id=1, source_target_pairs={{0,8},{8,16},{16,24},{24,0},{1,9},{9,17},{17,25},{25,1},{2,10},{10... | collective-permute-start | bytes 9224 | tf_op jit(solution)/shard_map/ppermute | solution.py:73
  60.2 34.5 %collective-permute-start.69 = (bf16[256,704]{0,1:T(8,128)(2,1)}, bf16[256,704]{0,1:T(8,128)(2,1)S(1)}, u32[]{:S(2)}, u32[]{:S(2)}) collective-permute-start(bf16[256,704]{0,1:T(8,128)(2,1)} %param.27), channel_id=1, source_target_pairs={{0,8},{8,16},{16,24},{24,0},{1,9},{9,17},{17,25},{25,1},{2,10},{10... | collective-permute-start | bytes 1081352 | tf_op jit(solution)/shard_map/ppermute | solution.py:73
  66.0 26.6 %collective-permute-start.68 = (bf16[256,704]{0,1:T(8,128)(2,1)}, bf16[256,704]{0,1:T(8,128)(2,1)S(1)}, u32[]{:S(2)}, u32[]{:S(2)}) collective-permute-start(bf16[256,704]{0,1:T(8,128)(2,1)} %param.27), channel_id=1, source_target_pairs={{0,4},{4,0},{1,5},{5,1},{2,6},{6,2},{3,7},{7,3},{8,12},{12,8},{9,1... | collective-permute-start | bytes 1081352 | tf_op jit(solution)/shard_map/ppermute | solution.py:73
  82.5 24.6 %collective-permute-start.49 = (bf16[256,768]{1,0:T(8,128)(2,1)}, bf16[256,768]{1,0:T(8,128)(2,1)S(1)}, u32[]{:S(2)}, u32[]{:S(2)}) collective-permute-start(bf16[256,768]{1,0:T(8,128)(2,1)} %param.20), channel_id=1, source_target_pairs={{0,8},{8,16},{16,24},{24,0},{1,9},{9,17},{17,25},{25,1},{2,10},{10... | collective-permute-start | bytes 1179656 | tf_op jit(solution)/shard_map/ppermute | solution.py:73
  90.2 58.6 %collective-permute-start.46 = (bf16[128,2048]{1,0:T(8,128)(2,1)S(1)}, bf16[128,2048]{1,0:T(8,128)(2,1)}, u32[]{:S(2)}, u32[]{:S(2)}) collective-permute-start(bf16[128,2048]{1,0:T(8,128)(2,1)S(1)} %bitcast.357), channel_id=1, source_target_pairs={{0,2},{2,0},{1,3},{3,1},{4,6},{6,4},{5,7},{7,5},{8,10},{10,8},{9,1... | collective-permute-start | bytes 1572872 | tf_op jit(solution)/shard_map/ppermute | solution.py:73
  118.8 27.1 %collective-permute-start.71 = (bf16[256,704]{0,1:T(8,128)(2,1)}, bf16[256,704]{0,1:T(8,128)(2,1)S(1)}, u32[]{:S(2)}, u32[]{:S(2)}) collective-permute-start(bf16[256,704]{0,1:T(8,128)(2,1)} %copy-done.120), channel_id=1, source_target_pairs={{0,8},{8,16},{16,24},{24,0},{1,9},{9,17},{17,25},{25,1},{2,10},{10... | collective-permute-start | bytes 1081352 | tf_op jit(solution)/shard_map/ppermute | solution.py:73
  156.8 49.5 %collective-permute-start.73 = (bf16[256,704]{0,1:T(8,128)(2,1)S(1)}, bf16[256,704]{0,1:T(8,128)(2,1)S(1)}, u32[]{:S(2)}, u32[]{:S(2)}) collective-permute-start(bf16[256,704]{0,1:T(8,128)(2,1)S(1)} %collective-permute-done.71), channel_id=1, source_target_pairs={{0,8},{8,16},{16,24},{24,0},{1,9},{9,17},{17,25},{25,1},{2,10},{10... | collective-permute-start | bytes 1081352 | tf_op jit(solution)/shard_map/ppermute | solution.py:73
  163.0 41.2 %collective-permute-start.72 = (bf16[256,704]{0,1:T(8,128)(2,1)S(1)}, bf16[256,704]{0,1:T(8,128)(2,1)S(1)}, u32[]{:S(2)}, u32[]{:S(2)}) collective-permute-start(bf16[256,704]{0,1:T(8,128)(2,1)S(1)} %collective-permute-done.71), channel_id=1, source_target_pairs={{0,4},{4,0},{1,5},{5,1},{2,6},{6,2},{3,7},{7,3},{8,12},{12,8},{9,1... | collective-permute-start | bytes 1081352 | tf_op jit(solution)/shard_map/ppermute | solution.py:73
  204.2 24.7 %collective-permute-start.88 = (bf16[704,256]{1,0:T(8,128)(2,1)}, bf16[704,256]{1,0:T(8,128)(2,1)}, u32[]{:S(2)}, u32[]{:S(2)}) collective-permute-start(bf16[704,256]{1,0:T(8,128)(2,1)} %collective-permute-done.87), channel_id=1, source_target_pairs={{0,4},{4,0},{1,5},{5,1},{2,6},{6,2},{3,7},{7,3},{8,12},{12,8},{9,1... | collective-permute-start | bytes 1081352 | tf_op jit(solution)/shard_map/ppermute | solution.py:73
  207.8 38.6 %collective-permute-start.54 = (bf16[256,768]{1,0:T(8,128)(2,1)}, bf16[256,768]{1,0:T(8,128)(2,1)}, u32[]{:S(2)}, u32[]{:S(2)}) collective-permute-start(bf16[256,768]{1,0:T(8,128)(2,1)} %collective-permute-done.53), channel_id=1, source_target_pairs={{0,4},{4,0},{1,5},{5,1},{2,6},{6,2},{3,7},{7,3},{8,12},{12,8},{9,1... | collective-permute-start | bytes 1179656 | tf_op jit(solution)/shard_map/ppermute | solution.py:73
  232.9 40.6 %collective-permute-start.22 = (bf16[128,576]{0,1:T(8,128)(2,1)}, bf16[128,576]{0,1:T(8,128)(2,1)}, u32[]{:S(2)}, u32[]{:S(2)}) collective-permute-start(bf16[128,576]{0,1:T(8,128)(2,1)} %collective-permute-done.14), channel_id=1, source_target_pairs={{0,8},{8,16},{16,24},{24,0},{1,9},{9,17},{17,25},{25,1},{2,10},{10... | collective-permute-start | bytes 442376 | tf_op jit(solution)/shard_map/ppermute | solution.py:73
  236.3 41.5 %collective-permute-start.18 = (bf16[128,576]{0,1:T(8,128)(2,1)}, bf16[128,576]{0,1:T(8,128)(2,1)}, u32[]{:S(2)}, u32[]{:S(2)}) collective-permute-start(bf16[128,576]{0,1:T(8,128)(2,1)} %collective-permute-done.14), channel_id=1, source_target_pairs={{0,4},{4,0},{1,5},{5,1},{2,6},{6,2},{3,7},{7,3},{8,12},{12,8},{9,1... | collective-permute-start | bytes 442376 | tf_op jit(solution)/shard_map/ppermute | solution.py:73
  237.7 41.8 %collective-permute-start.16 = (bf16[128,576]{0,1:T(8,128)(2,1)}, bf16[128,576]{0,1:T(8,128)(2,1)}, u32[]{:S(2)}, u32[]{:S(2)}) collective-permute-start(bf16[128,576]{0,1:T(8,128)(2,1)} %collective-permute-done.14), channel_id=1, source_target_pairs={{0,2},{2,0},{1,3},{3,1},{4,6},{6,4},{5,7},{7,5},{8,10},{10,8},{9,1... | collective-permute-start | bytes 442376 | tf_op jit(solution)/shard_map/ppermute | solution.py:73
  240.0 27.3 %collective-permute-start.12 = (bf16[128,576]{0,1:T(8,128)(2,1)}, bf16[128,576]{0,1:T(8,128)(2,1)}, u32[]{:S(2)}, u32[]{:S(2)}) collective-permute-start(bf16[128,576]{0,1:T(8,128)(2,1)} %collective-permute-done.10), channel_id=1, source_target_pairs={{0,2},{2,0},{1,3},{3,1},{4,6},{6,4},{5,7},{7,5},{8,10},{10,8},{9,1... | collective-permute-start | bytes 442376 | tf_op jit(solution)/shard_map/ppermute | solution.py:73
  273.5 33.1 %collective-permute-start.101 = (bf16[128,2048]{1,0:T(8,128)(2,1)}, bf16[128,2048]{1,0:T(8,128)(2,1)}, u32[]{:S(2)}, u32[]{:S(2)}) collective-permute-start(bf16[128,2048]{1,0:T(8,128)(2,1)} %bitcast.383), channel_id=1, source_target_pairs={{0,8},{8,16},{16,24},{24,0},{1,9},{9,17},{17,25},{25,1},{2,10},{10... | collective-permute-start | bytes 1572872 | tf_op jit(solution)/shard_map/ppermute | solution.py:73
  275.2 33.4 %collective-permute-start.30 = (bf16[128,576]{0,1:T(8,128)(2,1)}, bf16[128,576]{0,1:T(8,128)(2,1)S(1)}, u32[]{:S(2)}, u32[]{:S(2)}) collective-permute-start(bf16[128,576]{0,1:T(8,128)(2,1)} %collective-permute-done.22), channel_id=1, source_target_pairs={{0,8},{8,16},{16,24},{24,0},{1,9},{9,17},{17,25},{25,1},{2,10},{10... | collective-permute-start | bytes 442376 | tf_op jit(solution)/shard_map/ppermute | solution.py:73
  306.6 32.2 %collective-permute-start.108 = (bf16[128,2048]{1,0:T(8,128)(2,1)}, bf16[128,2048]{1,0:T(8,128)(2,1)}, u32[]{:S(2)}, u32[]{:S(2)}) collective-permute-start(bf16[128,2048]{1,0:T(8,128)(2,1)} %bitcast.384), channel_id=1, source_target_pairs={{0,2},{2,0},{1,3},{3,1},{4,6},{6,4},{5,7},{7,5},{8,10},{10,8},{9,1... | collective-permute-start | bytes 1572872 | tf_op jit(solution)/shard_map/ppermute | solution.py:73
  308.6 30.7 %collective-permute-start.102 = (bf16[128,2048]{1,0:T(8,128)(2,1)}, bf16[128,2048]{1,0:T(8,128)(2,1)}, u32[]{:S(2)}, u32[]{:S(2)}) collective-permute-start(bf16[128,2048]{1,0:T(8,128)(2,1)} %collective-permute-done.101), channel_id=1, source_target_pairs={{0,8},{8,16},{16,24},{24,0},{1,9},{9,17},{17,25},{25,1},{2,10},{10... | collective-permute-start | bytes 1572872 | tf_op jit(solution)/shard_map/ppermute | solution.py:73
  338.8 80.1 %collective-permute-start.107 = (bf16[128,2048]{1,0:T(8,128)(2,1)}, bf16[128,2048]{1,0:T(8,128)(2,1)}, u32[]{:S(2)}, u32[]{:S(2)}) collective-permute-start(bf16[128,2048]{1,0:T(8,128)(2,1)} %bitcast.385), channel_id=1, source_target_pairs={{0,1},{1,0},{2,3},{3,2},{4,5},{5,4},{6,7},{7,6},{8,9},{9,8},{10,11... | collective-permute-start | bytes 1572872 | tf_op jit(solution)/shard_map/ppermute | solution.py:73
  339.3 79.9 %collective-permute-start.109 = (bf16[128,2048]{1,0:T(8,128)(2,1)}, bf16[128,2048]{1,0:T(8,128)(2,1)}, u32[]{:S(2)}, u32[]{:S(2)}) collective-permute-start(bf16[128,2048]{1,0:T(8,128)(2,1)} %collective-permute-done.108), channel_id=1, source_target_pairs={{0,1},{1,0},{2,3},{3,2},{4,5},{5,4},{6,7},{7,6},{8,9},{9,8},{10,11... | collective-permute-start | bytes 1572872 | tf_op jit(solution)/shard_map/ppermute | solution.py:73
  339.4 88.7 %collective-permute-start.103 = (bf16[128,2048]{1,0:T(8,128)(2,1)}, bf16[128,2048]{1,0:T(8,128)(2,1)}, u32[]{:S(2)}, u32[]{:S(2)}) collective-permute-start(bf16[128,2048]{1,0:T(8,128)(2,1)} %collective-permute-done.102), channel_id=1, source_target_pairs={{0,8},{8,16},{16,24},{24,0},{1,9},{9,17},{17,25},{25,1},{2,10},{10... | collective-permute-start | bytes 1572872 | tf_op jit(solution)/shard_map/ppermute | solution.py:73
  360.6 65.8 %collective-permute-start.74 = (bf16[256,704]{0,1:T(8,128)(2,1)}, bf16[256,704]{0,1:T(8,128)(2,1)}, u32[]{:S(2)}, u32[]{:S(2)}) collective-permute-start(bf16[256,704]{0,1:T(8,128)(2,1)} %copy-done.118), channel_id=1, source_target_pairs={{0,4},{4,0},{1,5},{5,1},{2,6},{6,2},{3,7},{7,3},{8,12},{12,8},{9,1... | collective-permute-start | bytes 1081352 | tf_op jit(solution)/shard_map/ppermute | solution.py:73
  367.7 57.6 %collective-permute-start.81 = (bf16[256,704]{0,1:T(8,128)(2,1)}, bf16[256,704]{0,1:T(8,128)(2,1)}, u32[]{:S(2)}, u32[]{:S(2)}) collective-permute-start(bf16[256,704]{0,1:T(8,128)(2,1)} %copy-done.119), channel_id=1, source_target_pairs={{0,4},{4,0},{1,5},{5,1},{2,6},{6,2},{3,7},{7,3},{8,12},{12,8},{9,1... | collective-permute-start | bytes 1081352 | tf_op jit(solution)/shard_map/ppermute | solution.py:73
  441.1 41.6 %collective-permute-start.65 = (bf16[128,2048]{1,0:T(8,128)(2,1)S(1)}, bf16[128,2048]{1,0:T(8,128)(2,1)}, u32[]{:S(2)}, u32[]{:S(2)}) collective-permute-start(bf16[128,2048]{1,0:T(8,128)(2,1)S(1)} %multiply_convert_fusion.12), channel_id=1, source_target_pairs={{0,1},{1,0},{2,3},{3,2},{4,5},{5,4},{6,7},{7,6},{8,9},{9,8},{10,11... | collective-permute-start | bytes 1572872 | tf_op jit(solution)/shard_map/ppermute | solution.py:73
  444.6 37.9 %collective-permute-start.95 = (bf16[128,2176]{1,0:T(8,128)(2,1)}, bf16[128,2176]{1,0:T(8,128)(2,1)S(1)}, u32[]{:S(2)}, u32[]{:S(2)}) collective-permute-start(bf16[128,2176]{1,0:T(8,128)(2,1)} %concatenate.114), channel_id=1, source_target_pairs={{0,8},{8,16},{16,24},{24,0},{1,9},{9,17},{17,25},{25,1},{2,10},{10... | collective-permute-start | bytes 1671176 | tf_op jit(solution)/shard_map/ppermute | solution.py:73
  453.9 28.8 %collective-permute-start.67 = (bf16[128,2048]{1,0:T(8,128)(2,1)}, bf16[128,2048]{1,0:T(8,128)(2,1)S(1)}, u32[]{:S(2)}, u32[]{:S(2)}) collective-permute-start(bf16[128,2048]{1,0:T(8,128)(2,1)} %collective-permute-done.66), channel_id=1, source_target_pairs={{0,1},{1,0},{2,3},{3,2},{4,5},{5,4},{6,7},{7,6},{8,9},{9,8},{10,11... | collective-permute-start | bytes 1572872 | tf_op jit(solution)/shard_map/ppermute | solution.py:73
  482.5 34.4 %collective-permute-start.96 = (bf16[128,2176]{1,0:T(8,128)(2,1)S(1)}, bf16[128,2176]{1,0:T(8,128)(2,1)S(1)}, u32[]{:S(2)}, u32[]{:S(2)}) collective-permute-start(bf16[128,2176]{1,0:T(8,128)(2,1)S(1)} %collective-permute-done.95), channel_id=1, source_target_pairs={{0,8},{8,16},{16,24},{24,0},{1,9},{9,17},{17,25},{25,1},{2,10},{10... | collective-permute-start | bytes 1671176 | tf_op jit(solution)/shard_map/ppermute | solution.py:73
  495.2 51.1 %collective-permute-start.89 = (bf16[128,2048]{1,0:T(8,128)(2,1)}, bf16[128,2048]{1,0:T(8,128)(2,1)}, u32[]{:S(2)}, u32[]{:S(2)}) collective-permute-start(bf16[128,2048]{1,0:T(8,128)(2,1)} %get-tuple-element.109), channel_id=1, source_target_pairs={{0,1},{1,0},{2,3},{3,2},{4,5},{5,4},{6,7},{7,6},{8,9},{9,8},{10,11... | collective-permute-start | bytes 1572872 | tf_op jit(solution)/shard_map/ppermute | solution.py:73
  502.6 45.9 %collective-permute-start.110 = (bf16[128,2048]{1,0:T(8,128)(2,1)}, bf16[128,2048]{1,0:T(8,128)(2,1)}, u32[]{:S(2)}, u32[]{:S(2)}) collective-permute-start(bf16[128,2048]{1,0:T(8,128)(2,1)} %get-tuple-element.107), channel_id=1, source_target_pairs={{0,1},{1,0},{2,3},{3,2},{4,5},{5,4},{6,7},{7,6},{8,9},{9,8},{10,11... | collective-permute-start | bytes 1572872 | tf_op jit(solution)/shard_map/ppermute | solution.py:73
  518.7 355.8 %collective-permute-start.112 = (bf16[128,2048]{1,0:T(8,128)(2,1)}, bf16[128,2048]{1,0:T(8,128)(2,1)}, u32[]{:S(2)}, u32[]{:S(2)}) collective-permute-start(bf16[128,2048]{1,0:T(8,128)(2,1)} %get-tuple-element.108), channel_id=1, source_target_pairs={{0,1},{1,0},{2,3},{3,2},{4,5},{5,4},{6,7},{7,6},{8,9},{9,8},{10,11... | collective-permute-start | bytes 1572872 | tf_op jit(solution)/shard_map/ppermute | solution.py:73
  525.5 28.2 %collective-permute-start.205 = (bf16[704,256]{1,0:T(8,128)(2,1)}, bf16[704,256]{1,0:T(8,128)(2,1)}, u32[]{:S(2)}, u32[]{:S(2)}) collective-permute-start(bf16[704,256]{1,0:T(8,128)(2,1)} %get-tuple-element.80), channel_id=1, source_target_pairs={{0,4},{4,0},{1,5},{5,1},{2,6},{6,2},{3,7},{7,3},{8,12},{12,8},{9,1... | collective-permute-start | bytes 1081352 | tf_op jit(solution)/shard_map/ppermute | solution.py:73
  536.7 36.8 %all-to-all-start = ((bf16[8,56,2176]{2,1,0:T(8,128)(2,1)}), bf16[8,56,2176]{2,1,0:T(8,128)(2,1)}, u32[]{:S(2)}, u32[]{:S(2)}) async-start(bf16[8,56,2176]{2,1,0:T(8,128)(2,1)} %fusion.108), calls=%async_computation | async-start | bytes 3899392 | tf_op jit(solution)/shard_map/all_to_all | solution.py:256
  543.0 30.4 %collective-permute-start.198 = (bf16[256,704]{0,1:T(8,128)(2,1)}, bf16[256,704]{0,1:T(8,128)(2,1)}, u32[]{:S(2)}, u32[]{:S(2)}) collective-permute-start(bf16[256,704]{0,1:T(8,128)(2,1)} %get-tuple-element.84), channel_id=1, source_target_pairs={{0,4},{4,0},{1,5},{5,1},{2,6},{6,2},{3,7},{7,3},{8,12},{12,8},{9,1... | collective-permute-start | bytes 1081352 | tf_op jit(solution)/shard_map/ppermute | solution.py:73
  548.4 29.5 %collective-permute-start.197 = (bf16[256,704]{0,1:T(8,128)(2,1)}, bf16[256,704]{0,1:T(8,128)(2,1)}, u32[]{:S(2)}, u32[]{:S(2)}) collective-permute-start(bf16[256,704]{0,1:T(8,128)(2,1)} %add_convert_fusion.15), channel_id=1, source_target_pairs={{0,8},{8,16},{16,24},{24,0},{1,9},{9,17},{17,25},{25,1},{2,10},{10... | collective-permute-start | bytes 1081352 | tf_op jit(solution)/shard_map/ppermute | solution.py:73
  553.7 27.5 %collective-permute-start.191 = (bf16[256,704]{0,1:T(8,128)(2,1)}, bf16[256,704]{0,1:T(8,128)(2,1)}, u32[]{:S(2)}, u32[]{:S(2)}) collective-permute-start(bf16[256,704]{0,1:T(8,128)(2,1)} %get-tuple-element.88), channel_id=1, source_target_pairs={{0,4},{4,0},{1,5},{5,1},{2,6},{6,2},{3,7},{7,3},{8,12},{12,8},{9,1... | collective-permute-start | bytes 1081352 | tf_op jit(solution)/shard_map/ppermute | solution.py:73
  573.6 70.4 %all-to-all-start.2 = ((bf16[8,56,2176]{2,1,0:T(8,128)(2,1)}), bf16[8,56,2176]{2,1,0:T(8,128)(2,1)}, u32[]{:S(2)}, u32[]{:S(2)}) async-start(bf16[8,56,2176]{2,1,0:T(8,128)(2,1)} %fusion.107), calls=%async_computation.2 | async-start | bytes 3899392 | tf_op jit(solution)/shard_map/all_to_all | solution.py:256
  581.1 36.2 %collective-permute-start.200 = (bf16[256,704]{0,1:T(8,128)(2,1)}, bf16[256,704]{0,1:T(8,128)(2,1)S(1)}, u32[]{:S(2)}, u32[]{:S(2)}) collective-permute-start(bf16[256,704]{0,1:T(8,128)(2,1)} %get-tuple-element.83), channel_id=1, source_target_pairs={{0,4},{4,0},{1,5},{5,1},{2,6},{6,2},{3,7},{7,3},{8,12},{12,8},{9,1... | collective-permute-start | bytes 1081352 | tf_op jit(solution)/shard_map/ppermute | solution.py:73
  581.4 36.2 %collective-permute-start.199 = (bf16[256,704]{0,1:T(8,128)(2,1)S(1)}, bf16[256,704]{0,1:T(8,128)(2,1)S(1)}, u32[]{:S(2)}, u32[]{:S(2)}) collective-permute-start(bf16[256,704]{0,1:T(8,128)(2,1)S(1)} %add_convert_fusion.14), channel_id=1, source_target_pairs={{0,8},{8,16},{16,24},{24,0},{1,9},{9,17},{17,25},{25,1},{2,10},{10... | collective-permute-start | bytes 1081352 | tf_op jit(solution)/shard_map/ppermute | solution.py:73
  588.9 36.2 %collective-permute-start.193 = (bf16[256,704]{0,1:T(8,128)(2,1)}, bf16[256,704]{0,1:T(8,128)(2,1)S(1)}, u32[]{:S(2)}, u32[]{:S(2)}) collective-permute-start(bf16[256,704]{0,1:T(8,128)(2,1)} %get-tuple-element.87), channel_id=1, source_target_pairs={{0,4},{4,0},{1,5},{5,1},{2,6},{6,2},{3,7},{7,3},{8,12},{12,8},{9,1... | collective-permute-start | bytes 1081352 | tf_op jit(solution)/shard_map/ppermute | solution.py:73
  592.0 33.3 %collective-permute-start.192 = (bf16[256,704]{0,1:T(8,128)(2,1)S(1)}, bf16[256,704]{0,1:T(8,128)(2,1)S(1)}, u32[]{:S(2)}, u32[]{:S(2)}) collective-permute-start(bf16[256,704]{0,1:T(8,128)(2,1)S(1)} %add_convert_fusion.17), channel_id=1, source_target_pairs={{0,8},{8,16},{16,24},{24,0},{1,9},{9,17},{17,25},{25,1},{2,10},{10... | collective-permute-start | bytes 1081352 | tf_op jit(solution)/shard_map/ppermute | solution.py:73
  640.5 234.0 %collective-permute-start.111 = (bf16[128,2048]{1,0:T(8,128)(2,1)}, bf16[128,2048]{1,0:T(8,128)(2,1)}, u32[]{:S(2)}, u32[]{:S(2)}) collective-permute-start(bf16[128,2048]{1,0:T(8,128)(2,1)} %add_convert_fusion.4), channel_id=1, source_target_pairs={{0,2},{2,0},{1,3},{3,1},{4,6},{6,4},{5,7},{7,5},{8,10},{10,8},{9,1... | collective-permute-start | bytes 1572872 | tf_op jit(solution)/shard_map/ppermute | solution.py:73
  644.0 29.6 %all-to-all-start.6 = ((bf16[8,56,2048]{2,1,0:T(8,128)(2,1)}), bf16[8,56,2048]{2,1,0:T(8,128)(2,1)}, u32[]{:S(2)}, u32[]{:S(2)}) async-start(bf16[8,56,2048]{2,1,0:T(8,128)(2,1)} %fusion.109), calls=%async_computation.6 | async-start | bytes 3670016 | tf_op jit(solution)/shard_map/all_to_all | solution.py:256
  673.6 31.2 %all-to-all-start.4 = ((bf16[8,56,2048]{2,1,0:T(8,128)(2,1)}), bf16[8,56,2048]{2,1,0:T(8,128)(2,1)S(1)}, u32[]{:S(2)}, u32[]{:S(2)}) async-start(bf16[8,56,2048]{2,1,0:T(8,128)(2,1)} %fusion.111), calls=%async_computation.4 | async-start | bytes 3670016 | tf_op jit(solution)/shard_map/all_to_all | solution.py:256
  736.7 44.8 %all-to-all-start.5 = ((bf16[8,56,2176]{2,1,0:T(8,128)(2,1)}), bf16[8,56,2176]{2,1,0:T(8,128)(2,1)S(1)}, u32[]{:S(2)}, u32[]{:S(2)}) async-start(bf16[8,56,2176]{2,1,0:T(8,128)(2,1)} %bitcast.81), calls=%async_computation.5 | async-start | bytes 3899392 | tf_op jit(solution)/shard_map/all_to_all | solution.py:265
  782.8 29.2 %all-to-all-start.7 = ((bf16[8,56,2176]{2,1,0:T(8,128)(2,1)}), bf16[8,56,2176]{2,1,0:T(8,128)(2,1)S(1)}, u32[]{:S(2)}, u32[]{:S(2)}) async-start(bf16[8,56,2176]{2,1,0:T(8,128)(2,1)} %bitcast.85), calls=%async_computation.7 | async-start | bytes 3899392 | tf_op jit(solution)/shard_map/all_to_all | solution.py:265
  812.1 51.7 %all-to-all-start.1 = ((bf16[8,56,2048]{2,1,0:T(8,128)(2,1)}), bf16[8,56,2048]{2,1,0:T(8,128)(2,1)}, u32[]{:S(2)}, u32[]{:S(2)}) async-start(bf16[8,56,2048]{2,1,0:T(8,128)(2,1)} %bitcast.393), calls=%async_computation.1 | async-start | bytes 3670016 | tf_op jit(solution)/shard_map/all_to_all | solution.py:265
  863.8 27.3 %all-to-all-start.3 = ((bf16[8,56,2048]{2,1,0:T(8,128)(2,1)}), bf16[8,56,2048]{2,1,0:T(8,128)(2,1)S(1)}, u32[]{:S(2)}, u32[]{:S(2)}) async-start(bf16[8,56,2048]{2,1,0:T(8,128)(2,1)} %bitcast.392), calls=%async_computation.3 | async-start | bytes 3670016 | tf_op jit(solution)/shard_map/all_to_all | solution.py:265
  917.0 23.8 %collective-permute-start.113 = (bf16[128,2048]{1,0:T(8,128)(2,1)S(1)}, bf16[128,2048]{1,0:T(8,128)(2,1)S(1)}, u32[]{:S(2)}, u32[]{:S(2)}) collective-permute-start(bf16[128,2048]{1,0:T(8,128)(2,1)S(1)} %fusion.215), channel_id=1, source_target_pairs={{0,1},{1,0},{2,3},{3,2},{4,5},{5,4},{6,7},{7,6},{8,9},{9,8},{10,11... | collective-permute-start | bytes 1572872 | tf_op jit(solution)/shard_map/ppermute | solution.py:73
  1042.1 107.7 %collective-permute-start.116 = (bf16[128,2048]{1,0:T(8,128)(2,1)}, bf16[128,2048]{1,0:T(8,128)(2,1)}, u32[]{:S(2)}, u32[]{:S(2)}) collective-permute-start(bf16[128,2048]{1,0:T(8,128)(2,1)} %get-tuple-element.103), channel_id=1, source_target_pairs={{0,1},{1,0},{2,3},{3,2},{4,5},{5,4},{6,7},{7,6},{8,9},{9,8},{10,11... | collective-permute-start | bytes 1572872 | tf_op jit(solution)/shard_map/ppermute | solution.py:73
  1044.0 53.6 %collective-permute-start.147 = (bf16[128,576]{0,1:T(8,128)(2,1)}, bf16[128,576]{0,1:T(8,128)(2,1)}, u32[]{:S(2)}, u32[]{:S(2)}) collective-permute-start(bf16[128,576]{0,1:T(8,128)(2,1)} %copy.817), channel_id=1, source_target_pairs={{0,1},{1,0},{2,3},{3,2},{4,5},{5,4},{6,7},{7,6},{8,9},{9,8},{10,11... | collective-permute-start | bytes 442376 | tf_op jit(solution)/shard_map/ppermute | solution.py:73
  1050.2 50.8 %collective-permute-start.143 = (bf16[128,576]{0,1:T(8,128)(2,1)}, bf16[128,576]{0,1:T(8,128)(2,1)}, u32[]{:S(2)}, u32[]{:S(2)}) collective-permute-start(bf16[128,576]{0,1:T(8,128)(2,1)} %copy.813), channel_id=1, source_target_pairs={{0,1},{1,0},{2,3},{3,2},{4,5},{5,4},{6,7},{7,6},{8,9},{9,8},{10,11... | collective-permute-start | bytes 442376 | tf_op jit(solution)/shard_map/ppermute | solution.py:73
  1050.5 49.3 %collective-permute-start.139 = (bf16[128,576]{0,1:T(8,128)(2,1)}, bf16[128,576]{0,1:T(8,128)(2,1)}, u32[]{:S(2)}, u32[]{:S(2)}) collective-permute-start(bf16[128,576]{0,1:T(8,128)(2,1)} %copy.809), channel_id=1, source_target_pairs={{0,1},{1,0},{2,3},{3,2},{4,5},{5,4},{6,7},{7,6},{8,9},{9,8},{10,11... | collective-permute-start | bytes 442376 | tf_op jit(solution)/shard_map/ppermute | solution.py:73
  1050.7 74.9 %collective-permute-start.137 = (bf16[128,576]{0,1:T(8,128)(2,1)}, bf16[128,576]{0,1:T(8,128)(2,1)}, u32[]{:S(2)}, u32[]{:S(2)}) collective-permute-start(bf16[128,576]{0,1:T(8,128)(2,1)} %copy.807), channel_id=1, source_target_pairs={{0,1},{1,0},{2,3},{3,2},{4,5},{5,4},{6,7},{7,6},{8,9},{9,8},{10,11... | collective-permute-start | bytes 442376 | tf_op jit(solution)/shard_map/ppermute | solution.py:73
  1142.1 35.2 %collective-permute-start.173 = (bf16[512,256]{1,0:T(8,128)(2,1)}, bf16[512,256]{1,0:T(8,128)(2,1)}, u32[]{:S(2)}, u32[]{:S(2)}) collective-permute-start(bf16[512,256]{1,0:T(8,128)(2,1)} %get-tuple-element.99), channel_id=1, source_target_pairs={{0,4},{4,0},{1,5},{5,1},{2,6},{6,2},{3,7},{7,3},{8,12},{12,8},{9,1... | collective-permute-start | bytes 786440 | tf_op jit(solution)/shard_map/ppermute | solution.py:73
  1151.2 87.7 %collective-permute-start.177 = (bf16[512,256]{1,0:T(8,128)(2,1)S(1)}, bf16[512,256]{1,0:T(8,128)(2,1)}, u32[]{:S(2)}, u32[]{:S(2)}) collective-permute-start(bf16[512,256]{1,0:T(8,128)(2,1)S(1)} %copy-done.124), channel_id=1, source_target_pairs={{0,4},{4,0},{1,5},{5,1},{2,6},{6,2},{3,7},{7,3},{8,12},{12,8},{9,1... | collective-permute-start | bytes 786440 | tf_op jit(solution)/shard_map/ppermute | solution.py:73
  1151.8 58.8 %collective-permute-start.175 = (bf16[512,256]{1,0:T(8,128)(2,1)}, bf16[512,256]{1,0:T(8,128)(2,1)}, u32[]{:S(2)}, u32[]{:S(2)}) collective-permute-start(bf16[512,256]{1,0:T(8,128)(2,1)} %get-tuple-element.102), channel_id=1, source_target_pairs={{0,4},{4,0},{1,5},{5,1},{2,6},{6,2},{3,7},{7,3},{8,12},{12,8},{9,1... | collective-permute-start | bytes 786440 | tf_op jit(solution)/shard_map/ppermute | solution.py:73
  1160.5 33.1 %collective-permute-start.159 = (bf16[256,768]{1,0:T(8,128)(2,1)}, bf16[256,768]{1,0:T(8,128)(2,1)S(1)}, u32[]{:S(2)}, u32[]{:S(2)}) collective-permute-start(bf16[256,768]{1,0:T(8,128)(2,1)} %get-tuple-element.73), channel_id=1, source_target_pairs={{0,4},{4,0},{1,5},{5,1},{2,6},{6,2},{3,7},{7,3},{8,12},{12,8},{9,1... | collective-permute-start | bytes 1179656 | tf_op jit(solution)/shard_map/ppermute | solution.py:73
  1232.1 30.0 %collective-permute-start.91 = (bf16[128,2048]{1,0:T(8,128)(2,1)S(1)}, bf16[128,2048]{1,0:T(8,128)(2,1)S(1)}, u32[]{:S(2)}, u32[]{:S(2)}) collective-permute-start(bf16[128,2048]{1,0:T(8,128)(2,1)S(1)} %copy-done.101), channel_id=1, source_target_pairs={{0,1},{1,0},{2,3},{3,2},{4,5},{5,4},{6,7},{7,6},{8,9},{9,8},{10,11... | collective-permute-start | bytes 1572872 | tf_op jit(solution)/shard_map/ppermute | solution.py:73
  1237.3 24.9 %collective-permute-start.90 = (bf16[128,2048]{1,0:T(8,128)(2,1)S(1)}, bf16[128,2048]{1,0:T(8,128)(2,1)S(1)}, u32[]{:S(2)}, u32[]{:S(2)}) collective-permute-start(bf16[128,2048]{1,0:T(8,128)(2,1)S(1)} %copy-done.98), channel_id=1, source_target_pairs={{0,2},{2,0},{1,3},{3,1},{4,6},{6,4},{5,7},{7,5},{8,10},{10,8},{9,1... | collective-permute-start | bytes 1572872 | tf_op jit(solution)/shard_map/ppermute | solution.py:73
  1238.9 25.2 %collective-permute-start.100 = (bf16[128,2048]{1,0:T(8,128)(2,1)S(1)}, bf16[128,2048]{1,0:T(8,128)(2,1)S(1)}, u32[]{:S(2)}, u32[]{:S(2)}) collective-permute-start(bf16[128,2048]{1,0:T(8,128)(2,1)S(1)} %copy-done.102), channel_id=1, source_target_pairs={{0,8},{8,16},{16,24},{24,0},{1,9},{9,17},{17,25},{25,1},{2,10},{10... | collective-permute-start | bytes 1572872 | tf_op jit(solution)/shard_map/ppermute | solution.py:73
  (372 other events, 5121.5 us)

commit v2 on v1

v2 whole, which is shorter than its diff:
```python
import functools

import jax
import jax.numpy as jnp
from jax import lax
from jax.experimental import pallas as pl
from jax.experimental.pallas import tpu as pltpu
from jax.sharding import Mesh
from jax.sharding import PartitionSpec as P

H = 16
NOPE = 128
RD = 64
VH = 128
KVR = 512
EXPERTS = 64
TOP = 6
CAP = 14
SLOTS = 16
Z_SIZE = 4
CORES = 2

epsilon = 1e-06
rope_base = 10000.0
wide = jnp.float32
narrow = jnp.bfloat16


def dot(a, b, out=wide):
    return jnp.dot(a, b, preferred_element_type=out)


def dot_tn(a, b, out=wide):
    return lax.dot_general(a, b, (((0,), (0,)), ((), ())), preferred_element_type=out)


def dot_nt(a, b, out=wide):
    return lax.dot_general(a, b, (((1,), (1,)), ((), ())), preferred_element_type=out)


def norm_rows(values, gain):
    inverse = lax.rsqrt(jnp.mean(values * values, axis=-1, keepdims=True) + epsilon)
    normed = values * inverse
    return (normed * gain, normed, inverse)


def norm_input_back(grad_out, normed, inverse, gain):
    scaled = grad_out * gain
    return inverse * (scaled - normed * jnp.mean(scaled * normed, axis=-1, keepdims=True))


def rotary_tables(positions):
    half_width = RD // 2
    frequency = rope_base ** (-2.0 * jnp.arange(half_width).astype(wide) / RD)
    angles = positions.astype(wide)[:, None] * frequency[None, :]
    return (jnp.cos(angles), jnp.sin(angles))


def rotate(values, cosine, sine):
    half = RD // 2
    a, b = values[..., :half], values[..., half:]
    return jnp.concatenate([a * cosine - b * sine, b * cosine + a * sine], axis=-1)


def unrotate(values, cosine, sine):
    half = RD // 2
    a, b = values[..., :half], values[..., half:]
    return jnp.concatenate([a * cosine + b * sine, b * cosine - a * sine], axis=-1)


def silu_slope(values):
    s = jax.nn.sigmoid(values)
    return s * (1.0 + values * (1.0 - s))


def hop(value, axis):
    n = lax.axis_size(axis)
    return lax.ppermute(value, axis, [(i, (i + 1) % n) for i in range(n)])


def ring(value, axis):
    items = [value]
    for _ in range(lax.axis_size(axis) - 1):
        items.append(hop(items[-1], axis))
    return items


def ring_sum(blocks, axis):
    n = lax.axis_size(axis)
    if n == 1:
        return blocks[0].astype(wide)
    running = hop(blocks[1].astype(narrow), axis)
    for s in range(2, n):
        running = hop((running.astype(wide) + blocks[s].astype(wide)).astype(narrow), axis)
    return running.astype(wide) + blocks[0].astype(wide)


def flat_ring(value, axes):
    items = [value]
    for axis in axes:
        items = [piece for item in items for piece in ring(item, axis)]
    return items


def tree_sum(blocks, axes):
    for axis in reversed(axes):
        n = lax.axis_size(axis)
        blocks = [ring_sum(blocks[i : i + n], axis) for i in range(0, len(blocks), n)]
    return blocks[0]


ANY = pl.BlockSpec(memory_space=pl.ANY)
VMEM = pl.BlockSpec(memory_space=pltpu.VMEM)
MESH = pl.DeviceIdType.MESH
AXES = ("z", "x", "y", "core")


def behind(axis, steps):
    n = lax.axis_size(axis)
    return lax.rem(lax.axis_index(axis) + (n - steps), n)


def ahead(axis):
    n = lax.axis_size(axis)
    return lax.rem(lax.axis_index(axis) + 1, n)


def greet(axes):
    barrier = pltpu.get_barrier_semaphore()
    for axis in axes:
        pl.semaphore_signal(
            barrier, inc=1, device_id={axis: behind(axis, 1)}, device_id_type=MESH
        )
    pl.semaphore_wait(barrier, len(axes))


class Wires:
    def __init__(self, send, recv):
        self.send, self.recv, self.used, self.sent = send, recv, 0, []

    def port(self):
        self.used += 1
        return self.used - 1

    def push(self, src, dst, port, axis):
        copy = pltpu.make_async_remote_copy(
            src_ref=src,
            dst_ref=dst,
            send_sem=self.send.at[port],
            recv_sem=self.recv.at[port],
            device_id={axis: ahead(axis)},
            device_id_type=MESH,
        )
        copy.start()
        self.sent.append(copy)

    def arrived(self, dst, port, axis):
        pltpu.make_async_remote_copy(
            src_ref=dst,
            dst_ref=dst,
            send_sem=self.send.at[port],
            recv_sem=self.recv.at[port],
            device_id={axis: ahead(axis)},
            device_id_type=MESH,
        ).wait_recv()

    def drain(self):
        for copy in self.sent:
            copy.wait_send()


class BlockGather:
    def __init__(self, wires, src, dst, place, x_first):
        self.wires, self.src, self.dst, self.place, self.x_first = wires, src, dst, place, x_first
        self.nz, self.nx = lax.axis_size("z"), lax.axis_size("x")
        self.ports = {
            (sz, sx): wires.port() for sz in range(self.nz) for sx in range(self.nx) if sz or sx
        }

    def at(self, sz, sx):
        return self.place(self.dst, behind("z", sz) * self.nx + behind("x", sx))

    def forward(self, sz, sx):
        src = self.src if sz == 0 and sx == 0 else self.at(sz, sx)
        if self.x_first:
            go_x, go_z = sz == 0, True
        else:
            go_x, go_z = True, sx == 0
        if go_z and sz + 1 < self.nz:
            self.wires.push(src, self.at(sz, sx), self.ports[sz + 1, sx], "z")
        if go_x and sx + 1 < self.nx:
            self.wires.push(src, self.at(sz, sx), self.ports[sz, sx + 1], "x")

    def take(self, sz, sx):
        from_x = sx > 0 and (sz == 0 if self.x_first else True)
        self.wires.arrived(self.at(sz, sx), self.ports[sz, sx], "x" if from_x else "z")
        self.forward(sz, sx)

    def chain(self):
        self.forward(0, 0)
        for slots in self.rounds():
            for slot in slots:
                yield
                self.take(*slot)

    def rounds(self):
        if self.x_first:
            order = [[(0, sx)] for sx in range(1, self.nx)]
            order += [[(sz, sx) for sx in range(self.nx)] for sz in range(1, self.nz)]
            return order
        last = [[(sz, sx) for sz in range(self.nz)] for sx in range(1, self.nx)]
        return [[(sz, 0)] for sz in range(1, self.nz)] + last


def rows_of(size):
    return lambda ref, owner: ref.at[pl.ds(pl.multiple_of(owner * size, size), size)]


def columns_of(size):
    return lambda ref, owner: ref.at[:, pl.ds(pl.multiple_of(owner * size, size), size)]


def start_kernel(
    tokens, grads, cosine, sine, gains, small, routes, w_query, w_expand, w_output,
    gains_out, small_out, query_out, expand_out, output_out,
    tokens_out, grads_out, line_out, routes_out, latents_out, hidden_out, latent_all_out,
    own_latent, send, recv, local,
):
    nz, nx, ny, nc = (lax.axis_size(a) for a in AXES)
    nb, nu = nz * nx, ny * nc
    me = lax.axis_index("z") * nx + lax.axis_index("x")
    uly = lax.axis_index("y") * nc + lax.axis_index("core")
    seqs, local_len, features = tokens.shape
    rows = seqs * local_len
    greet(AXES)
    wires = Wires(send, recv)
    used, waited = [], set()

    def load(src, dst):
        copy = pltpu.make_async_copy(src, dst, local.at[len(used)])
        used.append(copy)
        copy.start()
        return copy

    def member(sy, sc):
        return behind("y", sy) * nc + behind("core", sc)

    def line_chain(src, dst):
        ports = [wires.port() for _ in range(nz)]
        wires.push(src, dst.at[1], ports[1], "z")
        load(src, dst.at[0])
        for sz in range(1, nz):
            yield
            wires.arrived(dst.at[sz], ports[sz], "z")
            if sz + 1 < nz:
                wires.push(dst.at[sz], dst.at[sz + 1], ports[sz + 1], "z")

    def main():
        g_gains = BlockGather(wires, gains, gains_out, lambda ref, owner: ref.at[owner], False)
        g_small = BlockGather(
            wires, small.at[uly], small_out, lambda ref, owner: ref.at[owner, uly], False
        )
        slots = [(0, 0)] + [slot for r in g_small.rounds() for slot in r]
        y_ports = {(slot, sy): wires.port() for slot in slots for sy in range(1, ny)}
        c_ports = {(slot, sy): wires.port() for slot in slots for sy in range(ny)}

        def piece(slot, sy, sc):
            owner = behind("z", slot[0]) * nx + behind("x", slot[1])
            return small_out.at[owner, member(sy, sc)]

        def spread(slot):
            here = piece(slot, 0, 0)
            if ny > 1:
                wires.push(here, here, y_ports[slot, 1], "y")
            wires.push(here, here, c_ports[slot, 0], "core")

        g_small.forward(0, 0)
        g_gains.forward(0, 0)
        mine = [load(small.at[uly], small_out.at[me, uly]), load(gains, gains_out.at[me])]
        yield
        for slots_now in g_small.rounds():
            for slot in slots_now:
                yield
                g_small.take(*slot)
                if mine:
                    for copy in mine:
                        copy.wait()
                    waited.update(id(copy) for copy in mine)
                    mine = []
                    spread((0, 0))
                spread(slot)
                g_gains.take(*slot)
        for sy in range(1, ny):
            for slot in slots:
                yield
                here = piece(slot, sy, 0)
                wires.arrived(here, y_ports[slot, sy], "y")
                if sy + 1 < ny:
                    wires.push(here, here, y_ports[slot, sy + 1], "y")
                wires.push(here, here, c_ports[slot, sy], "core")
        for sy in range(ny):
            for slot in slots:
                wires.arrived(piece(slot, sy, 1), c_ports[slot, sy], "core")
        gain = jnp.concatenate([gains_out[b, 0:1, : features // nb] for b in range(nb)], axis=1)
        latent_gain = sum(gains_out[b, 2:3, :] for b in range(nb))
        x = tokens[...].astype(wide).reshape(rows, features)
        hidden = norm_rows(x, gain)[0].astype(narrow)
        hidden_out[...] = hidden
        width = small_out.shape[-1]
        latent_all = dot(hidden, small_out[...].reshape(features, width))[:, : KVR + RD]
        latent_all_out[...] = latent_all
        latent = norm_rows(latent_all[:, :KVR], latent_gain)[0]
        rope = rotate(latent_all[:, KVR:], cosine[...], sine[...])
        own_latent[:, :, KVR:] = jnp.zeros((seqs, local_len, NOPE), narrow)
        own_latent[:, :, :KVR] = latent.astype(narrow).reshape(seqs, local_len, KVR)
        own_latent[:, :, KVR : KVR + RD] = rope.astype(narrow).reshape(seqs, local_len, RD)
        z_ports = [wires.port() for _ in range(nz)]
        x_ports = [wires.port() for _ in range(nx)]
        yx_ports = [[wires.port() for _ in range(nx)] for _ in range(ny)]
        cx_ports = [[wires.port() for _ in range(nx)] for _ in range(ny)]
        wires.push(own_latent, latents_out.at[:, 0, 0, 0, 1], z_ports[1], "z")
        own_place = load(own_latent, latents_out.at[:, 0, 0, 0, 0])
        for sz in range(1, nz):
            yield
            here = latents_out.at[:, 0, 0, 0, sz]
            wires.arrived(here, z_ports[sz], "z")
            if sz + 1 < nz:
                wires.push(here, latents_out.at[:, 0, 0, 0, sz + 1], z_ports[sz + 1], "z")
        own_place.wait()
        waited.add(id(own_place))
        for sx in range(nx):
            block = latents_out.at[:, 0, 0, sx]
            if sx:
                yield
                wires.arrived(block, x_ports[sx], "x")
            if sx + 1 < nx:
                wires.push(block, latents_out.at[:, 0, 0, sx + 1], x_ports[sx + 1], "x")
            if ny > 1:
                wires.push(block, latents_out.at[:, 0, 1, sx], yx_ports[1][sx], "y")
            wires.push(block, latents_out.at[:, 1, 0, sx], cx_ports[0][sx], "core")
        for sy in range(1, ny):
            for sx in range(nx):
                yield
                block = latents_out.at[:, 0, sy, sx]
                wires.arrived(block, yx_ports[sy][sx], "y")
                if sy + 1 < ny:
                    wires.push(block, latents_out.at[:, 0, sy + 1, sx], yx_ports[sy + 1][sx], "y")
                wires.push(block, latents_out.at[:, 1, sy, sx], cx_ports[sy][sx], "core")
        for sy in range(ny):
            for sx in range(nx):
                yield
                wires.arrived(latents_out.at[:, 1, sy, sx], cx_ports[sy][sx], "core")

    def group_chain(src, dst):
        gather = GroupGather(wires, src, dst)
        gather.start()
        load(src, dst.at[:, 0, 0])
        yield from gather.chain()

    def array_chain(src, dst, place, x_first):
        gather = BlockGather(wires, src, dst, place, x_first)
        load(src, gather.at(0, 0))
        yield from gather.chain()

    first = main()
    next(first)
    others = [
        array_chain(w_query, query_out, rows_of(w_query.shape[0]), False),
        array_chain(w_expand, expand_out, rows_of(w_expand.shape[0]), True),
        array_chain(w_output, output_out, columns_of(w_output.shape[1]), False),
        line_chain(routes, routes_out),
        group_chain(tokens, tokens_out),
        group_chain(grads, grads_out),
        line_chain(grads, line_out),
    ]
    weave(first, others, 1)
    wires.drain()
    for copy in used:
        if id(copy) not in waited:
            copy.wait()


def start(tokens, grads, cosine, sine, gains, small, routes, weights):
    nz, nx, ny, nc = (lax.axis_size(a) for a in AXES)
    nb, nu = nz * nx, ny * nc
    seqs, local_len, features = tokens.shape
    shape = jax.ShapeDtypeStruct

    def whole(w, dim):
        size = list(w.shape)
        size[dim] *= nb
        return shape(tuple(size), w.dtype)

    grouped = (seqs, ny, nc, local_len, features)
    outs = [
        shape((nb,) + gains.shape, wide),
        shape((nb,) + small.shape, narrow),
        *[whole(w, d) for w, d in zip(weights, (0, 0, 1))],
        shape(grouped, narrow),
        shape(grouped, narrow),
        shape((nz,) + grads.shape, narrow),
        shape((nz,) + routes.shape, routes.dtype),
        shape((seqs, nc, ny, nx, nz, local_len, KVR + NOPE), narrow),
        shape((seqs * local_len, features), narrow),
        shape((seqs * local_len, KVR + RD), wide),
    ]
    return pl.pallas_call(
        start_kernel,
        out_shape=outs,
        in_specs=[VMEM, ANY, VMEM, VMEM, VMEM, VMEM, VMEM] + [ANY] * 3,
        out_specs=[VMEM, VMEM] + [ANY] * 6 + [VMEM] + [ANY] + [VMEM, VMEM],
        scratch_shapes=[
            pltpu.VMEM((seqs, local_len, KVR + NOPE), narrow),
            pltpu.SemaphoreType.DMA((384,)),
            pltpu.SemaphoreType.DMA((384,)),
            pltpu.SemaphoreType.DMA((16,)),
        ],
        compiler_params=pltpu.CompilerParams(
            collective_id=0, has_side_effects=True, vmem_limit_bytes=40 * 1024 * 1024
        ),
        cost_estimate=costs(120),
    )(tokens, grads, cosine, sine, gains, small, routes, *weights)


def scores_of(query, keys, rope, scale):
    return (dot_nt(query[:, :NOPE], keys) + dot_nt(query[:, NOPE:], rope)) * scale


def attend_kernel(
    query, cosine, sine, keys, rope, query_pos, key_pos, query_out, attended, stats, head_lin,
    *, scale, sub,
):
    qk = NOPE + RD
    for head in range(query.shape[1] // qk):

        @pl.when(pl.program_id(1) == head)
        def _(head=head):
            head_lin[:, :qk] = query[:, head * qk : (head + 1) * qk]

    keys_ = keys[:, :NOPE]
    values = keys[:, NOPE:]

    @pl.loop(0, query.shape[0], step=sub)
    def _(first):
        span = pl.ds(pl.multiple_of(first, sub), sub)
        lin = head_lin[span, :]
        turned = rotate(lin[:, NOPE : NOPE + RD], cosine[span, :], sine[span, :])
        query_out[span, :NOPE] = lin[:, :NOPE].astype(narrow)
        query_out[span, NOPE:] = jnp.zeros((sub, NOPE), narrow)
        query_out[span, NOPE : NOPE + RD] = turned.astype(narrow)
        scores = scores_of(query_out[span, :], keys_, rope[0], scale)
        scores = jnp.where(key_pos[...] <= query_pos[span, :], scores, -jnp.inf)
        top = jnp.max(scores, axis=1, keepdims=True)
        raised = jnp.exp(scores - top)
        total = jnp.sum(raised, axis=1, keepdims=True)
        probability = (raised * (1.0 / total)).astype(narrow)
        attended[span, :] = dot(probability, values).astype(narrow)
        stats[0, 0, span, 0:1] = top
        stats[0, 0, span, 1:2] = top + jnp.log(total)


def attend_back_kernel(
    query, cosine, sine, keys, rope, query_pos, key_pos, stats, grads,
    query_grad, expand_grad, rope_grad, key_acc, *, scale, sub,
):
    keys_ = keys[:, :NOPE]
    values = keys[:, NOPE:]
    key_acc[...] = jnp.zeros(key_acc.shape, wide)

    @pl.loop(0, query.shape[0], step=sub)
    def _(first):
        span = pl.ds(pl.multiple_of(first, sub), sub)
        rows = query[span, :]
        scores = scores_of(rows, keys_, rope[0], scale)
        scores = jnp.where(key_pos[...] <= query_pos[span, :], scores, -jnp.inf)
        probability = jnp.exp(scores - stats[0, 0, span, 1:2])
        grad = grads[span, :]
        prob_grad = dot_nt(grad, values)
        weighted = probability * prob_grad
        delta = jnp.sum(weighted, axis=1, keepdims=True)
        score_grad = ((weighted - probability * delta) * scale).astype(narrow)
        back_plain = dot(score_grad, keys_).astype(narrow)
        back_turned = dot(score_grad, rope[0])[:, :RD].astype(narrow).astype(wide)
        turned = unrotate(back_turned, cosine[span, :], sine[span, :]).astype(narrow)
        head_grad = jnp.concatenate([back_plain, turned], axis=1)
        qk = NOPE + RD
        for head in range(query_grad.shape[1] // qk):

            @pl.when(pl.program_id(1) == head)
            def _(head=head):
                query_grad[span, head * qk : (head + 1) * qk] = head_grad

        key_acc[:, : 2 * NOPE] += dot_tn(score_grad, rows)
        key_acc[:, 2 * NOPE :] += dot_tn(probability.astype(narrow), grad)

    expand_grad[:, :NOPE] = key_acc[:, :NOPE].astype(narrow)
    expand_grad[:, NOPE:] = key_acc[:, 2 * NOPE :].astype(narrow)

    @pl.when(pl.program_id(1) == 0)
    def _():
        rope_grad[0] = key_acc[:, NOPE : 2 * NOPE]

    @pl.when(pl.program_id(1) > 0)
    def _():
        rope_grad[0] += key_acc[:, NOPE : 2 * NOPE]


def attention_specs(seqs, heads, reach, length):
    both = NOPE + VH
    return dict(
        query=pl.BlockSpec((reach, both), lambda s, h: (s, h)),
        heads=pl.BlockSpec((reach, heads * (NOPE + RD)), lambda s, h: (s, 0)),
        rope_grad=pl.BlockSpec((1, length, NOPE), lambda s, h: (s, 0, 0)),
        table=pl.BlockSpec((reach, RD // 2), lambda s, h: (0, 0)),
        keys=pl.BlockSpec((length, both), lambda s, h: (s, h)),
        rope=pl.BlockSpec((1, length, NOPE), lambda s, h: (s, 0, KVR // NOPE)),
        query_pos=pl.BlockSpec((reach, 1), lambda s, h: (0, 0)),
        key_pos=pl.BlockSpec((1, length), lambda s, h: (0, 0)),
        head=pl.BlockSpec((reach, VH), lambda s, h: (s, h)),
        stats=pl.BlockSpec((1, 1, reach, 2), lambda s, h: (s, h, 0, 0)),
    )


def attend(query_lin, cosine, sine, keys, rope, query_pos, key_pos, seqs, heads):
    reach, length = query_pos.shape[0], key_pos.shape[1]
    sub = min(reach, max(16, 256 * 2048 // length))
    sp = attention_specs(seqs, heads, reach, length)
    shape = jax.ShapeDtypeStruct
    return pl.pallas_call(
        functools.partial(attend_kernel, scale=(NOPE + RD) ** -0.5, sub=sub),
        grid=(seqs, heads),
        in_specs=[sp[k] for k in ("heads", "table", "table", "keys", "rope", "query_pos", "key_pos")],
        out_specs=[sp["query"], sp["head"], sp["stats"]],
        out_shape=[
            shape((seqs * reach, heads * 2 * NOPE), narrow),
            shape((seqs * reach, heads * VH), narrow),
            shape((seqs, heads, reach, 2), wide),
        ],
        scratch_shapes=[pltpu.VMEM((reach, 2 * NOPE), wide)],
        cost_estimate=costs(16),
        compiler_params=pltpu.CompilerParams(vmem_limit_bytes=61 * 1024 * 1024),
    )(query_lin, cosine, sine, keys, rope, query_pos, key_pos)


def attend_back(query, cosine, sine, keys, rope, query_pos, key_pos, stats, grads, seqs, heads):
    reach, length = query_pos.shape[0], key_pos.shape[1]
    sub = min(reach, max(16, 256 * 2048 // length))
    sp = attention_specs(seqs, heads, reach, length)
    shape = jax.ShapeDtypeStruct
    return pl.pallas_call(
        functools.partial(attend_back_kernel, scale=(NOPE + RD) ** -0.5, sub=sub),
        grid=(seqs, heads),
        in_specs=[
            sp[k]
            for k in (
                "query", "table", "table", "keys", "rope", "query_pos", "key_pos", "stats", "head",
            )
        ],
        out_specs=[sp["heads"], sp["keys"], sp["rope_grad"]],
        cost_estimate=costs(25),
        out_shape=[
            shape((seqs * reach, heads * (NOPE + RD)), narrow),
            shape(keys.shape, narrow),
            shape((seqs, length, NOPE), wide),
        ],
        scratch_shapes=[pltpu.VMEM((length, 2 * NOPE + VH), wide)],
        compiler_params=pltpu.CompilerParams(vmem_limit_bytes=61 * 1024 * 1024),
    )(query, cosine, sine, keys, rope, query_pos, key_pos, stats, grads)


def costs(us):
    return pl.CostEstimate(flops=int(us * 1e9), bytes_accessed=int(us * 1e6), transcendentals=0)


def add_into(target, *terms):
    lead, count = target.shape[:-2], target.shape[-2]
    step = 32 if count % 32 == 0 else 16 if count % 16 == 0 else count
    pieces = count // step
    total = pieces
    for size in lead:
        total *= size

    @pl.loop(0, total)
    def _(i):
        at = []
        rest = i // pieces
        for size in reversed(lead):
            at.insert(0, lax.rem(rest, size))
            rest = rest // size
        span = pl.ds(pl.multiple_of(lax.rem(i, pieces) * step, step), step)
        place = (*at, span, slice(None))
        target[place] = sum(term[place].astype(wide) for term in terms).astype(target.dtype)


class Queue:
    def __init__(self):
        self.items = []

    def add(self, place, thunk):
        self.items.append((place, len(self.items), thunk))
        self.items.sort(key=lambda item: item[:2])

    def go(self, count):
        for _, _, thunk in self.items[:count]:
            thunk()
        del self.items[:count]


class BlockScatter:
    def __init__(self, wires, loads, src, place, axes, acc, first, second, out):
        self.wires, self.loads, self.src, self.place, self.axes = wires, loads, src, place, axes
        self.acc, self.first, self.second, self.out = acc, first, second, out
        self.na, self.nb = (lax.axis_size(a) for a in axes)
        self.ports = {
            (a, b): wires.port() for b in range(self.nb) for a in range(self.na) if a or b
        }
        self.order = [*range(1, self.nb), 0]

    def mine(self, a, b):
        steps = dict(zip(self.axes, (a, b)))
        owner = behind("z", steps["z"]) * lax.axis_size("x") + behind("x", steps["x"])
        return self.place(self.src, owner)

    def slot(self, a, b):
        return self.acc.at[b, max(a - 1, 0)]

    def start(self, queue=None):
        self.loading, self.queue = {}, queue or Queue()
        for place, b in enumerate(self.order):
            self.queue.add(
                place,
                lambda b=b: self.wires.push(
                    self.mine(1, b), self.first.at[b, 0], self.ports[1, b], self.axes[0]
                ),
            )
        if queue is None:
            self.queue.go(self.nb)
        for b in self.order:
            for a in [*range(2, self.na), 0]:
                self.loading[a, b] = self.loads(self.mine(a, b), self.slot(a, b))

    def chain(self):
        wires, (axis_a, axis_b) = self.wires, self.axes
        for b in self.order:
            for a in [*range(2, self.na), 0]:
                came = self.first.at[b, (a or self.na) - 2]
                yield
                wires.arrived(came, self.ports[(a or self.na) - 1, b], axis_a)
                if not a:
                    self.queue.go(1)
                self.loading[a, b].wait()
                add_into(self.slot(a, b), self.slot(a, b), came)
                if a:
                    wires.push(self.slot(a, b), self.first.at[b, a - 1], self.ports[a, b], axis_a)
            if b >= 2:
                yield
                wires.arrived(self.second.at[b - 2], self.ports[0, b - 1], axis_b)
                add_into(self.slot(0, b), self.slot(0, b), self.second.at[b - 2])
            if b >= 1:
                wires.push(self.slot(0, b), self.second.at[b - 1], self.ports[0, b], axis_b)
        yield
        wires.arrived(self.second.at[self.nb - 2], self.ports[0, self.nb - 1], axis_b)
        add_into(self.out, self.slot(0, 0), self.second.at[self.nb - 2])


def scatter_scratch(shard, axes, dtype=narrow):
    na, nb = (lax.axis_size(a) for a in axes)
    return [
        pltpu.VMEM((nb, na - 1) + shard, dtype),
        pltpu.VMEM((nb, na - 1) + shard, dtype),
        pltpu.VMEM((nb - 1,) + shard, dtype),
    ]


class GroupGather:
    def __init__(self, wires, src, dst):
        self.wires, self.src, self.dst = wires, src, dst
        self.ny, self.nc = lax.axis_size("y"), lax.axis_size("core")
        self.ports = [wires.port() for _ in range(self.ny * self.nc)]

    def start(self):
        if self.ny > 1:
            self.wires.push(self.src, self.dst.at[:, 1, 0], self.ports[self.nc], "y")
        self.wires.push(self.src, self.dst.at[:, 0, 1], self.ports[1], "core")

    def chain(self):
        wires, dst, nc = self.wires, self.dst, self.nc
        for sy in range(1, self.ny):
            piece = dst.at[:, sy, 0]
            yield
            wires.arrived(piece, self.ports[sy * nc], "y")
            if sy + 1 < self.ny:
                wires.push(piece, dst.at[:, sy + 1, 0], self.ports[(sy + 1) * nc], "y")
            wires.push(piece, dst.at[:, sy, 1], self.ports[sy * nc + 1], "core")
        for sy in range(self.ny):
            yield
            wires.arrived(dst.at[:, sy, 1], self.ports[sy * nc + 1], "core")


def group_sum_chain(wires, src, own, other, came, load):
    ny = lax.axis_size("y")
    core_ports = [wires.port() for _ in range(ny)]
    y_ports = [wires.port() for _ in range(ny)]
    order = [*range(1, ny), 0]
    for sy in order:
        wires.push(src.at[:, sy, 1], other.at[:, sy], core_ports[sy], "core")
    loading = [load(src.at[:, sy, 0], own.at[:, sy]) for sy in range(ny)]
    for sy in order:
        yield
        wires.arrived(other.at[:, sy], core_ports[sy], "core")
        loading[sy].wait()
        add_into(own.at[:, sy], own.at[:, sy], other.at[:, sy])
        if ny > 1:
            last = (sy or ny) - 1
            if last:
                yield
                wires.arrived(came.at[:, last - 1], y_ports[last], "y")
                add_into(own.at[:, sy], own.at[:, sy], came.at[:, last - 1])
            if sy:
                wires.push(own.at[:, sy], came.at[:, sy - 1], y_ports[sy], "y")


def weave(main, others, share):
    others = list(others)
    running = True
    while running or others:
        if running:
            running = next(main, True) is None
        for _ in range(share if running else max(1, len(others))):
            if others:
                chain = others.pop(0)
                if next(chain, True) is None:
                    others.append(chain)


def finish_kernel(
    hidden_partial, latent_partial, tokens, residual_grad, small, hidden_t, mid_t, logit_grad,
    ffn_gain, gain_attn, gain_latent, latent_all, cosine, sine, residual, shared_sum, routed,
    *rest, modes,
):
    count = len(modes)
    partials, rest = rest[:count], rest[count:]
    tokens_grad, block_out, latent_w_out, gains_out, *rest = rest
    outs, rest = rest[:count], rest[count:]
    (
        hid_own, hid_other, hid_came, lat_own, lat_other, lat_came, lat_x, lat_z,
        own_lag, lag_group, wide_acc, lat_wgrad, gain_terms, routed_own, routed_came, *rest,
    ) = rest
    buffers, rest = rest[: 3 * count], rest[3 * count :]
    lw_buffers, g_buffers = rest[:3], rest[3:6]
    send, recv, local = rest[6:]
    nz, nx, ny, nc = (lax.axis_size(a) for a in AXES)
    nb, nu = nz * nx, ny * nc
    uly = lax.axis_index("y") * nc + lax.axis_index("core")
    seqs, local_len, features = tokens.shape
    rows = seqs * local_len
    greet(AXES)
    wires = Wires(send, recv)
    used = []

    def load(src, dst):
        copy = pltpu.make_async_copy(src, dst, local.at[len(used)])
        used.append(copy)
        copy.start()
        return copy

    def blocks_of(size, dim):
        return rows_of(size) if dim == 0 else columns_of(size)

    scatters = [
        BlockScatter(
            wires, load, partials[i], blocks_of(partials[i].shape[dim] // nb, dim), axes,
            *buffers[3 * i : 3 * i + 3], outs[i],
        )
        for i, (dim, axes) in enumerate(modes)
    ]

    def routed_chain():
        ports = [wires.port() for _ in range(nz)]
        loading = {s: load(routed.at[s], routed_own.at[s]) for s in [*range(1, nz), 0]}
        for s in [*range(1, nz), 0]:
            own = routed_own.at[s]
            last = (s or nz) - 1
            yield
            loading[s].wait()
            if last:
                wires.arrived(routed_came.at[last - 1], ports[last], "z")
                add_into(own, own, routed_came.at[last - 1])
            if s:
                wires.push(own, routed_came.at[s - 1], ports[s], "z")

    def output_chain():
        yield from routed_chain()
        total = residual[...] + shared_sum[...].astype(wide).reshape(rows, features)
        total = total + routed_own[0].astype(wide)
        block_out[...] = total.astype(narrow).reshape(tokens.shape)

    def latent_chain():
        c_ports = [[wires.port() for _ in range(nx)] for _ in range(ny)]
        y_ports = [[wires.port() for _ in range(nx)] for _ in range(ny)]
        x_ports = [wires.port() for _ in range(nx)]
        z_ports = [wires.port() for _ in range(nz)]
        order_y, order_x = [*range(1, ny), 0], [*range(1, nx), 0]
        blocks = [(sy, sx) for sy in order_y for sx in order_x]
        loading = []

        def load_block():
            number = len(loading)
            if number < len(blocks):
                sy, sx = blocks[number]
                loading.append(load(latent_partial.at[:, 0, sy, sx], lat_own.at[number % 2]))

        for sy, sx in blocks:
            wires.push(
                latent_partial.at[:, 1, sy, sx], lat_other.at[:, sy, sx], c_ports[sy][sx], "core"
            )
        load_block()
        load_block()
        yield
        for sy in order_y:
            for sx in order_x:
                own = lat_other.at[:, sy, sx]
                number = blocks.index((sy, sx))
                yield
                wires.arrived(own, c_ports[sy][sx], "core")
                loading[number].wait()
                add_into(own, own, lat_own.at[number % 2])
                load_block()
                last = (sy or ny) - 1
                if last:
                    yield
                    wires.arrived(lat_came.at[:, last - 1, sx], y_ports[last][sx], "y")
                    add_into(own, own, lat_came.at[:, last - 1, sx])
                if sy:
                    wires.push(own, lat_came.at[:, sy - 1, sx], y_ports[sy][sx], "y")
                    continue
                last = (sx or nx) - 1
                if last:
                    yield
                    wires.arrived(lat_x.at[:, last - 1], x_ports[last], "x")
                    add_into(own, own, lat_x.at[:, last - 1])
                if sx:
                    wires.push(own, lat_x.at[:, sx - 1], x_ports[sx], "x")
        for sz in [*range(1, nz), 0]:
            own = lat_other.at[:, 0, 0, sz]
            last = (sz or nz) - 1
            if last:
                yield
                wires.arrived(lat_z.at[:, last - 1], z_ports[last], "z")
                add_into(own, own, lat_z.at[:, last - 1])
            if sz:
                wires.push(own, lat_z.at[:, sz - 1], z_ports[sz], "z")

    def main():
        hidden = group_sum_chain(wires, hidden_partial, hid_own, hid_other, hid_came, load)
        latent = latent_chain()
        next(latent)
        next(hidden)
        for s in scatters:
            s.start(queue)
        queue.go(3)
        yield
        for _ in hidden:
            yield
        for _ in latent:
            yield
        width = KVR + RD
        lat = lat_other[:, 0, 0, 0].astype(wide).reshape(rows, KVR + NOPE)[:, :width]
        latent_grad = lat[:, :KVR]
        _, normed, inverse = norm_rows(latent_all[:, :KVR], gain_latent[...])
        lat_in = norm_input_back(latent_grad, normed, inverse, gain_latent[...])
        turned = unrotate(lat[:, KVR:], cosine[...], sine[...])
        own_lag[:, :, KVR:] = jnp.zeros((seqs, local_len, own_lag.shape[-1] - KVR), narrow)
        own_lag[:, :, :KVR] = lat_in.astype(narrow).reshape(seqs, local_len, KVR)
        own_lag[:, :, KVR:width] = turned.astype(narrow).reshape(seqs, local_len, RD)
        wide_acc[...] = dot_nt(own_lag[...].reshape(rows, own_lag.shape[-1]), small[...])
        own_lag[:, :, width:] = logit_grad[...].reshape(seqs, local_len, EXPERTS)
        lag_gather = GroupGather(wires, own_lag, lag_group)
        lag_gather.start()
        own_copy = load(own_lag, lag_group.at[:, 0, 0])
        x = tokens[...].astype(wide).reshape(rows, features)
        _, normed_in, inverse_in = norm_rows(x, gain_attn[...])
        hidden_grad = wide_acc[...] + hid_own[:, 0].astype(wide).reshape(rows, features)
        wide_acc[...] = residual_grad[...] + norm_input_back(
            hidden_grad, normed_in, inverse_in, gain_attn[...]
        )
        attn_gain = jnp.sum(hidden_grad * normed_in, axis=0, keepdims=True)
        latent_gain = jnp.sum(latent_grad * normed, axis=0, keepdims=True)
        tokens_grad[...] = wide_acc[...].astype(narrow).reshape(tokens.shape)
        shard = features // nb
        gain_terms[...] = jnp.zeros(gain_terms.shape, wide)
        for b in range(nb):
            gain_terms[b, 0:1, :shard] = attn_gain[:, b * shard : (b + 1) * shard]
            gain_terms[b, 0:1, shard:] = latent_gain
            gain_terms[b, 1:2, :shard] = ffn_gain[:, b * shard : (b + 1) * shard]
        gain_sum = BlockScatter(
            wires, load, gain_terms, lambda ref, owner: ref.at[owner], ("x", "z"), *g_buffers,
            gains_out.at[uly],
        )
        gain_sum.start()
        for _ in lag_gather.chain():
            yield
        own_copy.wait()
        lags = lag_group[...].reshape(nu * rows, own_lag.shape[-1])
        terms = dot(hidden_t[...], lags).astype(narrow)
        lat_wgrad[...] = terms.reshape(lat_wgrad.shape)
        terms = dot(mid_t[...], lags)[:, width:].astype(narrow)
        lat_wgrad[:, :, width:] = terms.reshape(lat_wgrad.shape[:2] + (EXPERTS,))
        w_sum = BlockScatter(
            wires, load, lat_wgrad, lambda ref, owner: ref.at[owner], ("x", "z"), *lw_buffers,
            latent_w_out.at[uly],
        )
        w_sum.start()
        chains = [gain_sum.chain(), w_sum.chain()]
        while chains:
            chain = chains.pop(0)
            if next(chain, True) is None:
                chains.append(chain)
                yield
        outs_ = (latent_w_out, gains_out)
        y_ports = [[wires.port() for _ in range(ny)] for _ in outs_]
        c_ports = [[wires.port() for _ in range(ny)] for _ in outs_]
        member = lambda sy, sc: behind("y", sy) * nc + behind("core", sc)
        for ref, yp, cp in zip(outs_, y_ports, c_ports):
            here = ref.at[uly]
            if ny > 1:
                wires.push(here, here, yp[1], "y")
            wires.push(here, here, cp[0], "core")
        for sy in range(1, ny):
            for ref, yp, cp in zip(outs_, y_ports, c_ports):
                piece = ref.at[member(sy, 0)]
                yield
                wires.arrived(piece, yp[sy], "y")
                if sy + 1 < ny:
                    wires.push(piece, piece, yp[sy + 1], "y")
                wires.push(piece, piece, cp[sy], "core")
        for sy in range(ny):
            for ref, cp in zip(outs_, c_ports):
                yield
                wires.arrived(ref.at[member(sy, 1)], cp[sy], "core")

    queue = Queue()
    weave(main(), [s.chain() for s in scatters] + [output_chain()], 1)
    wires.drain()


def finish(
    hidden_partial, latent_partial, tokens, residual_grad, small, hidden_t, mid_t, logit_grad,
    ffn_gain, gain_attn, gain_latent, latent_all, cosine, sine, residual, shared_sum, routed,
    partials, modes,
):
    nz, nx, ny, nc = (lax.axis_size(a) for a in AXES)
    nb, nu = nz * nx, ny * nc
    seqs, local_len, features = tokens.shape
    rows = seqs * local_len
    shape = jax.ShapeDtypeStruct
    shards = []
    for p, (dim, _) in zip(partials, modes):
        size = list(p.shape)
        size[dim] //= nb
        shards.append(tuple(size))
    width, shard = KVR + RD, features // nb
    padded = small.shape[-1]
    latents = (seqs, ny, nx, nz, local_len, KVR + NOPE)
    few = lambda n: max(n - 1, 1)
    scratch = [
        pltpu.VMEM((seqs, ny, local_len, features), narrow),
        pltpu.VMEM((seqs, ny, local_len, features), narrow),
        pltpu.VMEM((seqs, few(ny), local_len, features), narrow),
        pltpu.VMEM((2, seqs, nz, local_len, KVR + NOPE), narrow),
        pltpu.VMEM(latents, narrow),
        pltpu.VMEM((seqs, few(ny), nx, nz, local_len, KVR + NOPE), narrow),
        pltpu.VMEM((seqs, few(nx), nz, local_len, KVR + NOPE), narrow),
        pltpu.VMEM((seqs, few(nz), local_len, KVR + NOPE), narrow),
        pltpu.VMEM((seqs, local_len, padded), narrow),
        pltpu.VMEM((seqs, ny, nc, local_len, padded), narrow),
        pltpu.VMEM((rows, features), wide),
        pltpu.VMEM((nb, shard // nu, padded), narrow),
        pltpu.VMEM((nb, 8, shard + KVR), wide),
        pltpu.VMEM((nz, rows, features), narrow),
        pltpu.VMEM((few(nz), rows, features), narrow),
    ]
    for size, (_, axes) in zip(shards, modes):
        scratch += scatter_scratch(size, axes)
    scratch += scatter_scratch((shard // nu, padded), ("x", "z"))
    scratch += scatter_scratch((8, shard + KVR), ("x", "z"), wide)
    scratch += [
        pltpu.SemaphoreType.DMA((256,)),
        pltpu.SemaphoreType.DMA((256,)),
        pltpu.SemaphoreType.DMA((256,)),
    ]
    return pl.pallas_call(
        functools.partial(finish_kernel, modes=modes),
        out_shape=[
            shape(tokens.shape, narrow),
            shape(tokens.shape, narrow),
            shape((nu, shard // nu, padded), wide),
            shape((nu, 8, shard + KVR), wide),
            *[shape(size, wide) for size in shards],
        ],
        in_specs=[ANY, ANY] + [VMEM] * 14 + [ANY] * (1 + len(partials)),
        out_specs=[VMEM] * (4 + len(partials)),
        scratch_shapes=scratch,
        compiler_params=pltpu.CompilerParams(
            collective_id=1, has_side_effects=True, vmem_limit_bytes=62 * 1024 * 1024
        ),
        cost_estimate=costs(190),
    )(
        hidden_partial, latent_partial, tokens, residual_grad, small, hidden_t, mid_t, logit_grad,
        ffn_gain, gain_attn, gain_latent, latent_all, cosine, sine, residual, shared_sum, routed,
        *partials,
    )


class Layer:
    def __init__(self):
        self.sizes = [lax.axis_size(a) for a in AXES[1:]]
        self.count = self.sizes[0] * self.sizes[1] * self.sizes[2]

    def offsets(self, k):
        _, ny, nc = self.sizes
        return k // (ny * nc), k // nc % ny, k % nc

    def device(self, k, sign=1):
        return {
            axis: lax.rem(lax.axis_index(axis) + (sign * d) % n, n)
            for axis, d, n in zip(AXES[1:], self.offsets(k), self.sizes)
        }

    def number(self, k, sign=1):
        where = self.device(k, sign)
        return (where["x"] * self.sizes[1] + where["y"]) * self.sizes[2] + where["core"]

    def greet(self):
        barrier = pltpu.get_barrier_semaphore()
        for k in range(1, self.count):
            pl.semaphore_signal(barrier, inc=1, device_id=self.device(k), device_id_type=MESH)
        pl.semaphore_signal(
            barrier, inc=1, device_id={"z": behind("z", 1)}, device_id_type=MESH
        )
        pl.semaphore_wait(barrier, self.count)

    def push(self, wires, src, dst, port, k):
        copy = pltpu.make_async_remote_copy(
            src_ref=src,
            dst_ref=dst,
            send_sem=wires.send.at[port],
            recv_sem=wires.recv.at[port],
            device_id=self.device(k),
            device_id_type=MESH,
        )
        copy.start()
        wires.sent.append(copy)


def dispatch_kernel(
    partial, tokens, gain, router, member, picks, top, *rest, plan,
):
    count = len(plan)
    shards, rest = rest[:count], rest[count:]
    residual_out, gates_out, hidden_out, group_out, rows_out, tops_out, *rest = rest
    wholes, rest = rest[:count], rest[count:]
    own, other, came, hidden, line, outgoing, send, recv, local = rest
    nz, nx = lax.axis_size("z"), lax.axis_size("x")
    seqs, local_len, features = tokens.shape
    rows = seqs * local_len
    layer = Layer()
    layer.greet()
    wires = Wires(send, recv)
    used, waited = [], set()

    def load(src, dst):
        copy = pltpu.make_async_copy(src, dst, local.at[len(used)])
        used.append(copy)
        copy.start()
        return copy

    def main():
        for _ in group_sum_chain(wires, partial, own, other, came, load):
            yield
        waited.update(id(copy) for copy in used[: own.shape[1]])
        residual = tokens[...].astype(wide).reshape(rows, features)
        residual = residual + own[:, 0].astype(wide).reshape(rows, features)
        residual_out[...] = residual
        normed = norm_rows(residual, gain[...])[0].astype(narrow)
        hidden_out[...] = normed
        hidden[...] = normed.reshape(tokens.shape)
        line[0, :, :features] = normed
        logits = jnp.where(member[...] > 0, dot(normed, router[...]), -jnp.inf)
        raised = jnp.exp(logits - jnp.max(logits, axis=1, keepdims=True))
        gates = raised / jnp.sum(raised, axis=1, keepdims=True)
        gates_out[...] = gates
        high = gates.astype(narrow).astype(wide)
        line[0, :, features:] = jnp.concatenate([high, gates - high], axis=1).astype(narrow)
        z_ports = [wires.port() for _ in range(nz)]
        wires.push(line.at[0], line.at[1], z_ports[1], "z")
        gather = GroupGather(wires, hidden, group_out)
        gather.start()
        load(hidden, group_out.at[:, 0, 0])
        ports = [[wires.port() for _ in range(layer.count)] for _ in range(nz)]
        me = layer.number(0)
        chain = gather.chain()
        for s in range(nz):
            if s:
                yield
                wires.arrived(line.at[s], z_ports[s], "z")
                if s + 1 < nz:
                    wires.push(line.at[s], line.at[s + 1], z_ports[s + 1], "z")
            outgoing[s] = dot_tn(picks[s], line[s]).astype(narrow).reshape(outgoing.shape[1:])
            for k in range(1, layer.count):
                target = layer.number(k)
                layer.push(wires, outgoing.at[s, target], rows_out.at[s, me], ports[s][k], k)
            load(outgoing.at[s, me], rows_out.at[s, me])
            next(chain, None)
        for _ in chain:
            pass
        for s in range(nz):
            yield
            for k in range(1, layer.count):
                wires.arrived(rows_out.at[s, layer.number(k, -1)], ports[s][k], "z")

    def tops():
        z_ports = [wires.port() for _ in range(nz)]
        x_ports = [wires.port() for _ in range(nx)]
        mine = load(top, tops_out.at[0, 0])
        waited.add(id(mine))
        wires.push(top, tops_out.at[0, 1], z_ports[1], "z")
        for s in range(1, nz):
            yield
            wires.arrived(tops_out.at[0, s], z_ports[s], "z")
            if s + 1 < nz:
                wires.push(tops_out.at[0, s], tops_out.at[0, s + 1], z_ports[s + 1], "z")
        mine.wait()
        wires.push(tops_out.at[0], tops_out.at[1], x_ports[1], "x")
        for s in range(1, nx):
            yield
            wires.arrived(tops_out.at[s], x_ports[s], "x")
            if s + 1 < nx:
                wires.push(tops_out.at[s], tops_out.at[s + 1], x_ports[s + 1], "x")

    def array_chain(src, dst, dim, x_first):
        place = (rows_of if dim == 0 else columns_of)(src.shape[dim])
        gather = BlockGather(wires, src, dst, place, x_first)
        load(src, gather.at(0, 0))
        yield from gather.chain()

    first = main()
    next(first)
    others = [array_chain(a, b, *mode) for a, b, mode in zip(shards, wholes, plan)]
    weave(first, others + [tops()], 1)
    for copy in used:
        if id(copy) not in waited:
            copy.wait()
    wires.drain()


def whole_array(w, dim):
    size = list(w.shape)
    size[dim] *= lax.axis_size("z") * lax.axis_size("x")
    return jax.ShapeDtypeStruct(tuple(size), w.dtype)


def dispatch(partial, tokens, gain, router, member, picks, top, units, shards, plan):
    nz, nx, ny, nc = (lax.axis_size(a) for a in AXES)
    seqs, local_len, features = tokens.shape
    rows = seqs * local_len
    layer = nx * ny * nc
    shape = jax.ShapeDtypeStruct
    extended = features + 2 * EXPERTS
    part = pltpu.VMEM((seqs, ny, local_len, features), narrow)
    return pl.pallas_call(
        functools.partial(dispatch_kernel, plan=plan),
        out_shape=[
            shape((rows, features), wide),
            shape((rows, EXPERTS), wide),
            shape((rows, features), narrow),
            shape((seqs, ny, nc, local_len, features), narrow),
            shape((nz, layer, units, SLOTS, extended), narrow),
            shape((nx, nz) + top.shape, wide),
            *[whole_array(w, dim) for w, (dim, _) in zip(shards, plan)],
        ],
        in_specs=[ANY] + [VMEM] * 6 + [ANY] * len(shards),
        out_specs=[VMEM, VMEM, VMEM, ANY, ANY, VMEM] + [ANY] * len(shards),
        scratch_shapes=[
            part, part, part,
            pltpu.VMEM((seqs, local_len, features), narrow),
            pltpu.VMEM((nz, rows, extended), narrow),
            pltpu.VMEM((nz, layer, units, SLOTS, extended), narrow),
            pltpu.SemaphoreType.DMA((256,)),
            pltpu.SemaphoreType.DMA((256,)),
            pltpu.SemaphoreType.DMA((32,)),
        ],
        compiler_params=pltpu.CompilerParams(
            collective_id=2, has_side_effects=True, vmem_limit_bytes=48 * 1024 * 1024
        ),
        cost_estimate=costs(80),
    )(partial, tokens, gain, router, member, picks, top, *shards)


def return_kernel(
    returned, partial, shared_partial, residual, gates, router, gain, grads, picks, *rest, modes,
):
    count = len(modes)
    partials, rest = rest[:count], rest[count:]
    residual_grad_out, group_out, logit_out, gain_out, shared_out, *rest = rest
    outs, rest = rest[:count], rest[count:]
    own, other, came, sh_own, sh_other, sh_came, back, line, own_grad, *rest = rest
    buffers, rest = rest[: 3 * count], rest[3 * count :]
    send, recv, local = rest
    nz, nx = lax.axis_size("z"), lax.axis_size("x")
    seqs, local_len, features = grads.shape
    rows = seqs * local_len
    layer = Layer()
    layer.greet()
    wires = Wires(send, recv)
    used = []

    def load(src, dst):
        copy = pltpu.make_async_copy(src, dst, local.at[len(used)])
        used.append(copy)
        copy.start()
        return copy

    queue = Queue()
    scatters = [
        BlockScatter(
            wires, load, partials[i],
            (rows_of if dim == 0 else columns_of)(partials[i].shape[dim] // (nz * nx)), axes,
            *buffers[3 * i : 3 * i + 3], outs[i],
        )
        for i, (dim, axes) in enumerate(modes)
    ]

    def main():
        me = layer.number(0)
        ports = [[wires.port() for _ in range(layer.count)] for _ in range(nz)]
        z_ports = [wires.port() for _ in range(nz)]
        order = [*range(1, nz), 0]
        own_copies = {}
        for s in order:
            for k in range(1, layer.count):
                layer.push(
                    wires, returned.at[s, layer.number(k)], back.at[s, me], ports[s][k], k
                )
            own_copies[s] = load(returned.at[s, me], back.at[s, me])
        shared = group_sum_chain(wires, partial, own, other, came, load)
        next(shared)
        yield
        extended = back.shape[-1]
        total = None
        for s in order:
            for k in range(1, layer.count):
                wires.arrived(back.at[s, layer.number(k, -1)], ports[s][k], "z")
            own_copies[s].wait()
            term = dot(picks[s], back[s].reshape(picks.shape[2], extended))
            if s != 1:
                last = (s or nz) - 1
                yield
                wires.arrived(line.at[1, last - 1], z_ports[last], "z")
                term = term + line[1, last - 1].astype(wide)
            if s:
                line[0, s - 1] = term.astype(narrow)
                wires.push(line.at[0, s - 1], line.at[1, s - 1], z_ports[s], "z")
            else:
                total = term
            next(shared, None)
        for _ in shared:
            pass
        lanes = total[:, features:]
        gate_grad = lanes[:, :EXPERTS] + lanes[:, EXPERTS:]
        weight = gates[...]
        logit_grad = (
            weight * (gate_grad - jnp.sum(weight * gate_grad, axis=1, keepdims=True))
        ).astype(narrow)
        logit_out[...] = logit_grad
        mid = total[:, :features] + own[:, 0].astype(wide).reshape(rows, features)
        mid = mid + dot_nt(logit_grad, router[...])
        _, normed, inverse = norm_rows(residual[...], gain[...])
        grad = grads[...].astype(wide).reshape(rows, features)
        grad = grad + norm_input_back(mid, normed, inverse, gain[...])
        residual_grad_out[...] = grad
        own_grad[...] = grad.astype(narrow).reshape(grads.shape)
        gather = GroupGather(wires, own_grad, group_out)
        gather.start()
        mine = load(own_grad, group_out.at[:, 0, 0])
        gain_out[...] = jnp.sum(mid * normed, axis=0, keepdims=True)
        yield from gather.chain()
        mine.wait()

    def shared_sum():
        yield from group_sum_chain(wires, shared_partial, sh_own, sh_other, sh_came, load)
        shared_out[...] = sh_own[:, 0]

    first = main()
    next(first)
    for s in scatters:
        s.start(queue)
    queue.go(2)
    weave(first, [s.chain() for s in scatters] + [shared_sum()], 1)
    wires.drain()


def come_back(
    returned, partial, shared_partial, residual, gates, router, gain, grads, picks, partials, modes
):
    nz, nx, ny, nc = (lax.axis_size(a) for a in AXES)
    seqs, local_len, features = grads.shape
    rows = seqs * local_len
    shape = jax.ShapeDtypeStruct
    extended = returned.shape[-1]
    part = pltpu.VMEM((seqs, ny, local_len, features), narrow)
    shards = []
    for p, (dim, _) in zip(partials, modes):
        size = list(p.shape)
        size[dim] //= nz * nx
        shards.append(tuple(size))
    scratch = [
        part, part, part, part, part, part,
        pltpu.VMEM(returned.shape, narrow),
        pltpu.VMEM((2, nz - 1, rows, extended), narrow),
        pltpu.VMEM((seqs, local_len, features), narrow),
    ]
    for size, (_, axes) in zip(shards, modes):
        scratch += scatter_scratch(size, axes)
    scratch += [
        pltpu.SemaphoreType.DMA((256,)),
        pltpu.SemaphoreType.DMA((256,)),
        pltpu.SemaphoreType.DMA((96,)),
    ]
    return pl.pallas_call(
        functools.partial(return_kernel, modes=modes),
        out_shape=[
            shape((rows, features), wide),
            shape((seqs, ny, nc, local_len, features), narrow),
            shape((rows, EXPERTS), narrow),
            shape((1, features), wide),
            shape(grads.shape, narrow),
            *[shape(size, wide) for size in shards],
        ],
        in_specs=[ANY, ANY, ANY] + [VMEM] * 6 + [ANY] * len(partials),
        out_specs=[VMEM, ANY, VMEM, VMEM, VMEM] + [VMEM] * len(partials),
        scratch_shapes=scratch,
        compiler_params=pltpu.CompilerParams(
            collective_id=3, has_side_effects=True, vmem_limit_bytes=56 * 1024 * 1024
        ),
        cost_estimate=costs(100),
    )(returned, partial, shared_partial, residual, gates, router, gain, grads, picks, *partials)


def expert_kernel(
    rows_in, grads_in, wg, wu, wd, *rest, split, plan,
):
    count = len(plan)
    shards, rest = rest[:count], rest[count:]
    returned, outputs, gated, lin_gate, lin_up, *rest = rest
    wholes, rest = rest[:count], rest[count:]
    (
        rows, grads, bg, bu, bd, act, gated_buf, gate_buf, up_buf, dots,
        back_stage, out_stage, send, recv, local, turn,
    ) = rest
    nz, nx, ny, nc = (lax.axis_size(a) for a in AXES)
    nb = nz * nx
    layer = nx * ny * nc
    units, features, hidden = wg.shape
    first_unit = (
        (lax.axis_index("z") * nx + lax.axis_index("x")) * ny + lax.axis_index("y")
    ) * nc + lax.axis_index("core")
    first_unit = first_unit * units
    per = min(nz, max(1, 512 // (layer * SLOTS)))
    block = per * layer * SLOTS
    blocks = nz // per
    wires = Wires(send, recv)
    greet(("z", "x"))
    used = []

    def load(src, dst):
        copy = pltpu.make_async_copy(src, dst, local.at[len(used)])
        used.append(copy)
        copy.start()
        return copy

    gathers = [
        BlockGather(
            wires, src, dst, (rows_of if dim == 0 else columns_of)(src.shape[dim]), x_first
        )
        for src, dst, (dim, x_first) in zip(shards, wholes, plan)
    ]

    def transfers():
        for g in gathers:
            g.forward(0, 0)
        yield
        plans = [g.rounds() for g in gathers]
        for step in range(max(len(p) for p in plans)):
            for g, p in zip(gathers, plans):
                for slot in p[step] if step < len(p) else []:
                    g.take(*slot)
                    yield

    moving = transfers()
    next(moving, None)

    def tick():
        next(moving, None)

    def fetch(a):
        slot = a % rows.shape[0]
        return [
            load(rows_in.at[:, :, a], rows.at[slot]),
            load(wg.at[a], bg),
            load(wu.at[a], bu),
            load(grads_in.at[:, :, a], grads.at[slot]),
            load(wd.at[a], bd),
        ]

    fetched = fetch(0)
    kept = [load(g.src, g.at(0, 0)) for g in gathers]

    def pump(low, high, body, copies):
        @pl.loop(low, high)
        def _(i):
            slot = lax.rem(i, 2)

            @pl.when(i >= 2)
            def _():
                for copy in copies(i - 2, slot):
                    copy.wait()

            body(i, slot)
            for copy in copies(i, slot):
                copy.start()

    def settle(total, copies):
        for i in range(max(0, total - 2), total):
            for copy in copies(i, i % 2):
                copy.wait()

    saved, extra_copy = [], None
    for a in range(units):
        slot_a = a % rows.shape[0]
        expert = (first_unit + a) // split
        for copy in fetched[:3]:
            copy.wait()
        waiting = fetched[3:]

        def weights_of(b):
            extra = rows[slot_a, pl.ds(b * per, per), :, :, features:].astype(wide)
            extra = extra.reshape(block, 2 * EXPERTS)
            lane = lax.broadcasted_iota(jnp.int32, extra.shape, 1)
            mine = (lane == expert) | (lane == expert + EXPERTS)
            return jnp.sum(jnp.where(mine, extra, 0.0), axis=1, keepdims=True)

        def row_block(ref, b, columns):
            return ref[slot_a, pl.ds(b * per, per), :, :, columns].reshape(block, -1)

        for copy in waiting:
            copy.wait()

        def forward(b, cols):
            span = pl.ds(pl.multiple_of(b * block, block), block)
            picked = row_block(rows, b, slice(0, features))
            lin = dot(picked, bg[:, cols])
            up = dot(picked, bu[:, cols])
            grad = dot_nt(row_block(grads, b, slice(None)), bd[cols, :]) * weights_of(b)
            s = jax.nn.sigmoid(lin)
            silu = lin * s
            value = (silu * up).astype(narrow)
            act[span, cols] = value
            gated_buf[span, cols] = (value.astype(wide) * weights_of(b)).astype(narrow)
            gate_buf[span, cols] = (grad * up * (s * (1.0 + lin * (1.0 - s)))).astype(narrow)
            up_buf[span, cols] = (grad * silu).astype(narrow)

        full = hidden // 256
        for copy in saved:
            copy.wait()

        @pl.loop(0, blocks)
        def _(b):
            @pl.loop(0, full)
            def _(i):
                forward(b, pl.ds(pl.multiple_of(i * 256, 256), 256))

            if hidden % 256:
                forward(b, pl.ds(full * 256, hidden % 256))

        saved = [
            load(src, dst.at[a])
            for src, dst in ((gated_buf, gated), (gate_buf, lin_gate), (up_buf, lin_up))
        ]
        tick()
        tick()
        dots[...] = jnp.zeros(dots.shape, wide)

        def spread(i):
            return pl.ds(pl.multiple_of(i * 256, 256), 256)

        def back_copies(i, slot):
            return [
                pltpu.make_async_copy(
                    back_stage.at[slot], returned.at[:, :, a, :, spread(i)], turn.at[0, slot]
                ),
                pltpu.make_async_copy(
                    out_stage.at[slot], outputs.at[:, :, a, :, spread(i)], turn.at[1, slot]
                ),
            ]

        def backward(i, slot):
            @pl.loop(0, blocks)
            def _(b):
                span = pl.ds(pl.multiple_of(b * block, block), block)
                cols = spread(i)
                out = dot(act[span, :], bd[:, cols])
                dots[span, :] += jnp.sum(
                    out * row_block(grads, b, cols).astype(wide), axis=1, keepdims=True
                )
                shaped = (per, layer, SLOTS, 256)
                out_stage[slot, pl.ds(b * per, per)] = (
                    (out * weights_of(b)).astype(narrow).reshape(shaped)
                )
                inward = dot_nt(gate_buf[span, :], bg[cols, :]) + dot_nt(
                    up_buf[span, :], bu[cols, :]
                )
                back_stage[slot, pl.ds(b * per, per)] = inward.astype(narrow).reshape(shaped)

        chunks = features // 256
        for part in range(4):
            pump(part * chunks // 4, (part + 1) * chunks // 4, backward, back_copies)
            tick()
        settle(chunks, back_copies)

        @pl.loop(0, blocks)
        def _(b):
            span = pl.ds(pl.multiple_of(b * block, block), block)
            lane = lax.broadcasted_iota(jnp.int32, (block, 2 * EXPERTS), 1)
            value = dots[span, :]
            high = value.astype(narrow).astype(wide)
            lanes = jnp.where(lane == expert, high, 0.0)
            lanes = jnp.where(lane == expert + EXPERTS, value - high, lanes)
            rest_ = lanes.astype(narrow).reshape(per, layer, SLOTS, 2 * EXPERTS)
            back_stage[0, pl.ds(b * per, per), :, :, : 2 * EXPERTS] = rest_

        extra_copy = load(
            back_stage.at[0, :, :, :, : 2 * EXPERTS], returned.at[:, :, a, :, features:]
        )
        if a + 1 < units:
            fetched = fetch(a + 1)

        extra_copy.wait()
    for copy in saved:
        copy.wait()
    for _ in moving:
        pass
    for copy in kept:
        copy.wait()
    wires.drain()


def run_experts(rows_in, grads_in, wg, wu, wd, shards, plan, split):
    nz, nx, ny, nc = (lax.axis_size(a) for a in AXES)
    nb = nz * nx
    units, features, hidden = wg.shape
    layer = nx * ny * nc
    total = nz * layer * SLOTS
    shape = jax.ShapeDtypeStruct
    extended = rows_in.shape[-1]

    slots = min(units, 2)
    lines = (nz, layer, SLOTS)
    return pl.pallas_call(
        functools.partial(expert_kernel, split=split, plan=plan),
        out_shape=[
            shape(rows_in.shape, narrow),
            shape(grads_in.shape, narrow),
            *[shape((units, total, hidden), narrow)] * 3,
            *[whole_array(w, dim) for w, (dim, _) in zip(shards, plan)],
        ],
        in_specs=[ANY] * (5 + len(shards)),
        out_specs=[ANY] * (5 + len(shards)),
        scratch_shapes=[
            pltpu.VMEM((slots,) + lines + (extended,), narrow),
            pltpu.VMEM((slots,) + lines + (features,), narrow),
            pltpu.VMEM((features, hidden), narrow),
            pltpu.VMEM((features, hidden), narrow),
            pltpu.VMEM((hidden, features), narrow),
            pltpu.VMEM((total, hidden), narrow),
            pltpu.VMEM((total, hidden), narrow),
            pltpu.VMEM((total, hidden), narrow),
            pltpu.VMEM((total, hidden), narrow),
            pltpu.VMEM((total, 1), wide),
            pltpu.VMEM((2,) + lines + (256,), narrow),
            pltpu.VMEM((2,) + lines + (256,), narrow),
            pltpu.SemaphoreType.DMA((64,)),
            pltpu.SemaphoreType.DMA((64,)),
            pltpu.SemaphoreType.DMA((32,)),
            pltpu.SemaphoreType.DMA((4, 2)),
        ],
        compiler_params=pltpu.CompilerParams(
            collective_id=4, has_side_effects=True, vmem_limit_bytes=60 * 1024 * 1024
        ),
        cost_estimate=costs(80),
    )(rows_in, grads_in, wg, wu, wd, *shards)


def unit_grads_kernel(rows, grads, gated, lin_gate, lin_up, gate_out, up_out, down_out):
    picked = rows[...].reshape(gated.shape[1], rows.shape[-1])
    gate_out[0] = dot_tn(picked, lin_gate[0])
    up_out[0] = dot_tn(picked, lin_up[0])
    down_out[0] = dot_tn(gated[0], grads[...].reshape(gated.shape[1], grads.shape[-1]))


def unit_grads(rows, grads, gated, lin_gate, lin_up):
    nz, layer, units, _, features = grads.shape
    _, total, hidden = gated.shape
    step = 512 if total <= 512 else 128
    lines = (nz, layer, 1, SLOTS, step)
    shape = jax.ShapeDtypeStruct
    line_spec = pl.BlockSpec(lines, lambda a, i: (0, 0, a, 0, i))
    unit_spec = pl.BlockSpec((1, total, hidden), lambda a, i: (a, 0, 0))
    wide_spec = pl.BlockSpec((1, step, hidden), lambda a, i: (a, i, 0))
    return pl.pallas_call(
        unit_grads_kernel,
        grid=(units, features // step),
        in_specs=[line_spec, line_spec, unit_spec, unit_spec, unit_spec],
        out_specs=[wide_spec, wide_spec, pl.BlockSpec((1, hidden, step), lambda a, i: (a, 0, i))],
        out_shape=[
            shape((units, features, hidden), wide),
            shape((units, features, hidden), wide),
            shape((units, hidden, features), wide),
        ],
        cost_estimate=costs(35),
        compiler_params=pltpu.CompilerParams(vmem_limit_bytes=61 * 1024 * 1024),
    )(rows, grads, gated, lin_gate, lin_up)


def per_device(
    tokens, attn_gain, w_query, w_latent, latent_gain, w_expand, w_output, ffn_gain, w_router,
    w_shared_gate, w_shared_up, w_shared_down, w_gate, w_up, w_down, routes, clip_limit, out_grad,
):
    seqs, local_len, features = tokens.shape
    rows = seqs * local_len
    qk = NOPE + RD
    nz, nx, ny, nc = (lax.axis_size(a) for a in ("z", "x", "y", "core"))
    zi, xi, yi, ci = (lax.axis_index(a) for a in ("z", "x", "y", "core"))
    nb, nu = nz * nx, ny * nc
    layer = nx * nu
    heads = H // nu
    group = nu * rows
    all_rows = nb * group
    upd = w_gate.shape[0]
    split = upd * nz * layer // EXPERTS
    scale = qk ** (-0.5)
    GROUP = ("y", "core")
    ALL = ("z", "x", "y", "core")
    LAYER = ("x", "y", "core")

    def scatter_blk(whole, dim):
        size = whole.shape[dim] // nb
        blocks = []
        for sz in range(nz):
            for sx in range(nx):
                owner = ((zi + nz - sz) % nz) * nx + (xi + nx - sx) % nx
                blocks.append(lax.dynamic_slice_in_dim(whole, owner * size, size, dim))
        return tree_sum(blocks, ("z", "x"))

    def group_gather(value):
        return jnp.concatenate(
            [p.reshape(seqs, local_len, -1) for p in flat_ring(value, GROUP)], axis=1
        ).reshape(group, -1)

    def group_scatter(value):
        blocks = value.reshape(seqs, nu, local_len, -1)
        return tree_sum([blocks[:, i].reshape(rows, -1) for i in range(nu)], GROUP)

    def group_sum(value):
        for axis in GROUP:
            items = ring(value, axis)
            value = sum(item.astype(wide) for item in items)
        return value

    def device_positions(blk, u):
        return (blk * nu + u) * local_len + jnp.arange(local_len, dtype=jnp.int32)

    local_pos = device_positions(zi * nx + xi, yi * nc + ci)
    group_pos = jnp.concatenate(
        [
            device_positions(zi * nx + xi, (yi + ny - sy) % ny * nc + (ci + nc - sc) % nc)
            for sy in range(ny)
            for sc in range(nc)
        ]
    )
    key_pos = jnp.concatenate(
        [
            device_positions(
                (zi + nz - sz) % nz * nx + (xi + nx - sx) % nx,
                (yi + ny - sy) % ny * nc + (ci + nc - sc) % nc,
            )
            for sc in range(nc)
            for sy in range(ny)
            for sx in range(nx)
            for sz in range(nz)
        ]
    )

    shard = attn_gain.shape[0]
    lat_len = latent_gain.shape[0]
    gains = jnp.concatenate(
        [
            jnp.pad(jnp.stack([attn_gain, ffn_gain]).astype(wide), ((0, 0), (0, KVR - shard))),
            lax.dynamic_update_slice(
                jnp.zeros((1, KVR), wide),
                latent_gain.astype(wide)[None],
                (0, (zi * nx + xi) * lat_len),
            ),
            jnp.zeros((5, KVR), wide),
        ],
        axis=0,
    )
    small = jnp.concatenate([w_latent, w_router], axis=1).reshape(nu, shard // nu, -1)
    route_rows = jnp.swapaxes(routes, 0, 1).reshape(rows, TOP)
    cos_local, sin_local = rotary_tables(jnp.tile(local_pos, seqs))
    (
        gains_all, small_all, query_w, expand_w, output_w,
        tokens_group, grad_group, grad_line, route_line, latents, hidden_local, latent_all,
    ) = start(
        tokens, out_grad, cos_local, sin_local, gains, small,
        jnp.pad(route_rows, ((0, 0), (0, 128 - TOP))),
        (w_query, w_expand, w_output),
    )
    tokens_local = tokens.reshape(rows, features)
    grad_narrow = out_grad.reshape(rows, features)
    small_whole = small_all.reshape(features, -1)
    latent_w = small_whole[:, : KVR + RD]
    router_w = small_whole[:, KVR + RD :]
    gain_attn = gains_all[:, 0, :shard].reshape(-1)
    gain_ffn = gains_all[:, 1, :shard].reshape(-1)
    gain_latent = jnp.sum(gains_all[:, 2], axis=0)
    inputs = tokens_local.astype(wide)
    _, normed_in, inverse_in = norm_rows(inputs, gain_attn)
    _, normed_lat, inverse_lat = norm_rows(latent_all[:, :KVR], gain_latent)
    length = all_rows // seqs
    latent_keys = latents.reshape(seqs, length, KVR + NOPE)
    latent_rows = latents.reshape(all_rows, KVR + NOPE)
    expand_w = jnp.pad(expand_w, ((0, NOPE), (0, 0)))
    tokens_group = tokens_group.reshape(group, features)
    grad_group = grad_group.reshape(group, features)
    route_line = route_line[:, :, :TOP]

    member = jnp.any(
        route_line[..., None] == jnp.arange(EXPERTS, dtype=jnp.int32), axis=2
    )
    earlier = (
        jnp.arange(rows, dtype=jnp.int32)[None, :] < jnp.arange(rows, dtype=jnp.int32)[:, None]
    ).astype(narrow)
    rank = jnp.einsum(
        "tq,zqe->zte", earlier, member.astype(narrow), preferred_element_type=wide
    ).astype(jnp.int32)
    here = EXPERTS // nz
    rank = jnp.where(member, rank, -1)
    rank_layer = lax.dynamic_slice_in_dim(rank, zi * here, here, 2)
    experts = [(d * upd + a) // split for d in range(layer) for a in range(upd)]
    chosen = jnp.stack([rank_layer[..., e] for e in experts], axis=-1)
    picks = (
        (chosen[..., None] == jnp.arange(SLOTS, dtype=jnp.int32))
        .astype(narrow)
        .reshape(nz, rows, layer * upd * SLOTS)
    )

    def swap_layer(values):
        return lax.all_to_all(values, LAYER, split_axis=1, concat_axis=1, tiled=True)

    grad_line = grad_line.reshape(nz, rows, features)
    grad_slots = swap_layer(
        jnp.einsum("ztk,ztf->zkf", picks, grad_line, preferred_element_type=narrow).reshape(
            nz, layer, upd, SLOTS, features
        )
    )

    hidden_group = norm_rows(tokens_group.astype(wide), gain_attn)[0].astype(narrow)
    reach = nu * local_len
    cos_group, sin_group = rotary_tables(group_pos)
    query_lin = dot(hidden_group, query_w)
    expanded = dot(latent_rows, expand_w, narrow)
    query_pos, keys_pos = group_pos[:, None], key_pos[None, :]
    query_rows, attended, stats = attend(
        query_lin, cos_group, sin_group, expanded, latent_keys, query_pos, keys_pos, seqs, heads
    )
    top = jnp.pad(jnp.max(stats[..., 0], axis=(0, 2))[None], ((0, 7), (0, 128 - heads)))
    own_member = member[0]
    split_group = (seqs, ny, nc, local_len, features)
    residual, gates, hidden_mid, hidden_mid_group, expert_slots, tops, gate_w = dispatch(
        dot(attended, output_w, narrow).reshape(split_group),
        tokens, gain_ffn[None], router_w, own_member.astype(wide), picks, top, upd,
        (w_shared_gate,), ((0, False),),
    )
    clip_value = clip_limit[0]
    clip_factor = clip_value / jnp.maximum(jnp.max(tops, axis=(0, 1))[0, :heads], clip_value)
    hidden_mid_group = hidden_mid_group.reshape(group, features)

    returned, outputs, gated, lin_gate, lin_up, up_w, down_w = run_experts(
        expert_slots, grad_slots, w_gate, w_up, w_down,
        (w_shared_up, w_shared_down), ((0, False), (1, False)), split,
    )

    shared_gate = dot(hidden_mid_group, gate_w)
    shared_up = dot(hidden_mid_group, up_w)
    shared_act = (jax.nn.silu(shared_gate) * shared_up).astype(narrow)
    shared_partial = dot(shared_act, down_w, narrow)
    shared_act_grad = dot_nt(grad_group, down_w)
    shared_gate_grad = (shared_act_grad * shared_up * silu_slope(shared_gate)).astype(narrow)
    shared_up_grad = (shared_act_grad * jax.nn.silu(shared_gate)).astype(narrow)
    mid_shared = dot_nt(shared_gate_grad, gate_w) + dot_nt(shared_up_grad, up_w)

    usual = ("x", "z")
    shared_gate_wgrad = dot_tn(hidden_mid_group, shared_gate_grad, narrow)
    shared_up_wgrad = dot_tn(hidden_mid_group, shared_up_grad, narrow)
    (
        residual_grad, attn_grad, logit_grad, ffn_gain_part, shared_sum,
        shared_gate_wgrad, shared_up_wgrad,
    ) = come_back(
        returned, mid_shared.astype(narrow).reshape(split_group),
        shared_partial.reshape(split_group), residual, gates,
        router_w, gain_ffn[None], out_grad, picks,
        (shared_gate_wgrad, shared_up_wgrad), ((0, usual), (0, usual)),
    )
    attn_grad = attn_grad.reshape(group, features)
    outputs, shared_act, attn_grad = lax.optimization_barrier((outputs, shared_act, attn_grad))
    outputs = swap_layer(outputs)
    gate_wgrad, up_wgrad, down_wgrad = unit_grads(expert_slots, grad_slots, gated, lin_gate, lin_up)
    shared_down_wgrad = dot_tn(shared_act, grad_group, narrow)
    attended_grad = dot_nt(attn_grad, output_w, narrow)
    output_wgrad = dot_tn(attended, attn_grad, narrow)

    query_lin_grad, expand_grad, rope_partial = attend_back(
        query_rows, cos_group, sin_group, expanded, latent_keys, query_pos, keys_pos, stats,
        attended_grad, seqs, heads,
    )
    hidden_partial = dot_nt(query_lin_grad, query_w, narrow)
    latent_partial = (
        dot_nt(expand_grad, expand_w).reshape(seqs, length, KVR + NOPE)
        + jnp.pad(rope_partial, ((0, 0), (0, 0), (KVR, 0)))
    ).astype(narrow)
    routed = jnp.einsum(
        "ztk,zkf->ztf", picks, outputs.reshape(nz, layer * upd * SLOTS, features),
        preferred_element_type=narrow,
    )
    query_wgrad = dot_tn(hidden_group, query_lin_grad, narrow)
    expand_wgrad = dot_tn(latent_rows, expand_grad, narrow)
    uly = yi * nc + ci

    def own_columns(values):
        return lax.dynamic_slice_in_dim(
            values.T.reshape(nb, nu, shard // nu, group), uly, 1, 1
        ).reshape(features // nu, group)

    (
        tokens_grad, block_out, latent_wgrad, gain_sums, query_wgrad, expand_wgrad, output_wgrad,
        shared_down_wgrad,
    ) = finish(
        hidden_partial.reshape(seqs, ny, nc, local_len, features),
        latent_partial.reshape(seqs, nc, ny, nx, nz, local_len, KVR + NOPE),
        tokens, residual_grad, small_whole, own_columns(hidden_group), own_columns(hidden_mid_group),
        logit_grad, ffn_gain_part, gain_attn[None], gain_latent[None],
        latent_all, cos_local, sin_local, residual,
        shared_sum, routed,
        (query_wgrad, expand_wgrad[:KVR], output_wgrad, shared_down_wgrad),
        ((0, usual), (0, ("z", "x")), (1, usual), (1, usual)),
    )
    width = KVR + RD
    small_wgrad = latent_wgrad.reshape(shard, -1)
    latent_wgrad, router_wgrad = small_wgrad[:, :width], small_wgrad[:, width:]
    ffn_gain_grad = jnp.sum(gain_sums[:, 1, :shard], axis=0)
    gain_sums = jnp.sum(gain_sums[:, 0], axis=0)
    attn_gain_grad = gain_sums[:shard]
    latent_gain_grad = lax.dynamic_slice_in_dim(
        gain_sums, shard + (zi * nx + xi) * lat_len, lat_len, 0
    )
    return (
        block_out,
        tokens_grad,
        attn_gain_grad,
        query_wgrad,
        latent_wgrad,
        latent_gain_grad,
        expand_wgrad,
        output_wgrad,
        ffn_gain_grad,
        router_wgrad,
        shared_gate_wgrad,
        shared_up_wgrad,
        shared_down_wgrad,
        gate_wgrad,
        up_wgrad,
        down_wgrad,
        clip_factor,
    )


def solution(mesh):
    blocks, group = mesh.shape["blk"], mesh.shape["ulysses"]
    chips = Mesh(
        mesh.devices.reshape(Z_SIZE, blocks // Z_SIZE, group // CORES, CORES),
        ("z", "x", "y", "core"),
    )
    blk, uly, every = ("z", "x"), ("y", "core"), ("z", "x", "y", "core")
    rows = P(None, every, None)
    unit = P(every, None, None)
    return jax.shard_map(
        per_device,
        mesh=chips,
        in_specs=(
            rows, P(blk), P(blk, uly), P(blk, None), P(blk), P(blk, uly), P(uly, blk), P(blk),
            P(blk, None), P(blk, uly), P(blk, uly), P(uly, blk), unit, unit, unit, unit, P(), rows,
        ),
        out_specs=(
            rows, rows, P(blk), P(blk, uly), P(blk, None), P(blk), P(blk, uly), P(uly, blk), P(blk),
            P(blk, None), P(blk, uly), P(blk, uly), P(uly, blk), unit, unit, unit, P(uly),
        ),
        check_vma=False,
    )
```

time: 1290 us -> 907 us (0.70)
  Pallas kernels: 0 us -> 726 us
  waiting for transfers between devices: 362 us -> 2.76 us
  local copies, waits for them, and re-layouts: 291 us -> 56.5 us
  matrix products: 294 us -> 82.9 us
  starting transfers between devices: 187 us -> 10.1 us
  other arithmetic: 139 us -> 19 us
    pallas_call x0 -> x8, Pallas kernels: none -> 726 us  [the longest x1 176 us: finish(): pl.pallas_call(functools.partial(finish_kernel, modes=modes), out_shape=[...]
    ppermute x214 -> x0, waiting for transfers between devices: 338 us -> none  [hop(): return lax.ppermute(value, axis, [(i, (i + 1) % n) for i in range(n)])]
    ppermute x214 -> x0, starting transfers between devices: 154 us -> none  [hop(): return lax.ppermute(value, axis, [(i, (i + 1) % n) for i in range(n)])]
    dot_general x18 -> x6, matrix products: 84.2 us -> 21.9 us  [dot_tn(): lax.dot_general(a, b, (((0,), (0,)), ((), ())), preferred_element_type=out)]
    dot_general x18 -> x6, matrix products: 88.5 us -> 29.8 us  [dot(): return jnp.dot(a, b, preferred_element_type=out)]
    dynamic_update_slice x56 -> x1, local copies, waits for them, and re-layouts: 52.8 us -> 0.16 us  [per_device(): lax.dynamic_update_slice(jnp.zeros((1, KVR), wide), latent_gain.astype(wi...]
    ppermute x31 -> x0, local copies, waits for them, and re-layouts: 49.6 us -> none  [hop(): return lax.ppermute(value, axis, [(i, (i + 1) % n) for i in range(n)])]
    dot_general x6 -> x2, matrix products: 53.6 us -> 5.06 us  [the longest x1 3.02 us: per_device(): jnp.einsum('ztk,ztf->zkf', picks, grad_line, preferred_element_type=narrow)]
  transfers between devices with their start and end apart: 222 -> 2, of which waited for: 84 -> 1; matrix products, arithmetic and copies ran while one was open for 48% -> 6% of each run, Pallas kernels for 0% -> 17%
where the time goes in v2:
time: 907 us; the launch traced here: 900 us
  Pallas kernels  726 us (80%)
  matrix products  82.9 us (9%)
  local copies, waits for them, and re-layouts  56.5 us (6%)
  other arithmetic  19 us (2%)
  starting transfers between devices  10.1 us (1%)
    pallas_call x1, Pallas kernels, finish(): pl.pallas_call(functools.partial(finish_kernel, modes=modes), out_shape=[...  176 us
    pallas_call x1, Pallas kernels, start(): pl.pallas_call(start_kernel, out_shape=outs, in_specs=[VMEM, ANY, VMEM, V...  151 us
    pallas_call x1, Pallas kernels, come_back(): pl.pallas_call(functools.partial(return_kernel, modes=modes), out_shape=[...  129 us
    pallas_call x1, Pallas kernels, dispatch(): pl.pallas_call(functools.partial(dispatch_kernel, plan=plan), out_shape=[...  104 us
    pallas_call x1, Pallas kernels, run_experts(): pl.pallas_call(functools.partial(expert_kernel, split=split, plan=plan),...  87.8 us
    pallas_call x1, Pallas kernels, unit_grads(): pl.pallas_call(unit_grads_kernel, grid=(units, features // step), in_spec...  31.5 us
    dot_general x6, matrix products, dot(): return jnp.dot(a, b, preferred_element_type=out)  29.8 us
    pallas_call x1, Pallas kernels, attend_back(): pl.pallas_call(functools.partial(attend_back_kernel, scale=(NOPE + RD) **...  28.8 us
  transfers between devices with their start and end apart: 2, of which 1 were waited for; matrix products, arithmetic and copies ran while one was open for 6% of the time, Pallas kernels for 17%

profile of v2, /device:TPU:0, one launch (start us, length us, event | category | flops | bytes accessed | tf_op | source)
XLA Modules:
  0.0 900.4 jit_solution(2055682230967223271)
XLA Ops:
  3.7 1.0 pad_maximum_fusion
  5.6 1.0 copy-done.6
  6.6 1.0 copy-done.7
  7.6 1.0 copy-done.9
  8.6 0.9 copy-done.10
  9.6 0.9 copy-done.11
  10.5 151.4 %shard_map.305 = (f32[8,8,512]{2,1,0:T(8,128)S(1)}, bf16[8,4,64,640]{3,2,1,0:T(8,128)(2,1)}, bf16[2048,768]{1,0:T(8,128)(2,1)}, bf16[512,1024]{1,0:T(8,128)(2,1)...) custom-call(bf16[2,64,2048]{2,1,0:T(8,128)(2,1)S(1)} %copy-done.7, ...), custom_call_target="tpu_custom_call" | custom-call | flops 120000004096 | bytes 120000000 | tf_op jit(solution)/shard_map/pallas_call | solution.py:407
  161.9 1.3 copy-done
  163.2 1.3 copy-done.12
  164.5 1.3 copy-done.15
  165.8 1.0 copy-done.17
  168.8 3.0 fusion.22
  171.8 2.3 copy.100
  174.1 5.2 all-to-all-start
  180.4 1.2 multiply_sine_fusion
  182.6 1.2 slice.74.router
  183.8 2.9 copy.93
  187.0 2.8 multiply_convert_fusion
  189.8 5.7 fusion.20.query
  195.5 8.1 fusion.5.keys
  204.2 17.8 %shard_map.306 = (bf16[512,1024]{1,0:T(8,128)(2,1)}, bf16[512,512]{1,0:T(8,128)(2,1)}, f32[2,4,256,2]{3,2,1,0:T(8,128)}) custom-call(f32[512,768]{1,0:T(8,128)} %fusion.20.query, f32[256,32]{1,0:T(8,128)} %get-tuple-element.197.cosine, f32[256,32]{1,0:T(8,128)} %get-tuple-element.196.sine, bf16[4096,1024]{1,0:T(8,128)(2,1)} %fusion.5.keys, ...), custom_call_target="tpu_custom_call" | custom-call | flops 16000000000 | bytes 16000000 | tf_op jit(solution)/shard_map/pallas_call | solution.py:529
  222.0 1.4 slice_reduce_fusion
  223.4 4.4 fusion.21
  227.9 103.7 %shard_map.307 = (f32[128,2048]{1,0:T(8,128)S(1)}, f32[128,64]{1,0:T(8,128)S(1)}, bf16[128,2048]{1,0:T(8,128)(2,1)}, bf16[2,2,2,64,2048]{4,3,2,1,0:T(8,128)(2,1)...) custom-call(bf16[2,2,2,64,2048]{4,3,2,1,0:T(8,128)(2,1)} %bitcast.139, ...), custom_call_target="tpu_custom_call" | custom-call | flops 80000000000 | bytes 80000000 | tf_op jit(solution)/shard_map/pallas_call | solution.py:1171
  331.6 1.0 copy-done.20
  333.9 1.9 copy.102.rest_0_
  335.8 2.5 copy.106
  338.9 1.9 constant_dynamic-slice_fusion.1
  340.8 1.9 constant_dynamic-slice_fusion
  343.2 4.7 fusion.23
  347.9 4.8 copy.101.grads_in.grads
  352.7 87.8 %shard_map.308 = (bf16[4,8,2,16,2176]{4,3,2,1,0:T(8,128)(2,1)}, bf16[4,8,2,16,2048]{4,3,2,1,0:T(8,128)(2,1)}, bf16[2,512,1408]{2,1,0:T(8,128)(2,1)}, bf16[2,512,...) custom-call(bf16[4,8,2,16,2176]{4,3,2,1,0:T(8,128)(2,1)} %get-tuple-e, ...), custom_call_target="tpu_custom_call" | custom-call | flops 80000000000 | bytes 80000000 | tf_op jit(solution)/shard_map/pallas_call | solution.py:1569
  440.5 3.7 fusion.24
  444.3 2.2 multiply_convert_fusion.1
  446.5 1.9 fusion.25
  448.4 3.5 fusion.27.rest_0_
  451.9 3.2 fusion.26
  455.1 3.5 fusion.28.rest_1_
  458.7 3.4 add_convert_fusion.1
  462.1 129.1 %shard_map.309 = (f32[128,2048]{1,0:T(8,128)}, bf16[2,2,2,64,2048]{4,3,2,1,0:T(8,128)(2,1)}, bf16[128,64]{1,0:T(8,128)(2,1)}, f32[1,2048]{1,0:T(1,128)}, bf16[2,...) custom-call(bf16[4,8,2,16,2176]{4,3,2,1,0:T(8,128)(2,1)} %get-tuple-element.85.returned, ...), custom_call_target="tpu_custom_call" | custom-call | flops 99999997952 | bytes 100000000 | tf_op jit(solution)/shard_map/pallas_call | solution.py:1330
  591.2 3.7 fusion.29.grads
  594.8 28.8 %shard_map.310 = (bf16[512,768]{1,0:T(8,128)(2,1)}, bf16[4096,1024]{1,0:T(8,128)(2,1)}, f32[2,2048,128]{2,1,0:T(8,128)}) custom-call(bf16[512,1024]{1,0:T(8,128)(2,1)} %get-tuple-element.73.query, f32[256,32]{1,0:T(8,128)} %get-tuple-element.197.cosine, f32[256,32]{1,0:T(8,128)} %get-tuple-element.196.sine, bf16[4096,1024]{1,0:T(8,128)(2,1)} %fusion.5.keys, ...), custom_call_target="tpu_custom_call" | custom-call | flops 24999999488 | bytes 25000000 | tf_op jit(solution)/shard_map/pallas_call | solution.py:550
  623.6 5.5 fusion.30
  629.1 3.5 fusion.32.rest_0_
  632.6 2.6 fusion.33.rest_2_
  635.3 5.5 fusion.rest_1_
  640.8 9.4 %fusion.3 = f32[4096,640]{1,0:T(8,128)} fusion(bf16[4096,1024]{1,0:T(8,128)(2,1)S(1)} %bitcast.141, bf16[512,1024]{1,0:T(8,128)(2,1)S(1)} %copy-done.19), kind=kOutput, calls=%fused_computation.11 | convolution fusion | flops 5368709120 | bytes 19922944 | tf_op jit(solution)/shard_map/dot_general | solution.py:38
  650.2 2.4 copy.107
  652.6 4.9 all-to-all-start.1
  657.5 2.4 copy.112
  659.9 1.1 copy.113
  661.0 7.1 add_convert_fusion
  668.1 3.3 fusion.34.rest_3_
  671.4 31.5 %shard_map.312 = (f32[2,2048,1408]{2,1,0:T(8,128)}, f32[2,2048,1408]{2,1,0:T(8,128)}, f32[2,1408,2048]{2,1,0:T(8,128)}) custom-call(bf16[4,8,2,16,2176]{4,3,2,1,0:T(8,128)(2,1)} %get-tuple-element.79.rows_in.rows, bf16[4,8,2,16,2048]{4,3,2,1,0:T(8,128)(2,1)} %copy.101.grads_in.grads, bf16[2,512,1408]{2,1,0:T(8,128)(2,1)} %get-tuple-element.112.gated, ...), custom_call_target="tpu_custom_call" | custom-call | flops 35000000512 | bytes 35000000 | tf_op jit(solution)/shard_map/pallas_call | solution.py:1620
  702.9 2.8 all-to-all-done.1
  705.7 2.5 copy.108
  708.2 2.0 fusion.31.routed
  710.2 176.3 %shard_map.311 = (bf16[2,64,2048]{2,1,0:T(8,128)(2,1)}, bf16[2,64,2048]{2,1,0:T(8,128)(2,1)}, f32[4,64,640]{2,1,0:T(8,128)}, f32[4,8,768]{2,1,0:T(8,128)}, f32[2...) custom-call(bf16[2,2,2,64,2048]{4,3,2,1,0:T(8,128)(2,1)} %bitcast.134, ...), custom_call_target="tpu_custom_call" | custom-call | flops 190000005120 | bytes 190000000 | tf_op jit(solution)/shard_map/pallas_call | solution.py:992
  886.6 1.5 slice_reduce_fusion.3
  888.0 0.9 slice_reduce_fusion.2
  890.1 1.0 slice.78
  891.8 2.1 copy.118
  893.9 1.9 copy.131
  896.7 0.9 copy.133
  (167 shorter events, 15.2 us)
Async XLA Ops:
  5.3 156.6 %copy-start.3 = (f32[128,32]{1,0:T(8,128)}, f32[128,32]{1,0:T(8,128)S(1)}, u32[]{:S(2)}) copy-start(f32[128,32]{1,0:T(8,128)S(1)} %get-tuple-element.198.sine) | copy-start | bytes 49156
  5.3 156.6 %copy-start.4 = (f32[128,32]{1,0:T(8,128)}, f32[128,32]{1,0:T(8,128)S(1)}, u32[]{:S(2)}) copy-start(f32[128,32]{1,0:T(8,128)S(1)} %get-tuple-element.199.cosine) | copy-start | bytes 49156
  5.6 1.0 copy-start.6
  6.6 1.0 copy-start.7
  7.6 1.0 copy-start.9
  8.6 0.9 copy-start.10
  9.6 0.9 copy-start.11
  161.9 1.3 copy-start
  163.2 1.3 copy-start.12
  164.5 1.3 copy-start.15
  165.8 1.0 copy-start.17
  166.8 0.7 copy-start.21
  167.8 0.6 copy-start.36
  168.8 3.0 copy-start.27
  168.8 59.1 %copy-start.2 = (bf16[4,128,256]{2,1,0:T(8,128)(2,1)}, bf16[4,128,256]{2,1,0:T(8,128)(2,1)S(1)}, u32[]{:S(2)}) copy-start(bf16[4,128,256]{2,1,0:T(8,128)(2,1)S(1)} %get-tuple-element.187.picks) | copy-start | bytes 786436
  174.1 7.5 copy-start.34
  174.1 173.8 %all-to-all-start = ((bf16[4,8,2,16,2048]{4,3,2,0,1:T(8,128)(2,1)}), bf16[4,8,2,16,2048]{4,3,2,0,1:T(8,128)(2,1)}, u32[]{:S(2)}, u32[]{:S(2)}) async-start(bf16[4,8,2,16,2048]{4,3,2,0,1:T(8,128)(2,1)} %copy.100), calls=%async_computation | async-start | bytes 8388608 | tf_op jit(solution)/shard_map/all_to_all | solution.py:1769
  179.3 3.1 slice-start
  181.8 5.1 copy-start.37
  181.8 46.0 %copy-start.5 = (f32[8,1,256]{2,1,0:T(1,128)}, f32[8,1,256]{2,1,0:T(1,128)S(1)}, u32[]{:S(2)}) copy-start(f32[8,1,256]{2,1,0:T(1,128)S(1)} %get-tuple-element.194) | copy-start | bytes 24580
  183.8 44.0 %copy-start.1 = (bf16[2048,64]{1,0:T(8,128)(2,1)}, bf16[2048,64]{1,0:T(8,128)(2,1)S(1)}, u32[]{:S(2)}) copy-start(bf16[2048,64]{1,0:T(8,128)(2,1)S(1)} %slice.74.router) | copy-start | bytes 786436
  186.9 8.5 slice-start.1
  189.7 5.7 copy-start.24
  189.7 5.7 copy-start.18
  189.8 5.7 slice-start.2
  223.4 4.4 copy-start.8
  331.6 1.0 copy-start.20
  332.6 0.6 copy-start.22
  440.5 3.8 copy-start.13
  440.5 3.8 copy-start.39
  440.5 3.8 copy-start.45
  444.3 2.2 copy-start.43
  446.5 5.4 copy-start.40
  455.1 3.5 copy-start.42
  462.1 129.1 %copy-start.16 = (bf16[512,2048]{1,0:T(8,128)(2,1)S(1)}, bf16[512,2048]{1,0:T(8,128)(2,1)}, u32[]{:S(2)}) copy-start(bf16[512,2048]{1,0:T(8,128)(2,1)} %copy-done.15) | copy-start | bytes 6291460
  623.6 5.5 copy-start.25
  623.6 5.5 copy-start.46
  623.6 11.6 %slice-start.3 = ((s8[5242880]{0:T(1024)(128)(4,1)}), s8[4194304]{0:T(1024)(128)(4,1)S(1)}, s32[]{:S(2)}) async-start(s8[5242880]{0:T(1024)(128)(4,1)} %bitcast.131), calls=%async_computation.5 | async-start | bytes 8388608
  623.6 11.6 %slice-start.5 = ((s8[8388608]{0:T(1024)(128)(4,1)}), s8[4194304]{0:T(1024)(128)(4,1)S(1)}, s32[]{:S(2)}) async-start(s8[8388608]{0:T(1024)(128)(4,1)} %bitcast.140), calls=%async_computation.7 | async-start | bytes 8388608
  629.1 3.5 copy-start.38
  629.1 3.5 copy-start.44
  629.1 6.1 slice-start.4
  629.1 6.1 slice-start.6
  635.2 5.5 copy-start.19
  640.8 9.4 %copy-start.23 = (bf16[4,8,2,16,2048]{4,3,2,1,0:T(8,128)(2,1)S(1)}, bf16[4,8,2,16,2048]{4,3,2,1,0:T(8,128)(2,1)}, u32[]{:S(2)}) copy-start(bf16[4,8,2,16,2048]{4,3,2,1,0:T(8,128)(2,1)} %get-tuple-element.100) | copy-start | bytes 12582916
  652.6 7.4 copy-start.29
  652.6 53.1 %all-to-all-start.1 = ((bf16[4,8,2,16,2048]{4,3,2,0,1:T(8,128)(2,1)}), bf16[4,8,2,16,2048]{4,3,2,0,1:T(8,128)(2,1)}, u32[]{:S(2)}, u32[]{:S(2)}) async-start(bf16[4,8,2,16,2048]{4,3,2,0,1:T(8,128)(2,1)} %copy.107), calls=%async_computation.1 | async-start | bytes 8388608 | tf_op jit(solution)/shard_map/all_to_all | solution.py:1769
  657.5 3.5 copy-start.26
  661.0 7.1 copy-start.14
  661.0 7.1 copy-start.41
  702.9 5.3 copy-start.28
  886.6 9.3 %copy-start.33 = (bf16[2,64,2048]{2,1,0:T(8,128)(2,1)S(1)}, bf16[2,64,2048]{2,1,0:T(8,128)(2,1)}, u32[]{:S(2)}) copy-start(bf16[2,64,2048]{2,1,0:T(8,128)(2,1)} %get-tuple-element.254) | copy-start | bytes 1572868
  886.6 10.1 %copy-start.30 = (f32[256,768]{1,0:T(8,128)S(1)}, f32[256,768]{1,0:T(8,128)}, u32[]{:S(2)}) copy-start(f32[256,768]{1,0:T(8,128)} %get-tuple-element.256) | copy-start | bytes 2359300
  886.6 11.0 %copy-start.35 = (f32[64,1024]{1,0:T(8,128)S(1)}, f32[64,1024]{1,0:T(8,128)}, u32[]{:S(2)}) copy-start(f32[64,1024]{1,0:T(8,128)} %get-tuple-element.259) | copy-start | bytes 786436
  891.1 7.2 copy-start.32
  893.9 5.1 copy-start.31

commit v3 on v2

--- a/solution.py
+++ b/solution.py
@@ -17,6 +17,7 @@
 TOP = 6
 CAP = 14
 SLOTS = 16
+HEAD_START = 12
 Z_SIZE = 4
 CORES = 2
 
@@ -223,8 +224,8 @@
 def start_kernel(
     tokens, grads, cosine, sine, gains, small, routes, w_query, w_expand, w_output,
     gains_out, small_out, query_out, expand_out, output_out,
-    tokens_out, grads_out, line_out, routes_out, latents_out, hidden_out, latent_all_out,
-    own_latent, send, recv, local,
+    group_out, grads_out, picks_out, member_out, slots_out, latents_out, hidden_out, latent_all_out,
+    own_latent, own_hidden, routes_line, grads_line, send, recv, local, *, units, split,
 ):
     nz, nx, ny, nc = (lax.axis_size(a) for a in AXES)
     nb, nu = nz * nx, ny * nc
@@ -248,12 +249,14 @@
     def line_chain(src, dst):
         ports = [wires.port() for _ in range(nz)]
         wires.push(src, dst.at[1], ports[1], "z")
-        load(src, dst.at[0])
+        mine = load(src, dst.at[0])
         for sz in range(1, nz):
             yield
             wires.arrived(dst.at[sz], ports[sz], "z")
             if sz + 1 < nz:
                 wires.push(dst.at[sz], dst.at[sz + 1], ports[sz + 1], "z")
+        mine.wait()
+        waited.add(id(mine))
 
     def main():
         g_gains = BlockGather(wires, gains, gains_out, lambda ref, owner: ref.at[owner], False)
@@ -306,6 +309,10 @@
         x = tokens[...].astype(wide).reshape(rows, features)
         hidden = norm_rows(x, gain)[0].astype(narrow)
         hidden_out[...] = hidden
+        own_hidden[...] = hidden.reshape(tokens.shape)
+        spread_hidden = GroupGather(wires, own_hidden, group_out)
+        spread_hidden.start()
+        load(own_hidden, group_out.at[:, 0, 0])
         width = small_out.shape[-1]
         latent_all = dot(hidden, small_out[...].reshape(features, width))[:, : KVR + RD]
         latent_all_out[...] = latent_all
@@ -350,6 +357,38 @@
             for sx in range(nx):
                 yield
                 wires.arrived(latents_out.at[:, 1, sy, sx], cx_ports[sy][sx], "core")
+        yield from spread_hidden.chain()
+
+    def slots_chain():
+        yield from line_chain(routes, routes_line)
+        yield from line_chain(grads, grads_line)
+        count = rows
+        earlier = (
+            lax.broadcasted_iota(jnp.int32, (count, count), 1)
+            < lax.broadcasted_iota(jnp.int32, (count, count), 0)
+        ).astype(narrow)
+        columns = picks_out.shape[-1]
+        expert = lax.broadcasted_iota(jnp.int32, (EXPERTS, columns), 0)
+        column = lax.broadcasted_iota(jnp.int32, (EXPERTS, columns), 1)
+        unit = column // SLOTS
+        if split > 1:
+            unit = unit // split
+        chosen = (expert == unit + lax.axis_index("z") * (EXPERTS // nz)).astype(narrow)
+        slot = lax.rem(lax.broadcasted_iota(jnp.int32, (count, columns), 1), SLOTS)
+        names = lax.broadcasted_iota(jnp.int32, (count, EXPERTS), 1)
+        for s in range(nz):
+            member = sum(
+                (routes_line[s, :, j : j + 1] == names).astype(wide) for j in range(TOP)
+            )
+            if s == 0:
+                member_out[...] = member
+            rank = dot(earlier, member.astype(narrow))
+            code = jnp.where(member > 0, rank, -1.0).astype(narrow)
+            pick = (dot(code, chosen) == slot.astype(wide)).astype(narrow)
+            picks_out[s] = pick
+            row_grads = grads_line[s].reshape(rows, features)
+            shaped = (slots_out.shape[0],) + slots_out.shape[2:]
+            slots_out[:, s] = dot_tn(pick, row_grads).astype(narrow).reshape(shaped)
 
     def group_chain(src, dst):
         gather = GroupGather(wires, src, dst)
@@ -368,19 +407,19 @@
         array_chain(w_query, query_out, rows_of(w_query.shape[0]), False),
         array_chain(w_expand, expand_out, rows_of(w_expand.shape[0]), True),
         array_chain(w_output, output_out, columns_of(w_output.shape[1]), False),
-        line_chain(routes, routes_out),
-        group_chain(tokens, tokens_out),
+        slots_chain(),
         group_chain(grads, grads_out),
-        line_chain(grads, line_out),
     ]
-    weave(first, others, 1)
+    for _ in range(HEAD_START):
+        next(first)
+    weave(first, others, 2)
     wires.drain()
     for copy in used:
         if id(copy) not in waited:
             copy.wait()
 
 
-def start(tokens, grads, cosine, sine, gains, small, routes, weights):
+def start(tokens, grads, cosine, sine, gains, small, routes, weights, units, split):
     nz, nx, ny, nc = (lax.axis_size(a) for a in AXES)
     nb, nu = nz * nx, ny * nc
     seqs, local_len, features = tokens.shape
@@ -391,6 +430,7 @@
         size[dim] *= nb
         return shape(tuple(size), w.dtype)
 
+    rows = seqs * local_len
     grouped = (seqs, ny, nc, local_len, features)
     outs = [
         shape((nb,) + gains.shape, wide),
@@ -398,19 +438,23 @@
         *[whole(w, d) for w, d in zip(weights, (0, 0, 1))],
         shape(grouped, narrow),
         shape(grouped, narrow),
-        shape((nz,) + grads.shape, narrow),
-        shape((nz,) + routes.shape, routes.dtype),
+        shape((nz, rows, nx * nu * units * SLOTS), narrow),
+        shape((rows, EXPERTS), wide),
+        shape((nx * nu, nz, units, SLOTS, features), narrow),
         shape((seqs, nc, ny, nx, nz, local_len, KVR + NOPE), narrow),
         shape((seqs * local_len, features), narrow),
         shape((seqs * local_len, KVR + RD), wide),
     ]
     return pl.pallas_call(
-        start_kernel,
+        functools.partial(start_kernel, units=units, split=split),
         out_shape=outs,
         in_specs=[VMEM, ANY, VMEM, VMEM, VMEM, VMEM, VMEM] + [ANY] * 3,
-        out_specs=[VMEM, VMEM] + [ANY] * 6 + [VMEM] + [ANY] + [VMEM, VMEM],
+        out_specs=[VMEM, VMEM] + [ANY] * 5 + [VMEM] * 3 + [ANY] + [VMEM, VMEM],
         scratch_shapes=[
             pltpu.VMEM((seqs, local_len, KVR + NOPE), narrow),
+            pltpu.VMEM(tokens.shape, narrow),
+            pltpu.VMEM((nz,) + routes.shape, routes.dtype),
+            pltpu.VMEM((nz,) + grads.shape, narrow),
             pltpu.SemaphoreType.DMA((384,)),
             pltpu.SemaphoreType.DMA((384,)),
             pltpu.SemaphoreType.DMA((16,)),
@@ -734,8 +778,8 @@
 
 
 def finish_kernel(
-    hidden_partial, latent_partial, tokens, residual_grad, small, hidden_t, mid_t, logit_grad,
-    ffn_gain, gain_attn, gain_latent, latent_all, cosine, sine, residual, shared_sum, routed,
+    hidden_sum, latent_partial, tokens, residual_grad, small, hidden_t, mid_t, logit_grad,
+    ffn_gain, gain_attn, gain_latent, latent_all, cosine, sine, residual, shared_sum, picks, slots,
     *rest, modes,
 ):
     count = len(modes)
@@ -743,8 +787,8 @@
     tokens_grad, block_out, latent_w_out, gains_out, *rest = rest
     outs, rest = rest[:count], rest[count:]
     (
-        hid_own, hid_other, hid_came, lat_own, lat_other, lat_came, lat_x, lat_z,
-        own_lag, lag_group, wide_acc, lat_wgrad, gain_terms, routed_own, routed_came, *rest,
+        lat_own, lat_x, lat_z,
+        own_lag, lag_group, wide_acc, lat_wgrad, gain_terms, routed_slots, routed_own, routed_came, *rest,
     ) = rest
     buffers, rest = rest[: 3 * count], rest[3 * count :]
     lw_buffers, g_buffers = rest[:3], rest[3:6]
@@ -777,12 +821,14 @@
 
     def routed_chain():
         ports = [wires.port() for _ in range(nz)]
-        loading = {s: load(routed.at[s], routed_own.at[s]) for s in [*range(1, nz), 0]}
+        loading = {s: load(slots.at[:, s], routed_slots.at[s]) for s in [*range(1, nz), 0]}
         for s in [*range(1, nz), 0]:
             own = routed_own.at[s]
             last = (s or nz) - 1
             yield
             loading[s].wait()
+            term = dot(picks[s], routed_slots[s].reshape(picks.shape[2], features))
+            routed_own[s] = term.astype(narrow)
             if last:
                 wires.arrived(routed_came.at[last - 1], ports[last], "z")
                 add_into(own, own, routed_came.at[last - 1])
@@ -796,53 +842,22 @@
         block_out[...] = total.astype(narrow).reshape(tokens.shape)
 
     def latent_chain():
-        c_ports = [[wires.port() for _ in range(nx)] for _ in range(ny)]
-        y_ports = [[wires.port() for _ in range(nx)] for _ in range(ny)]
         x_ports = [wires.port() for _ in range(nx)]
         z_ports = [wires.port() for _ in range(nz)]
-        order_y, order_x = [*range(1, ny), 0], [*range(1, nx), 0]
-        blocks = [(sy, sx) for sy in order_y for sx in order_x]
-        loading = []
-
-        def load_block():
-            number = len(loading)
-            if number < len(blocks):
-                sy, sx = blocks[number]
-                loading.append(load(latent_partial.at[:, 0, sy, sx], lat_own.at[number % 2]))
-
-        for sy, sx in blocks:
-            wires.push(
-                latent_partial.at[:, 1, sy, sx], lat_other.at[:, sy, sx], c_ports[sy][sx], "core"
-            )
-        load_block()
-        load_block()
+        wires.push(latent_partial.at[:, 1], lat_x.at[:, 0], x_ports[1], "x")
+        order_x = [*range(2, nx), 0]
+        loading = {sx: load(latent_partial.at[:, sx], lat_own.at[:, sx]) for sx in order_x}
         yield
-        for sy in order_y:
-            for sx in order_x:
-                own = lat_other.at[:, sy, sx]
-                number = blocks.index((sy, sx))
-                yield
-                wires.arrived(own, c_ports[sy][sx], "core")
-                loading[number].wait()
-                add_into(own, own, lat_own.at[number % 2])
-                load_block()
-                last = (sy or ny) - 1
-                if last:
-                    yield
-                    wires.arrived(lat_came.at[:, last - 1, sx], y_ports[last][sx], "y")
-                    add_into(own, own, lat_came.at[:, last - 1, sx])
-                if sy:
-                    wires.push(own, lat_came.at[:, sy - 1, sx], y_ports[sy][sx], "y")
-                    continue
-                last = (sx or nx) - 1
-                if last:
-                    yield
-                    wires.arrived(lat_x.at[:, last - 1], x_ports[last], "x")
-                    add_into(own, own, lat_x.at[:, last - 1])
-                if sx:
-                    wires.push(own, lat_x.at[:, sx - 1], x_ports[sx], "x")
+        for sx in order_x:
+            own, last = lat_own.at[:, sx], (sx or nx) - 1
+            yield
+            wires.arrived(lat_x.at[:, last - 1], x_ports[last], "x")
+            loading[sx].wait()
+            add_into(own, own, lat_x.at[:, last - 1])
+            if sx:
+                wires.push(own, lat_x.at[:, sx - 1], x_ports[sx], "x")
         for sz in [*range(1, nz), 0]:
-            own = lat_other.at[:, 0, 0, sz]
+            own = lat_own.at[:, 0, sz]
             last = (sz or nz) - 1
             if last:
                 yield
@@ -852,20 +867,16 @@
                 wires.push(own, lat_z.at[:, sz - 1], z_ports[sz], "z")
 
     def main():
-        hidden = group_sum_chain(wires, hidden_partial, hid_own, hid_other, hid_came, load)
         latent = latent_chain()
         next(latent)
-        next(hidden)
         for s in scatters:
             s.start(queue)
         queue.go(3)
         yield
-        for _ in hidden:
-            yield
         for _ in latent:
             yield
         width = KVR + RD
-        lat = lat_other[:, 0, 0, 0].astype(wide).reshape(rows, KVR + NOPE)[:, :width]
+        lat = lat_own[:, 0, 0].astype(wide).reshape(rows, KVR + NOPE)[:, :width]
         latent_grad = lat[:, :KVR]
         _, normed, inverse = norm_rows(latent_all[:, :KVR], gain_latent[...])
         lat_in = norm_input_back(latent_grad, normed, inverse, gain_latent[...])
@@ -880,7 +891,7 @@
         own_copy = load(own_lag, lag_group.at[:, 0, 0])
         x = tokens[...].astype(wide).reshape(rows, features)
         _, normed_in, inverse_in = norm_rows(x, gain_attn[...])
-        hidden_grad = wide_acc[...] + hid_own[:, 0].astype(wide).reshape(rows, features)
+        hidden_grad = wide_acc[...] + hidden_sum[...].astype(wide).reshape(rows, features)
         wide_acc[...] = residual_grad[...] + norm_input_back(
             hidden_grad, normed_in, inverse_in, gain_attn[...]
         )
@@ -945,8 +956,8 @@
 
 
 def finish(
-    hidden_partial, latent_partial, tokens, residual_grad, small, hidden_t, mid_t, logit_grad,
-    ffn_gain, gain_attn, gain_latent, latent_all, cosine, sine, residual, shared_sum, routed,
+    hidden_sum, latent_partial, tokens, residual_grad, small, hidden_t, mid_t, logit_grad,
+    ffn_gain, gain_attn, gain_latent, latent_all, cosine, sine, residual, shared_sum, picks, slots,
     partials, modes,
 ):
     nz, nx, ny, nc = (lax.axis_size(a) for a in AXES)
@@ -961,15 +972,9 @@
         shards.append(tuple(size))
     width, shard = KVR + RD, features // nb
     padded = small.shape[-1]
-    latents = (seqs, ny, nx, nz, local_len, KVR + NOPE)
     few = lambda n: max(n - 1, 1)
     scratch = [
-        pltpu.VMEM((seqs, ny, local_len, features), narrow),
-        pltpu.VMEM((seqs, ny, local_len, features), narrow),
-        pltpu.VMEM((seqs, few(ny), local_len, features), narrow),
-        pltpu.VMEM((2, seqs, nz, local_len, KVR + NOPE), narrow),
-        pltpu.VMEM(latents, narrow),
-        pltpu.VMEM((seqs, few(ny), nx, nz, local_len, KVR + NOPE), narrow),
+        pltpu.VMEM((seqs, nx, nz, local_len, KVR + NOPE), narrow),
         pltpu.VMEM((seqs, few(nx), nz, local_len, KVR + NOPE), narrow),
         pltpu.VMEM((seqs, few(nz), local_len, KVR + NOPE), narrow),
         pltpu.VMEM((seqs, local_len, padded), narrow),
@@ -977,6 +982,7 @@
         pltpu.VMEM((rows, features), wide),
         pltpu.VMEM((nb, shard // nu, padded), narrow),
         pltpu.VMEM((nb, 8, shard + KVR), wide),
+        pltpu.VMEM((nz, nx * nu, *slots.shape[2:]), narrow),
         pltpu.VMEM((nz, rows, features), narrow),
         pltpu.VMEM((few(nz), rows, features), narrow),
     ]
@@ -998,7 +1004,7 @@
             shape((nu, 8, shard + KVR), wide),
             *[shape(size, wide) for size in shards],
         ],
-        in_specs=[ANY, ANY] + [VMEM] * 14 + [ANY] * (1 + len(partials)),
+        in_specs=[VMEM, ANY] + [VMEM] * 15 + [ANY] * (1 + len(partials)),
         out_specs=[VMEM] * (4 + len(partials)),
         scratch_shapes=scratch,
         compiler_params=pltpu.CompilerParams(
@@ -1006,8 +1012,8 @@
         ),
         cost_estimate=costs(190),
     )(
-        hidden_partial, latent_partial, tokens, residual_grad, small, hidden_t, mid_t, logit_grad,
-        ffn_gain, gain_attn, gain_latent, latent_all, cosine, sine, residual, shared_sum, routed,
+        hidden_sum, latent_partial, tokens, residual_grad, small, hidden_t, mid_t, logit_grad,
+        ffn_gain, gain_attn, gain_latent, latent_all, cosine, sine, residual, shared_sum, picks, slots,
         *partials,
     )
 
@@ -1109,15 +1115,15 @@
             outgoing[s] = dot_tn(picks[s], line[s]).astype(narrow).reshape(outgoing.shape[1:])
             for k in range(1, layer.count):
                 target = layer.number(k)
-                layer.push(wires, outgoing.at[s, target], rows_out.at[s, me], ports[s][k], k)
-            load(outgoing.at[s, me], rows_out.at[s, me])
+                layer.push(wires, outgoing.at[s, target], rows_out.at[me, s], ports[s][k], k)
+            load(outgoing.at[s, me], rows_out.at[me, s])
             next(chain, None)
         for _ in chain:
             pass
         for s in range(nz):
             yield
             for k in range(1, layer.count):
-                wires.arrived(rows_out.at[s, layer.number(k, -1)], ports[s][k], "z")
+                wires.arrived(rows_out.at[layer.number(k, -1), s], ports[s][k], "z")
 
     def tops():
         z_ports = [wires.port() for _ in range(nz)]
@@ -1175,7 +1181,7 @@
             shape((rows, EXPERTS), wide),
             shape((rows, features), narrow),
             shape((seqs, ny, nc, local_len, features), narrow),
-            shape((nz, layer, units, SLOTS, extended), narrow),
+            shape((layer, nz, units, SLOTS, extended), narrow),
             shape((nx, nz) + top.shape, wide),
             *[whole_array(w, dim) for w, (dim, _) in zip(shards, plan)],
         ],
@@ -1240,9 +1246,9 @@
         for s in order:
             for k in range(1, layer.count):
                 layer.push(
-                    wires, returned.at[s, layer.number(k)], back.at[s, me], ports[s][k], k
+                    wires, returned.at[layer.number(k), s], back.at[s, me], ports[s][k], k
                 )
-            own_copies[s] = load(returned.at[s, me], back.at[s, me])
+            own_copies[s] = load(returned.at[me, s], back.at[s, me])
         shared = group_sum_chain(wires, partial, own, other, came, load)
         next(shared)
         yield
@@ -1316,7 +1322,7 @@
         shards.append(tuple(size))
     scratch = [
         part, part, part, part, part, part,
-        pltpu.VMEM(returned.shape, narrow),
+        pltpu.VMEM((nz, nx * ny * nc) + returned.shape[2:], narrow),
         pltpu.VMEM((2, nz - 1, rows, extended), narrow),
         pltpu.VMEM((seqs, local_len, features), narrow),
     ]
@@ -1366,11 +1372,12 @@
         (lax.axis_index("z") * nx + lax.axis_index("x")) * ny + lax.axis_index("y")
     ) * nc + lax.axis_index("core")
     first_unit = first_unit * units
-    per = min(nz, max(1, 512 // (layer * SLOTS)))
-    block = per * layer * SLOTS
-    blocks = nz // per
+    per = min(layer, max(1, 512 // (nz * SLOTS)))
+    block = per * nz * SLOTS
+    blocks = layer // per
     wires = Wires(send, recv)
-    greet(("z", "x"))
+    if count:
+        greet(("z", "x"))
     used = []
 
     def load(src, dst):
@@ -1391,7 +1398,7 @@
             g.forward(0, 0)
         yield
         plans = [g.rounds() for g in gathers]
-        for step in range(max(len(p) for p in plans)):
+        for step in range(max([len(p) for p in plans] + [0])):
             for g, p in zip(gathers, plans):
                 for slot in p[step] if step < len(p) else []:
                     g.take(*slot)
@@ -1407,10 +1414,10 @@
         slot = a % rows.shape[0]
         return [
             load(rows_in.at[:, :, a], rows.at[slot]),
-            load(wg.at[a], bg),
-            load(wu.at[a], bu),
+            load(wg.at[a], bg.at[slot]),
+            load(wu.at[a], bu.at[slot]),
             load(grads_in.at[:, :, a], grads.at[slot]),
-            load(wd.at[a], bd),
+            load(wd.at[a], bd.at[slot]),
         ]
 
     fetched = fetch(0)
@@ -1455,13 +1462,15 @@
 
         for copy in waiting:
             copy.wait()
+        if a + 1 < units:
+            fetched = fetch(a + 1)
 
         def forward(b, cols):
             span = pl.ds(pl.multiple_of(b * block, block), block)
             picked = row_block(rows, b, slice(0, features))
-            lin = dot(picked, bg[:, cols])
-            up = dot(picked, bu[:, cols])
-            grad = dot_nt(row_block(grads, b, slice(None)), bd[cols, :]) * weights_of(b)
+            lin = dot(picked, bg[slot_a, :, cols])
+            up = dot(picked, bu[slot_a, :, cols])
+            grad = dot_nt(row_block(grads, b, slice(None)), bd[slot_a, cols, :]) * weights_of(b)
             s = jax.nn.sigmoid(lin)
             silu = lin * s
             value = (silu * up).astype(narrow)
@@ -1509,16 +1518,16 @@
             def _(b):
                 span = pl.ds(pl.multiple_of(b * block, block), block)
                 cols = spread(i)
-                out = dot(act[span, :], bd[:, cols])
+                out = dot(act[span, :], bd[slot_a, :, cols])
                 dots[span, :] += jnp.sum(
                     out * row_block(grads, b, cols).astype(wide), axis=1, keepdims=True
                 )
-                shaped = (per, layer, SLOTS, 256)
+                shaped = (per, nz, SLOTS, 256)
                 out_stage[slot, pl.ds(b * per, per)] = (
                     (out * weights_of(b)).astype(narrow).reshape(shaped)
                 )
-                inward = dot_nt(gate_buf[span, :], bg[cols, :]) + dot_nt(
-                    up_buf[span, :], bu[cols, :]
+                inward = dot_nt(gate_buf[span, :], bg[slot_a, cols, :]) + dot_nt(
+                    up_buf[span, :], bu[slot_a, cols, :]
                 )
                 back_stage[slot, pl.ds(b * per, per)] = inward.astype(narrow).reshape(shaped)
 
@@ -1536,15 +1545,12 @@
             high = value.astype(narrow).astype(wide)
             lanes = jnp.where(lane == expert, high, 0.0)
             lanes = jnp.where(lane == expert + EXPERTS, value - high, lanes)
-            rest_ = lanes.astype(narrow).reshape(per, layer, SLOTS, 2 * EXPERTS)
+            rest_ = lanes.astype(narrow).reshape(per, nz, SLOTS, 2 * EXPERTS)
             back_stage[0, pl.ds(b * per, per), :, :, : 2 * EXPERTS] = rest_
 
         extra_copy = load(
             back_stage.at[0, :, :, :, : 2 * EXPERTS], returned.at[:, :, a, :, features:]
         )
-        if a + 1 < units:
-            fetched = fetch(a + 1)
-
         extra_copy.wait()
     for copy in saved:
         copy.wait()
@@ -1565,7 +1571,7 @@
     extended = rows_in.shape[-1]
 
     slots = min(units, 2)
-    lines = (nz, layer, SLOTS)
+    lines = (layer, nz, SLOTS)
     return pl.pallas_call(
         functools.partial(expert_kernel, split=split, plan=plan),
         out_shape=[
@@ -1579,9 +1585,9 @@
         scratch_shapes=[
             pltpu.VMEM((slots,) + lines + (extended,), narrow),
             pltpu.VMEM((slots,) + lines + (features,), narrow),
-            pltpu.VMEM((features, hidden), narrow),
-            pltpu.VMEM((features, hidden), narrow),
-            pltpu.VMEM((hidden, features), narrow),
+            pltpu.VMEM((slots, features, hidden), narrow),
+            pltpu.VMEM((slots, features, hidden), narrow),
+            pltpu.VMEM((slots, hidden, features), narrow),
             pltpu.VMEM((total, hidden), narrow),
             pltpu.VMEM((total, hidden), narrow),
             pltpu.VMEM((total, hidden), narrow),
@@ -1595,7 +1601,8 @@
             pltpu.SemaphoreType.DMA((4, 2)),
         ],
         compiler_params=pltpu.CompilerParams(
-            collective_id=4, has_side_effects=True, vmem_limit_bytes=60 * 1024 * 1024
+            collective_id=4 if shards else None, has_side_effects=bool(shards),
+            vmem_limit_bytes=60 * 1024 * 1024,
         ),
         cost_estimate=costs(80),
     )(rows_in, grads_in, wg, wu, wd, *shards)
@@ -1609,10 +1616,10 @@
 
 
 def unit_grads(rows, grads, gated, lin_gate, lin_up):
-    nz, layer, units, _, features = grads.shape
+    layer, nz, units, _, features = grads.shape
     _, total, hidden = gated.shape
     step = 512 if total <= 512 else 128
-    lines = (nz, layer, 1, SLOTS, step)
+    lines = (layer, nz, 1, SLOTS, step)
     shape = jax.ShapeDtypeStruct
     line_spec = pl.BlockSpec(lines, lambda a, i: (0, 0, a, 0, i))
     unit_spec = pl.BlockSpec((1, total, hidden), lambda a, i: (a, 0, 0))
@@ -1720,12 +1727,19 @@
     cos_local, sin_local = rotary_tables(jnp.tile(local_pos, seqs))
     (
         gains_all, small_all, query_w, expand_w, output_w,
-        tokens_group, grad_group, grad_line, route_line, latents, hidden_local, latent_all,
+        hidden_group, grad_group, picks, own_member, grad_slots, latents, _, latent_all,
     ) = start(
         tokens, out_grad, cos_local, sin_local, gains, small,
-        jnp.pad(route_rows, ((0, 0), (0, 128 - TOP))),
-        (w_query, w_expand, w_output),
+        jnp.pad(route_rows, ((0, 0), (0, 128 - TOP)), constant_values=-1),
+        (w_query, w_expand, w_output), upd, split,
     )
+    blk = ("z", "x")
+    grad_slots, later_gate, later_up, later_down = lax.optimization_barrier(
+        (grad_slots, w_shared_gate, w_shared_up, w_shared_down)
+    )
+    gate_w = lax.all_gather(later_gate, blk, axis=0, tiled=True)
+    up_w = lax.all_gather(later_up, blk, axis=0, tiled=True)
+    down_w = lax.all_gather(later_down, blk, axis=1, tiled=True)
     tokens_local = tokens.reshape(rows, features)
     grad_narrow = out_grad.reshape(rows, features)
     small_whole = small_all.reshape(features, -1)
@@ -1741,41 +1755,14 @@
     latent_keys = latents.reshape(seqs, length, KVR + NOPE)
     latent_rows = latents.reshape(all_rows, KVR + NOPE)
     expand_w = jnp.pad(expand_w, ((0, NOPE), (0, 0)))
-    tokens_group = tokens_group.reshape(group, features)
+    hidden_group = hidden_group.reshape(group, features)
     grad_group = grad_group.reshape(group, features)
-    route_line = route_line[:, :, :TOP]
-
-    member = jnp.any(
-        route_line[..., None] == jnp.arange(EXPERTS, dtype=jnp.int32), axis=2
-    )
-    earlier = (
-        jnp.arange(rows, dtype=jnp.int32)[None, :] < jnp.arange(rows, dtype=jnp.int32)[:, None]
-    ).astype(narrow)
-    rank = jnp.einsum(
-        "tq,zqe->zte", earlier, member.astype(narrow), preferred_element_type=wide
-    ).astype(jnp.int32)
-    here = EXPERTS // nz
-    rank = jnp.where(member, rank, -1)
-    rank_layer = lax.dynamic_slice_in_dim(rank, zi * here, here, 2)
-    experts = [(d * upd + a) // split for d in range(layer) for a in range(upd)]
-    chosen = jnp.stack([rank_layer[..., e] for e in experts], axis=-1)
-    picks = (
-        (chosen[..., None] == jnp.arange(SLOTS, dtype=jnp.int32))
-        .astype(narrow)
-        .reshape(nz, rows, layer * upd * SLOTS)
-    )
 
     def swap_layer(values):
-        return lax.all_to_all(values, LAYER, split_axis=1, concat_axis=1, tiled=True)
-
-    grad_line = grad_line.reshape(nz, rows, features)
-    grad_slots = swap_layer(
-        jnp.einsum("ztk,ztf->zkf", picks, grad_line, preferred_element_type=narrow).reshape(
-            nz, layer, upd, SLOTS, features
-        )
-    )
-
-    hidden_group = norm_rows(tokens_group.astype(wide), gain_attn)[0].astype(narrow)
+        return lax.all_to_all(values, LAYER, split_axis=0, concat_axis=0, tiled=True)
+
+    grad_slots = swap_layer(grad_slots)
+
     reach = nu * local_len
     cos_group, sin_group = rotary_tables(group_pos)
     query_lin = dot(hidden_group, query_w)
@@ -1785,20 +1772,18 @@
         query_lin, cos_group, sin_group, expanded, latent_keys, query_pos, keys_pos, seqs, heads
     )
     top = jnp.pad(jnp.max(stats[..., 0], axis=(0, 2))[None], ((0, 7), (0, 128 - heads)))
-    own_member = member[0]
     split_group = (seqs, ny, nc, local_len, features)
-    residual, gates, hidden_mid, hidden_mid_group, expert_slots, tops, gate_w = dispatch(
+    residual, gates, hidden_mid, hidden_mid_group, expert_slots, tops = dispatch(
         dot(attended, output_w, narrow).reshape(split_group),
-        tokens, gain_ffn[None], router_w, own_member.astype(wide), picks, top, upd,
-        (w_shared_gate,), ((0, False),),
+        tokens, gain_ffn[None], router_w, own_member, picks, top, upd,
+        (), (),
     )
     clip_value = clip_limit[0]
     clip_factor = clip_value / jnp.maximum(jnp.max(tops, axis=(0, 1))[0, :heads], clip_value)
     hidden_mid_group = hidden_mid_group.reshape(group, features)
 
-    returned, outputs, gated, lin_gate, lin_up, up_w, down_w = run_experts(
-        expert_slots, grad_slots, w_gate, w_up, w_down,
-        (w_shared_up, w_shared_down), ((0, False), (1, False)), split,
+    returned, outputs, gated, lin_gate, lin_up = run_experts(
+        expert_slots, grad_slots, w_gate, w_up, w_down, (), (), split
     )
 
     shared_gate = dot(hidden_mid_group, gate_w)
@@ -1811,23 +1796,32 @@
     mid_shared = dot_nt(shared_gate_grad, gate_w) + dot_nt(shared_up_grad, up_w)
 
     usual = ("x", "z")
-    shared_gate_wgrad = dot_tn(hidden_mid_group, shared_gate_grad, narrow)
-    shared_up_wgrad = dot_tn(hidden_mid_group, shared_up_grad, narrow)
+    def spread_sum(value, dim):
+        return lax.psum_scatter(value, blk, scatter_dimension=dim, tiled=True).astype(wide)
+
+    shared_gate_wgrad, shared_up_wgrad, shared_down_wgrad, returned = lax.optimization_barrier(
+        (
+            dot_tn(hidden_mid_group, shared_gate_grad, narrow),
+            dot_tn(hidden_mid_group, shared_up_grad, narrow),
+            dot_tn(shared_act, grad_group, narrow),
+            returned,
+        )
+    )
+    shared_up_wgrad = spread_sum(shared_up_wgrad, 0)
+    shared_down_wgrad = spread_sum(shared_down_wgrad, 1)
     (
-        residual_grad, attn_grad, logit_grad, ffn_gain_part, shared_sum,
-        shared_gate_wgrad, shared_up_wgrad,
+        residual_grad, attn_grad, logit_grad, ffn_gain_part, shared_sum, shared_gate_wgrad,
     ) = come_back(
         returned, mid_shared.astype(narrow).reshape(split_group),
         shared_partial.reshape(split_group), residual, gates,
         router_w, gain_ffn[None], out_grad, picks,
-        (shared_gate_wgrad, shared_up_wgrad), ((0, usual), (0, usual)),
+        (shared_gate_wgrad,), ((0, usual),),
     )
     attn_grad = attn_grad.reshape(group, features)
-    outputs, shared_act, attn_grad = lax.optimization_barrier((outputs, shared_act, attn_grad))
+    outputs, attn_grad = lax.optimization_barrier((outputs, attn_grad))
     outputs = swap_layer(outputs)
-    gate_wgrad, up_wgrad, down_wgrad = unit_grads(expert_slots, grad_slots, gated, lin_gate, lin_up)
-    shared_down_wgrad = dot_tn(shared_act, grad_group, narrow)
     attended_grad = dot_nt(attn_grad, output_w, narrow)
+    attended_grad, shared_up_wgrad = lax.optimization_barrier((attended_grad, shared_up_wgrad))
     output_wgrad = dot_tn(attended, attn_grad, narrow)
 
     query_lin_grad, expand_grad, rope_partial = attend_back(
@@ -1839,13 +1833,21 @@
         dot_nt(expand_grad, expand_w).reshape(seqs, length, KVR + NOPE)
         + jnp.pad(rope_partial, ((0, 0), (0, 0), (KVR, 0)))
     ).astype(narrow)
-    routed = jnp.einsum(
-        "ztk,zkf->ztf", picks, outputs.reshape(nz, layer * upd * SLOTS, features),
-        preferred_element_type=narrow,
-    )
+    latent_blocks = latent_partial.reshape(seqs, nc, ny, nx, nz, local_len, KVR + NOPE)
+    latent_blocks = ring_sum([latent_blocks[:, i] for i in range(nc)], "core").astype(narrow)
+    latent_blocks, gated, outputs = lax.optimization_barrier((latent_blocks, gated, outputs))
+    gated, shared_down_wgrad = lax.optimization_barrier((gated, shared_down_wgrad))
+    gate_wgrad, up_wgrad, down_wgrad = unit_grads(expert_slots, grad_slots, gated, lin_gate, lin_up)
+    latent_blocks = ring_sum([latent_blocks[:, i] for i in range(ny)], "y").astype(narrow)
+    hidden_blocks = hidden_partial.reshape(split_group)
+    hidden_blocks = ring_sum([hidden_blocks[:, :, i] for i in range(nc)], "core").astype(narrow)
+    hidden_sum = ring_sum([hidden_blocks[:, i] for i in range(ny)], "y").astype(narrow)
     query_wgrad = dot_tn(hidden_group, query_lin_grad, narrow)
     expand_wgrad = dot_tn(latent_rows, expand_grad, narrow)
     uly = yi * nc + ci
+    hidden_sum, gate_wgrad, up_wgrad, down_wgrad = lax.optimization_barrier(
+        (hidden_sum, gate_wgrad, up_wgrad, down_wgrad)
+    )
 
     def own_columns(values):
         return lax.dynamic_slice_in_dim(
@@ -1854,16 +1856,14 @@
 
     (
         tokens_grad, block_out, latent_wgrad, gain_sums, query_wgrad, expand_wgrad, output_wgrad,
-        shared_down_wgrad,
     ) = finish(
-        hidden_partial.reshape(seqs, ny, nc, local_len, features),
-        latent_partial.reshape(seqs, nc, ny, nx, nz, local_len, KVR + NOPE),
+        hidden_sum, latent_blocks,
         tokens, residual_grad, small_whole, own_columns(hidden_group), own_columns(hidden_mid_group),
         logit_grad, ffn_gain_part, gain_attn[None], gain_latent[None],
         latent_all, cos_local, sin_local, residual,
-        shared_sum, routed,
-        (query_wgrad, expand_wgrad[:KVR], output_wgrad, shared_down_wgrad),
-        ((0, usual), (0, ("z", "x")), (1, usual), (1, usual)),
+        shared_sum, picks, outputs,
+        (query_wgrad, expand_wgrad[:KVR], output_wgrad),
+        ((0, usual), (0, usual), (1, usual)),
     )
     width = KVR + RD
     small_wgrad = latent_wgrad.reshape(shard, -1)

time: 907 us -> 869 us (0.958)
  Pallas kernels: 726 us -> 653 us
  between operations: 2.73 us -> 15.8 us
  waiting for transfers between devices: 2.76 us -> 15.7 us
    pallas_call x1, Pallas kernels: 176 us -> 136 us  [finish(): pl.pallas_call(functools.partial(finish_kernel, modes=modes), out_shape=[...]
    pallas_call x1, Pallas kernels: 87.8 us -> 58.2 us  [run_experts(): pl.pallas_call(functools.partial(expert_kernel, split=split, plan=plan),...]
    reduce_scatter x0 -> x2, waiting for transfers between devices: none -> 14.2 us  [spread_sum(): lax.psum_scatter(value, blk, scatter_dimension=dim, tiled=True).astype(wide)]
    convert_element_type x3 -> x6, other arithmetic: 2.88 us -> 12.9 us  [the longest x2 3.78 us: spread_sum(): lax.psum_scatter(value, blk, scatter_dimension=dim, tiled=True).astype(wide)]
    unnamed x119 -> x112, local copies, waits for them, and re-layouts: 27.3 us -> 29.5 us
  transfers between devices with their start and end apart: 2 -> 11, of which waited for: 1 -> 1; matrix products, arithmetic and copies ran while one was open for 6% -> 13% of each run, Pallas kernels for 17% -> 43%
where the time goes in v3:
time: 869 us; the launch traced here: 861 us
  Pallas kernels  653 us (75%)
  matrix products  84.3 us (10%)
  local copies, waits for them, and re-layouts  53.1 us (6%)
  other arithmetic  25.9 us (3%)
  between operations  15.8 us (2%)
  waiting for transfers between devices  15.7 us (2%)
  starting transfers between devices  13.5 us (2%)
    pallas_call x1, Pallas kernels, start(): pl.pallas_call(functools.partial(start_kernel, units=units, split=split),...  146 us
    pallas_call x1, Pallas kernels, finish(): pl.pallas_call(functools.partial(finish_kernel, modes=modes), out_shape=[...  136 us
    pallas_call x1, Pallas kernels, come_back(): pl.pallas_call(functools.partial(return_kernel, modes=modes), out_shape=[...  125 us
    pallas_call x1, Pallas kernels, dispatch(): pl.pallas_call(functools.partial(dispatch_kernel, plan=plan), out_shape=[...  109 us
    pallas_call x1, Pallas kernels, run_experts(): pl.pallas_call(functools.partial(expert_kernel, split=split, plan=plan),...  58.2 us
    dot_general x6, matrix products, dot(): return jnp.dot(a, b, preferred_element_type=out)  32.6 us
    pallas_call x1, Pallas kernels, unit_grads(): pl.pallas_call(unit_grads_kernel, grid=(units, features // step), in_spec...  31.5 us
    unnamed x112, local copies, waits for them, and re-layouts  29.5 us
  transfers between devices with their start and end apart: 11, of which 1 were waited for; matrix products, arithmetic and copies ran while one was open for 13% of the time, Pallas kernels for 43%

profile of v3, /device:TPU:0, one launch (start us, length us, event | category | flops | bytes accessed | tf_op | source)
XLA Modules:
  0.0 860.8 jit_solution(5759919918129227816)
XLA Ops:
  10.1 1.0 pad_maximum_fusion
  12.0 1.0 copy-done.9
  13.1 1.0 copy-done.10
  14.1 1.0 copy-done.12
  17.0 146.1 %shard_map.305 = (f32[8,8,512]{2,1,0:T(8,128)S(1)}, bf16[8,4,64,640]{3,2,1,0:T(8,128)(2,1)S(1)}, bf16[2048,768]{1,0:T(8,128)(2,1)}, bf16[512,1024]{1,0:T(8,128)(...) custom-call(bf16[2,64,2048]{2,1,0:T(8,128)(2,1)S(1)} %copy-done.10, ...), custom_call_target="tpu_custom_call" | custom-call | flops 120000004096 | bytes 120000000 | tf_op jit(solution)/shard_map/pallas_call | solution.py:448
  163.1 1.5 copy-done.5
  164.5 1.4 copy-done.15
  165.9 1.4 copy-done.17
  169.7 4.6 all-to-all-start
  176.2 1.2 multiply_sine_fusion
  178.0 1.4 slice.81.router
  179.7 5.0 fusion.21.query
  184.7 8.2 fusion.8.keys
  193.6 17.8 %shard_map.306 = (bf16[512,1024]{1,0:T(8,128)(2,1)}, bf16[512,512]{1,0:T(8,128)(2,1)}, f32[2,4,256,2]{3,2,1,0:T(8,128)}) custom-call(f32[512,768]{1,0:T(8,128)} %fusion.21.query, f32[256,32]{1,0:T(8,128)} %get-tuple-element.193.cosine, f32[256,32]{1,0:T(8,128)} %get-tuple-element.192.sine, bf16[4096,1024]{1,0:T(8,128)(2,1)} %fusion.8.keys, ...), custom_call_target="tpu_custom_call" | custom-call | flops 16000000000 | bytes 16000000 | tf_op jit(solution)/shard_map/pallas_call | solution.py:573
  211.4 1.4 slice_reduce_fusion
  212.8 4.4 fusion.22
  217.3 108.8 %shard_map.307 = (f32[128,2048]{1,0:T(8,128)S(1)}, f32[128,64]{1,0:T(8,128)S(1)}, bf16[128,2048]{1,0:T(8,128)(2,1)}, bf16[2,2,2,64,2048]{4,3,2,1,0:T(8,128)(2,1)...) custom-call(bf16[2,2,2,64,2048]{4,3,2,1,0:T(8,128)(2,1)} %bitcast.144, ...), custom_call_target="tpu_custom_call" | custom-call | flops 80000000000 | bytes 80000000 | tf_op jit(solution)/shard_map/pallas_call | solution.py:1177
  326.0 1.4 copy-done.2
  327.4 1.0 copy-done.22
  329.0 2.5 copy.50
  332.2 2.9 copy.51
  335.7 1.9 constant_dynamic-slice_fusion.1
  338.9 58.2 %shard_map.308 = (bf16[8,4,2,16,2176]{4,3,2,1,0:T(8,128)(2,1)}, bf16[8,4,2,16,2048]{4,3,2,1,0:T(8,128)(2,1)}, bf16[2,512,1408]{2,1,0:T(8,128)(2,1)}, bf16[2,512,1408]{2,1,0:T(8,128)(2,1)}, bf16[2,512,1408]{2,1,0:T(8,128)(2,1)}) custom-call(bf16[8,4,2,16,2176]{4,3,2,1,0:T(8,128)(2,1)} %get-tuple-element.94.rows_in.rows, ...), custom_call_target="tpu_custom_call" | custom-call | flops 80000000000 | bytes 80000000 | tf_op jit(solution)/shard_map/pallas_call | solution.py:1575
  397.2 4.6 fusion.24
  401.8 5.2 fusion.23
  407.0 5.0 multiply_convert_fusion
  412.9 3.2 fusion.25
  416.1 3.3 fusion.33
  419.4 3.2 fusion.32
  422.6 1.8 copy-done.29
  424.4 3.0 copy.44.rest_0_
  427.5 5.4 fusion.27
  432.9 1.9 fusion.26
  434.8 3.4 add_convert_fusion.1
  438.2 125.2 %shard_map.309 = (f32[128,2048]{1,0:T(8,128)}, bf16[2,2,2,64,2048]{4,3,2,1,0:T(8,128)(2,1)}, bf16[128,64]{1,0:T(8,128)(2,1)}, f32[1,2048]{1,0:T(1,128)}, bf16[2,...) custom-call(bf16[8,4,2,16,2176]{4,3,2,1,0:T(8,128)(2,1)} %get-tuple-element.104.returned, ...), custom_call_target="tpu_custom_call" | custom-call | flops 99999997952 | bytes 100000000 | tf_op jit(solution)/shard_map/pallas_call | solution.py:1336
  563.5 4.8 all-to-all-start.1
  568.4 1.1 copy.54
  569.5 2.6 fusion.31.rest_2_
  572.2 2.1 fusion.28.grads
  574.3 1.9 convert_element_type.115
  576.2 28.8 %shard_map.310 = (bf16[512,768]{1,0:T(8,128)(2,1)}, bf16[4096,1024]{1,0:T(8,128)(2,1)}, f32[2,2048,128]{2,1,0:T(8,128)}) custom-call(bf16[512,1024]{1,0:T(8,128)(2,1)} %get-tuple-element.86.query, f32[256,32]{1,0:T(8,128)} %get-tuple-element.193.cosine, f32[256,32]{1,0:T(8,128)} %get-tuple-element.192.sine, bf16[4096,1024]{1,0:T(8,128)(2,1)} %fusion.8.keys, ...), custom_call_target="tpu_custom_call" | custom-call | flops 24999999488 | bytes 25000000 | tf_op jit(solution)/shard_map/pallas_call | solution.py:594
  605.0 4.1 fusion.29
  609.3 1.0 copy.70
  610.6 9.5 %fusion.6 = f32[4096,640]{1,0:T(8,128)} fusion(bf16[4096,1024]{1,0:T(8,128)(2,1)S(1)} %copy-done.44, bf16[512,1024]{1,0:T(8,128)(2,1)S(1)} %copy-done.21), kind=kOutput, calls=%fused_computation.18 | convolution fusion | flops 5368709120 | bytes 19922944 | tf_op jit(solution)/shard_map/dot_general | solution.py:39
  620.1 4.6 add_convert_fusion
  624.7 2.0 fusion.18
  626.7 1.8 copy.69
  630.0 1.6 fusion.4
  632.4 1.7 collective-permute-start.1
  634.1 8.5 fusion.1.rest_1_
  642.6 14.2 %reduce-scatter.5.cloned.1.call-done = bf16[704,256]{1,0:T(8,128)(2,1)} async-done(((bf16[704,2048]{1,0:T(8,128)(2,1)}), bf16[704,256]{1,0:T(8,128)(2,1)}) %reduce-scatter.5.cloned.1.call-update) | async-done | bytes 360464 | tf_op jit(solution)/shard_map/reduce_scatter | solution.py:1800
  656.8 1.9 convert_element_type.129
  658.7 4.8 fusion.30.rest_0_
  663.5 2.0 fusion.10.hidden_sum
  665.4 2.7 fusion
  668.1 1.2 slice_bitcast_fusion
  669.3 1.4 collective-permute-start.3
  670.7 31.5 %shard_map.311 = (f32[2,2048,1408]{2,1,0:T(8,128)}, f32[2,2048,1408]{2,1,0:T(8,128)}, f32[2,1408,2048]{2,1,0:T(8,128)}) custom-call(bf16[8,4,2,16,2176]{4,3,2,1,0:T(8,128)(2,1)} %get-tuple-element.94.rows_in.rows, bf16[8,4,2,16,2048]{4,3,2,1,0:T(8,128)(2,1)} %all-to-all-done.grads_in.grads, bf16[2,512,1408]{2,1,0:T(8,128)(2,1)} %get-tuple-element.119.gated, ...), custom_call_target="tpu_custom_call" | custom-call | flops 35000000512 | bytes 35000000 | tf_op jit(solution)/shard_map/pallas_call | solution.py:1627
  702.2 2.8 fusion.3.latent_partial
  705.1 136.2 %shard_map.312 = (bf16[2,64,2048]{2,1,0:T(8,128)(2,1)}, bf16[2,64,2048]{2,1,0:T(8,128)(2,1)}, f32[4,64,640]{2,1,0:T(8,128)}, f32[4,8,768]{2,1,0:T(8,128)}, f32[2...) custom-call(bf16[2,64,2048]{2,1,0:T(8,128)(2,1)} %fusion.10.hidden_sum, ...), custom_call_target="tpu_custom_call" | custom-call | flops 190000005120 | bytes 190000000 | tf_op jit(solution)/shard_map/pallas_call | solution.py:998
  841.3 1.4 slice_reduce_fusion.3
  844.8 1.0 slice.90
  846.5 2.2 copy.59
  848.7 1.9 copy.78
  (171 shorter events, 23.5 us)
Async XLA Ops:
  7.2 390.0 %all-gather.8.cloned.1.call-start = ((), (), s32[]{:S(2)}) async-start(), calls=%async_computation.6 | async-start | bytes 3244032 | tf_op jit(solution)/shard_map/all_gather | solution.py:1740
  11.8 151.3 %copy-start.6 = (f32[128,32]{1,0:T(8,128)}, f32[128,32]{1,0:T(8,128)S(1)}, u32[]{:S(2)}) copy-start(f32[128,32]{1,0:T(8,128)S(1)} %get-tuple-element.194.sine) | copy-start | bytes 49156
  11.8 151.3 %copy-start.7 = (f32[128,32]{1,0:T(8,128)}, f32[128,32]{1,0:T(8,128)S(1)}, u32[]{:S(2)}) copy-start(f32[128,32]{1,0:T(8,128)S(1)} %get-tuple-element.195.cosine) | copy-start | bytes 49156
  12.0 1.0 copy-start.9
  13.1 1.0 copy-start.10
  14.1 1.0 copy-start.12
  15.1 0.9 copy-start.13
  16.1 0.9 copy-start.14
  163.1 1.5 copy-start.5
  164.5 1.4 copy-start.15
  165.9 1.4 copy-start.17
  167.2 1.0 copy-start.19
  168.2 0.7 copy-start.24
  169.0 0.8 copy-start.25
  169.0 48.3 %copy-start.23 = (bf16[4,128,256]{2,1,0:T(8,128)(2,1)}, bf16[4,128,256]{2,1,0:T(8,128)(2,1)S(1)}, u32[]{:S(2)}) copy-start(bf16[4,128,256]{2,1,0:T(8,128)(2,1)S(1)} %get-tuple-element.93.picks) | copy-start | bytes 786436
  169.0 160.0 %copy-start = (bf16[2,2,2,64,2048]{4,3,2,1,0:T(8,128)(2,1)}, bf16[2,2,2,64,2048]{4,3,2,1,0:T(8,128)(2,1)S(1)}, u32[]{:S(2)}) copy-start(bf16[2,2,2,64,2048]{4,3,2,1,0:T(8,128)(2,1)S(1)} %get-tuple-element.82) | copy-start | bytes 6291460
  169.0 232.8 %all-gather.4.cloned.1.call-start = ((), (), s32[]{:S(2)}) async-start(), calls=%async_computation.4 | async-start | bytes 3244032 | tf_op jit(solution)/shard_map/all_gather | solution.py:1742
  169.7 169.2 %all-to-all-start = ((bf16[8,4,2,16,2048]{4,3,2,1,0:T(8,128)(2,1)}), bf16[8,4,2,16,2048]{4,3,2,1,0:T(8,128)(2,1)}, u32[]{:S(2)}, u32[]{:S(2)}) async-start(bf16[8,4,2,16,2048]{4,3,2,1,0:T(8,128)(2,1)} %get-tuple-element.96), calls=%async_computation | async-start | bytes 8388608 | tf_op jit(solution)/shard_map/all_to_all | solution.py:1762
  174.3 232.7 %all-gather.6.cloned.1.call-start = ((), (), s32[]{:S(2)}) async-start(), calls=%async_computation.5 | async-start | bytes 3244032 | tf_op jit(solution)/shard_map/all_gather | solution.py:1741
  175.1 399.2 %reduce-scatter.3.cloned.1.call-start = ((), (), s32[]{:S(2)}) async-start(), calls=%async_computation.7 | async-start | bytes 3244032 | tf_op jit(solution)/shard_map/reduce_scatter | solution.py:1800
  178.0 39.2 %copy-start.8 = (f32[8,1,256]{2,1,0:T(1,128)}, f32[8,1,256]{2,1,0:T(1,128)S(1)}, u32[]{:S(2)}) copy-start(f32[8,1,256]{2,1,0:T(1,128)S(1)} %get-tuple-element.191) | copy-start | bytes 24580
  178.0 6.6 slice-start
  179.4 37.8 %copy-start.4 = (bf16[2048,64]{1,0:T(8,128)(2,1)}, bf16[2048,64]{1,0:T(8,128)(2,1)S(1)}, u32[]{:S(2)}) copy-start(bf16[2048,64]{1,0:T(8,128)(2,1)S(1)} %slice.81.router) | copy-start | bytes 786436
  179.6 5.0 copy-start.20
  179.6 5.0 slice-start.1
  212.8 4.4 copy-start.11
  212.8 4.4 copy-start.26
  326.0 1.4 copy-start.2
  327.4 1.0 copy-start.22
  328.4 0.6 copy-start.27
  338.9 58.3 %copy-start.3 = (bf16[2,2,2,64,2048]{4,3,2,1,0:T(8,128)(2,1)S(1)}, bf16[2,2,2,64,2048]{4,3,2,1,0:T(8,128)(2,1)}, u32[]{:S(2)}) copy-start(bf16[2,2,2,64,2048]{4,3,2,1,0:T(8,128)(2,1)} %copy-done.2) | copy-start | bytes 6291460
  407.0 5.9 copy-start.16
  412.0 0.9 copy-start.42
  412.0 4.1 copy-start.45
  412.0 7.3 copy-start.35
  422.6 1.8 copy-start.29
  427.5 5.4 copy-start.30
  427.5 5.4 copy-start.36
  432.9 1.9 copy-start.40
  432.9 2.0 copy-start.46
  563.5 4.9 copy-start.34
  563.5 6.0 copy-start.41
  563.5 6.0 copy-start.43
  563.5 104.6 %all-to-all-start.1 = ((bf16[8,4,2,16,2048]{4,3,2,1,0:T(8,128)(2,1)}), bf16[8,4,2,16,2048]{4,3,2,1,0:T(8,128)(2,1)}, u32[]{:S(2)}, u32[]{:S(2)}) async-start(bf16[8,4,2,16,2048]{4,3,2,1,0:T(8,128)(2,1)} %get-tuple-element.116), calls=%async_computation.2 | async-start | bytes 8388608 | tf_op jit(solution)/shard_map/all_to_all | solution.py:1762
  568.3 88.5 %reduce-scatter.5.cloned.1.call-start = ((), (), s32[]{:S(2)}) async-start(), calls=%async_computation.8 | async-start | bytes 3244032 | tf_op jit(solution)/shard_map/reduce_scatter | solution.py:1800
  569.5 2.6 copy-start.18
  605.0 5.6 copy-start.44
  609.1 1.5 copy-start.21
  610.3 18.7 %collective-permute-start = (bf16[2,2,64,2048]{3,2,0,1:T(8,128)(2,1)}, bf16[2,2,64,2048]{3,2,0,1:T(8,128)(2,1)S(1)}, u32[]{:S(2)}, u32[]{:S(2)}) collective-permute-start(bf16[2,2,64,2048]{3,2,0,1:T(8,128)(2,1)} %bitcast.97), channel_id=1, source_target_pairs={{0,1},{1,0},{2,3},{3,2},{4,5},{5,4},{6,7},{7,6},{8,9},{9,8},{10,11... | collective-permute-start | bytes 3145736 | tf_op jit(solution)/shard_map/ppermute | solution.py:79
  610.6 9.5 %copy-start.31 = (f32[2,2048,128]{2,1,0:T(8,128)S(1)}, f32[2,2048,128]{2,1,0:T(8,128)}, u32[]{:S(2)}) copy-start(f32[2,2048,128]{2,1,0:T(8,128)} %get-tuple-element.114) | copy-start | bytes 6291460
  626.7 7.4 slice-start.2
  626.7 7.4 slice-start.3
  628.6 36.9 %collective-permute-start.2 = (bf16[2,2,2,4,64,640]{5,4,3,2,0,1:T(8,128)(2,1)}, bf16[2,2,2,4,64,640]{5,4,3,2,0,1:T(8,128)(2,1)}, u32[]{:S(2)}, u32[]{:S(2)}) collective-permute-start(bf16[2,2,2,4,64,640]{5,4,3,2,0,1:T(8,128)(2,1)} %bitcast.96), channel_id=1, source_target_pairs={{0,1},{1,0},{2,3},{3,2},{4,5},{5,4},{6,7},{7,6},{8,9},{9,8},{10,11... | collective-permute-start | bytes 7864328 | tf_op jit(solution)/shard_map/ppermute | solution.py:79
  629.0 1.0 copy-start.32
  632.4 26.3 %copy-start.1 = (bf16[2,2,2,64,2048]{4,3,2,1,0:T(8,128)(2,1)S(1)}, bf16[2,2,2,64,2048]{4,3,2,1,0:T(8,128)(2,1)}, u32[]{:S(2)}) copy-start(bf16[2,2,2,64,2048]{4,3,2,1,0:T(8,128)(2,1)} %copy-done) | copy-start | bytes 6291460
  632.4 31.1 %collective-permute-start.1 = (bf16[2,64,2048]{2,1,0:T(8,128)(2,1)}, bf16[2,64,2048]{2,1,0:T(8,128)(2,1)}, u32[]{:S(2)}, u32[]{:S(2)}) collective-permute-start(bf16[2,64,2048]{2,1,0:T(8,128)(2,1)} %slice_bitcast_fusion.2), channel_id=1, source_target_pairs={{0,2},{2,0},{1,3},{3,1},{4,6},{6,4},{5,7},{7,5},{8,10},{10,8},{9,1... | collective-permute-start | bytes 1572872 | tf_op jit(solution)/shard_map/ppermute | solution.py:79
  658.7 6.7 copy-start.28
  669.3 32.9 %collective-permute-start.3 = (bf16[2,2,4,64,640]{4,3,2,1,0:T(8,128)(2,1)}, bf16[2,2,4,64,640]{4,3,2,1,0:T(8,128)(2,1)}, u32[]{:S(2)}, u32[]{:S(2)}) collective-permute-start(bf16[2,2,4,64,640]{4,3,2,1,0:T(8,128)(2,1)} %slice_bitcast_fusion), channel_id=1, source_target_pairs={{0,2},{2,0},{1,3},{3,1},{4,6},{6,4},{5,7},{7,5},{8,10},{10,8},{9,1... | collective-permute-start | bytes 3932168 | tf_op jit(solution)/shard_map/ppermute | solution.py:79
  841.3 9.3 %copy-start.38 = (bf16[2,64,2048]{2,1,0:T(8,128)(2,1)S(1)}, bf16[2,64,2048]{2,1,0:T(8,128)(2,1)}, u32[]{:S(2)}) copy-start(bf16[2,64,2048]{2,1,0:T(8,128)(2,1)} %get-tuple-element.250) | copy-start | bytes 1572868
  841.3 10.1 %copy-start.33 = (f32[256,768]{1,0:T(8,128)S(1)}, f32[256,768]{1,0:T(8,128)}, u32[]{:S(2)}) copy-start(f32[256,768]{1,0:T(8,128)} %get-tuple-element.252) | copy-start | bytes 2359300
  845.8 6.5 copy-start.39
  846.5 6.4 copy-start.37
Sparse Core Ops, SparseCore 0:
  169.1 87.8 all-gather.7
  259.0 77.9 all-gather.3
  339.0 57.8 all-gather.5
  422.7 90.3 reduce-scatter.2
  574.4 82.3 reduce-scatter.4

commit v4 on v3

--- a/solution.py
+++ b/solution.py
@@ -404,15 +404,15 @@
     first = main()
     next(first)
     others = [
+        slots_chain(),
         array_chain(w_query, query_out, rows_of(w_query.shape[0]), False),
-        array_chain(w_expand, expand_out, rows_of(w_expand.shape[0]), True),
+        array_chain(w_expand, expand_out, rows_of(w_expand.shape[0]), False),
         array_chain(w_output, output_out, columns_of(w_output.shape[1]), False),
-        slots_chain(),
         group_chain(grads, grads_out),
     ]
     for _ in range(HEAD_START):
         next(first)
-    weave(first, others, 2)
+    weave(first, others, 3)
     wires.drain()
     for copy in used:
         if id(copy) not in waited:
@@ -1799,9 +1799,9 @@
     def spread_sum(value, dim):
         return lax.psum_scatter(value, blk, scatter_dimension=dim, tiled=True).astype(wide)
 
-    shared_gate_wgrad, shared_up_wgrad, shared_down_wgrad, returned = lax.optimization_barrier(
+    shared_gate_wgrad = dot_tn(hidden_mid_group, shared_gate_grad, narrow)
+    shared_up_wgrad, shared_down_wgrad, returned = lax.optimization_barrier(
         (
-            dot_tn(hidden_mid_group, shared_gate_grad, narrow),
             dot_tn(hidden_mid_group, shared_up_grad, narrow),
             dot_tn(shared_act, grad_group, narrow),
             returned,
@@ -1835,7 +1835,9 @@
     ).astype(narrow)
     latent_blocks = latent_partial.reshape(seqs, nc, ny, nx, nz, local_len, KVR + NOPE)
     latent_blocks = ring_sum([latent_blocks[:, i] for i in range(nc)], "core").astype(narrow)
-    latent_blocks, gated, outputs = lax.optimization_barrier((latent_blocks, gated, outputs))
+    latent_blocks, gated, outputs, late_hidden, late_mid = lax.optimization_barrier(
+        (latent_blocks, gated, outputs, hidden_group, hidden_mid_group)
+    )
     gated, shared_down_wgrad = lax.optimization_barrier((gated, shared_down_wgrad))
     gate_wgrad, up_wgrad, down_wgrad = unit_grads(expert_slots, grad_slots, gated, lin_gate, lin_up)
     latent_blocks = ring_sum([latent_blocks[:, i] for i in range(ny)], "y").astype(narrow)
@@ -1858,7 +1860,7 @@
         tokens_grad, block_out, latent_wgrad, gain_sums, query_wgrad, expand_wgrad, output_wgrad,
     ) = finish(
         hidden_sum, latent_blocks,
-        tokens, residual_grad, small_whole, own_columns(hidden_group), own_columns(hidden_mid_group),
+        tokens, residual_grad, small_whole, own_columns(late_hidden), own_columns(late_mid),
         logit_grad, ffn_gain_part, gain_attn[None], gain_latent[None],
         latent_all, cos_local, sin_local, residual,
         shared_sum, picks, outputs,

time: 869 us -> 857 us (0.986)
  Pallas kernels: 653 us -> 639 us
    pallas_call x1, Pallas kernels: 146 us -> 133 us  [start(): pl.pallas_call(functools.partial(start_kernel, units=units, split=split),...]
    unnamed x112 -> x104, local copies, waits for them, and re-layouts: 29.5 us -> 27.5 us
  transfers between devices with their start and end apart: 11 -> 11, of which waited for: 1 -> 1; matrix products, arithmetic and copies ran while one was open for 13% -> 13% of each run, Pallas kernels for 43% -> 44%
where the time goes in v4:
time: 857 us; the launch traced here: 849 us
  Pallas kernels  639 us (75%)
  matrix products  86.5 us (10%)
  local copies, waits for them, and re-layouts  51.6 us (6%)
  other arithmetic  25 us (3%)
  waiting for transfers between devices  17.5 us (2%)
  between operations  15.7 us (2%)
  starting transfers between devices  13.4 us (2%)
    pallas_call x1, Pallas kernels, finish(): pl.pallas_call(functools.partial(finish_kernel, modes=modes), out_shape=[...  136 us
    pallas_call x1, Pallas kernels, start(): pl.pallas_call(functools.partial(start_kernel, units=units, split=split),...  133 us
    pallas_call x1, Pallas kernels, come_back(): pl.pallas_call(functools.partial(return_kernel, modes=modes), out_shape=[...  127 us
    pallas_call x1, Pallas kernels, dispatch(): pl.pallas_call(functools.partial(dispatch_kernel, plan=plan), out_shape=[...  108 us
    pallas_call x1, Pallas kernels, run_experts(): pl.pallas_call(functools.partial(expert_kernel, split=split, plan=plan),...  57.4 us
    dot_general x6, matrix products, dot(): return jnp.dot(a, b, preferred_element_type=out)  33.3 us
    pallas_call x1, Pallas kernels, unit_grads(): pl.pallas_call(unit_grads_kernel, grid=(units, features // step), in_spec...  31.5 us
    pallas_call x1, Pallas kernels, attend_back(): pl.pallas_call(functools.partial(attend_back_kernel, scale=(NOPE + RD) **...  28.8 us
  transfers between devices with their start and end apart: 11, of which 1 were waited for; matrix products, arithmetic and copies ran while one was open for 13% of the time, Pallas kernels for 44%

profile of v4, /device:TPU:0, one launch (start us, length us, event | category | flops | bytes accessed | tf_op | source)
XLA Modules:
  0.0 849.1 jit_solution(16210873423094361287)
XLA Ops:
  10.1 1.0 pad_maximum_fusion
  12.0 1.0 copy-done.8
  13.1 1.0 copy-done.9
  14.1 1.0 copy-done.11
  15.1 0.9 copy-done.12
  17.0 132.8 %shard_map.305 = (f32[8,8,512]{2,1,0:T(8,128)S(1)}, bf16[8,4,64,640]{3,2,1,0:T(8,128)(2,1)S(1)}, bf16[2048,768]{1,0:T(8,128)(2,1)}, bf16[512,1024]{1,0:T(8,128)(...) custom-call(bf16[2,64,2048]{2,1,0:T(8,128)(2,1)S(1)} %copy-done.9, ...), custom_call_target="tpu_custom_call" | custom-call | flops 120000004096 | bytes 120000000 | tf_op jit(solution)/shard_map/pallas_call | solution.py:448
  149.8 1.5 copy-done.4
  151.4 1.3 copy-done.14
  152.7 1.4 copy-done.16
  154.0 1.0 copy-done.18
  156.5 4.6 all-to-all-start
  162.9 1.2 multiply_sine_fusion
  164.8 1.4 slice.81.router
  166.4 5.0 fusion.21.query
  171.4 8.2 fusion.8.keys
  180.3 17.8 %shard_map.306 = (bf16[512,1024]{1,0:T(8,128)(2,1)}, bf16[512,512]{1,0:T(8,128)(2,1)}, f32[2,4,256,2]{3,2,1,0:T(8,128)}) custom-call(f32[512,768]{1,0:T(8,128)} %fusion.21.query, f32[256,32]{1,0:T(8,128)} %get-tuple-element.195.cosine, f32[256,32]{1,0:T(8,128)} %get-tuple-element.194.sine, bf16[4096,1024]{1,0:T(8,128)(2,1)} %fusion.8.keys, ...), custom_call_target="tpu_custom_call" | custom-call | flops 16000000000 | bytes 16000000 | tf_op jit(solution)/shard_map/pallas_call | solution.py:573
  198.1 1.4 slice_reduce_fusion
  199.6 4.4 fusion.22
  204.0 108.1 %shard_map.307 = (f32[128,2048]{1,0:T(8,128)S(1)}, f32[128,64]{1,0:T(8,128)S(1)}, bf16[128,2048]{1,0:T(8,128)(2,1)}, bf16[2,2,2,64,2048]{4,3,2,1,0:T(8,128)(2,1)...) custom-call(bf16[2,2,2,64,2048]{4,3,2,1,0:T(8,128)(2,1)} %bitcast.144, ...), custom_call_target="tpu_custom_call" | custom-call | flops 80000000000 | bytes 80000000 | tf_op jit(solution)/shard_map/pallas_call | solution.py:1177
  312.1 1.0 copy-done.21
  315.5 57.4 %shard_map.308 = (bf16[8,4,2,16,2176]{4,3,2,1,0:T(8,128)(2,1)}, bf16[8,4,2,16,2048]{4,3,2,1,0:T(8,128)(2,1)}, bf16[2,512,1408]{2,1,0:T(8,128)(2,1)}, bf16[2,512,1408]{2,1,0:T(8,128)(2,1)}, bf16[2,512,1408]{2,1,0:T(8,128)(2,1)}) custom-call(bf16[8,4,2,16,2176]{4,3,2,1,0:T(8,128)(2,1)} %get-tuple-element.95.rows_in.rows, ...), custom_call_target="tpu_custom_call" | custom-call | flops 80000000000 | bytes 80000000 | tf_op jit(solution)/shard_map/pallas_call | solution.py:1575
  372.9 5.4 fusion.23
  378.3 4.6 fusion.24
  382.9 6.0 multiply_convert_fusion
  389.7 3.2 fusion.25
  392.9 4.3 fusion.33
  397.2 3.5 fusion.28.rest_0_
  400.7 1.1 copy-done.39
  401.8 5.1 fusion.27
  406.9 2.1 fusion.26
  409.0 3.3 add_convert_fusion.1
  412.3 126.8 %shard_map.309 = (f32[128,2048]{1,0:T(8,128)}, bf16[2,2,2,64,2048]{4,3,2,1,0:T(8,128)(2,1)}, bf16[128,64]{1,0:T(8,128)(2,1)}, f32[1,2048]{1,0:T(1,128)}, bf16[2,...) custom-call(bf16[8,4,2,16,2176]{4,3,2,1,0:T(8,128)(2,1)} %get-tuple-element.105.returned, ...), custom_call_target="tpu_custom_call" | custom-call | flops 99999997952 | bytes 100000000 | tf_op jit(solution)/shard_map/pallas_call | solution.py:1336
  539.2 4.8 all-to-all-start.1
  544.1 1.1 copy.54
  545.2 2.6 fusion.32.rest_2_
  547.9 2.1 fusion.29.grads
  550.0 1.9 convert_element_type.115
  551.9 28.8 %shard_map.310 = (bf16[512,768]{1,0:T(8,128)(2,1)}, bf16[4096,1024]{1,0:T(8,128)(2,1)}, f32[2,2048,128]{2,1,0:T(8,128)}) custom-call(bf16[512,1024]{1,0:T(8,128)(2,1)} %get-tuple-element.87.query, f32[256,32]{1,0:T(8,128)} %get-tuple-element.195.cosine, f32[256,32]{1,0:T(8,128)} %get-tuple-element.194.sine, bf16[4096,1024]{1,0:T(8,128)(2,1)} %fusion.8.keys, ...), custom_call_target="tpu_custom_call" | custom-call | flops 24999999488 | bytes 25000000 | tf_op jit(solution)/shard_map/pallas_call | solution.py:594
  580.7 4.1 fusion.30
  585.0 1.0 copy.71
  586.4 9.4 %fusion.6 = f32[4096,640]{1,0:T(8,128)} fusion(bf16[4096,1024]{1,0:T(8,128)(2,1)S(1)} %copy-done.41, bf16[512,1024]{1,0:T(8,128)(2,1)S(1)} %copy-done.20), kind=kOutput, calls=%fused_computation.18 | convolution fusion | flops 5368709120 | bytes 19922944 | tf_op jit(solution)/shard_map/dot_general | solution.py:39
  595.8 4.6 add_convert_fusion
  600.5 2.0 fusion.18
  602.5 1.8 copy.70
  605.1 1.0 copy-done.27
  606.9 1.7 collective-permute-start.1
  608.6 8.5 fusion.1.rest_1_
  617.1 16.0 %reduce-scatter.5.cloned.1.call-done = bf16[704,256]{1,0:T(8,128)(2,1)} async-done(((bf16[704,2048]{1,0:T(8,128)(2,1)}), bf16[704,256]{1,0:T(8,128)(2,1)}) %reduce-scatter.5.cloned.1.call-update) | async-done | bytes 360464 | tf_op jit(solution)/shard_map/reduce_scatter | solution.py:1800
  633.1 1.9 convert_element_type.129
  635.0 4.7 fusion.31.rest_0_
  640.7 4.2 fusion
  644.9 2.6 slice_bitcast_fusion
  647.5 1.4 collective-permute-start.3
  648.9 31.5 %shard_map.311 = (f32[2,2048,1408]{2,1,0:T(8,128)}, f32[2,2048,1408]{2,1,0:T(8,128)}, f32[2,1408,2048]{2,1,0:T(8,128)}) custom-call(bf16[8,4,2,16,2176]{4,3,2,1,0:T(8,128)(2,1)} %get-tuple-element.95.rows_in.rows, bf16[8,4,2,16,2048]{4,3,2,1,0:T(8,128)(2,1)} %all-to-all-done.grads_in.grads, bf16[2,512,1408]{2,1,0:T(8,128)(2,1)} %get-tuple-element.119.gated, ...), custom_call_target="tpu_custom_call" | custom-call | flops 35000000512 | bytes 35000000 | tf_op jit(solution)/shard_map/pallas_call | solution.py:1627
  680.4 2.5 copy.50
  682.9 4.1 copy.51
  687.0 1.9 constant_dynamic-slice_fusion.1
  688.8 1.9 constant_dynamic-slice_fusion
  690.7 2.8 fusion.3.latent_partial
  693.5 136.2 %shard_map.312 = (bf16[2,64,2048]{2,1,0:T(8,128)(2,1)}, bf16[2,64,2048]{2,1,0:T(8,128)(2,1)}, f32[4,64,640]{2,1,0:T(8,128)}, f32[4,8,768]{2,1,0:T(8,128)}, f32[2...) custom-call(bf16[2,64,2048]{2,1,0:T(8,128)(2,1)} %fusion.10.hidden_sum, ...), custom_call_target="tpu_custom_call" | custom-call | flops 190000005120 | bytes 190000000 | tf_op jit(solution)/shard_map/pallas_call | solution.py:998
  829.7 1.4 slice_reduce_fusion.3
  833.2 1.0 slice.90
  834.9 2.2 copy.60
  837.1 1.9 copy.79
  (162 shorter events, 20.9 us)
Async XLA Ops:
  7.2 365.7 %all-gather.4.cloned.1.call-start = ((), (), s32[]{:S(2)}) async-start(), calls=%async_computation.4 | async-start | bytes 3244032 | tf_op jit(solution)/shard_map/all_gather | solution.py:1742
  11.8 138.0 %copy-start.5 = (f32[128,32]{1,0:T(8,128)}, f32[128,32]{1,0:T(8,128)S(1)}, u32[]{:S(2)}) copy-start(f32[128,32]{1,0:T(8,128)S(1)} %get-tuple-element.196.sine) | copy-start | bytes 49156
  11.8 138.0 %copy-start.6 = (f32[128,32]{1,0:T(8,128)}, f32[128,32]{1,0:T(8,128)S(1)}, u32[]{:S(2)}) copy-start(f32[128,32]{1,0:T(8,128)S(1)} %get-tuple-element.197.cosine) | copy-start | bytes 49156
  12.0 1.0 copy-start.8
  13.1 1.0 copy-start.9
  14.1 1.0 copy-start.11
  15.1 0.9 copy-start.12
  16.1 0.9 copy-start.13
  149.8 1.5 copy-start.4
  151.4 1.3 copy-start.14
  152.7 1.4 copy-start.16
  154.0 1.0 copy-start.18
  155.0 0.7 copy-start.23
  155.7 10.6 %copy-start = (bf16[2,2,2,64,2048]{4,3,2,1,0:T(8,128)(2,1)}, bf16[2,2,2,64,2048]{4,3,2,1,0:T(8,128)(2,1)S(1)}, u32[]{:S(2)}) copy-start(bf16[2,2,2,64,2048]{4,3,2,1,0:T(8,128)(2,1)S(1)} %get-tuple-element.83) | copy-start | bytes 6291460
  155.7 48.2 %copy-start.22 = (bf16[4,128,256]{2,1,0:T(8,128)(2,1)}, bf16[4,128,256]{2,1,0:T(8,128)(2,1)S(1)}, u32[]{:S(2)}) copy-start(bf16[4,128,256]{2,1,0:T(8,128)(2,1)S(1)} %get-tuple-element.94.picks) | copy-start | bytes 786436
  155.8 222.5 %all-gather.8.cloned.1.call-start = ((), (), s32[]{:S(2)}) async-start(), calls=%async_computation.6 | async-start | bytes 3244032 | tf_op jit(solution)/shard_map/all_gather | solution.py:1741
  156.5 159.0 %all-to-all-start = ((bf16[8,4,2,16,2048]{4,3,2,1,0:T(8,128)(2,1)}), bf16[8,4,2,16,2048]{4,3,2,1,0:T(8,128)(2,1)}, u32[]{:S(2)}, u32[]{:S(2)}) async-start(bf16[8,4,2,16,2048]{4,3,2,1,0:T(8,128)(2,1)} %get-tuple-element.97), calls=%async_computation | async-start | bytes 8388608 | tf_op jit(solution)/shard_map/all_to_all | solution.py:1762
  161.1 221.8 %all-gather.6.cloned.1.call-start = ((), (), s32[]{:S(2)}) async-start(), calls=%async_computation.5 | async-start | bytes 3244032 | tf_op jit(solution)/shard_map/all_gather | solution.py:1740
  161.8 388.2 %reduce-scatter.3.cloned.1.call-start = ((), (), s32[]{:S(2)}) async-start(), calls=%async_computation.7 | async-start | bytes 3244032 | tf_op jit(solution)/shard_map/reduce_scatter | solution.py:1800
  164.8 39.2 %copy-start.7 = (f32[8,1,256]{2,1,0:T(1,128)}, f32[8,1,256]{2,1,0:T(1,128)S(1)}, u32[]{:S(2)}) copy-start(f32[8,1,256]{2,1,0:T(1,128)S(1)} %get-tuple-element.193) | copy-start | bytes 24580
  164.8 6.6 slice-start
  166.2 37.8 %copy-start.3 = (bf16[2048,64]{1,0:T(8,128)(2,1)}, bf16[2048,64]{1,0:T(8,128)(2,1)S(1)}, u32[]{:S(2)}) copy-start(bf16[2048,64]{1,0:T(8,128)(2,1)S(1)} %slice.81.router) | copy-start | bytes 786436
  166.4 5.0 copy-start.19
  166.4 5.0 slice-start.1
  199.6 4.4 copy-start.10
  312.1 1.0 copy-start.21
  313.1 0.6 copy-start.24
  313.7 83.5 %copy-start.2 = (bf16[2,2,2,64,2048]{4,3,2,1,0:T(8,128)(2,1)}, bf16[2,2,2,64,2048]{4,3,2,1,0:T(8,128)(2,1)S(1)}, u32[]{:S(2)}) copy-start(bf16[2,2,2,64,2048]{4,3,2,1,0:T(8,128)(2,1)S(1)} %get-tuple-element.99) | copy-start | bytes 6291460
  382.8 6.8 copy-start.15
  388.8 0.9 copy-start.38
  400.7 1.1 copy-start.39
  401.8 5.1 copy-start.29
  406.9 2.1 copy-start.36
  406.9 2.1 copy-start.42
  539.2 4.9 copy-start.32
  539.2 6.0 copy-start.37
  539.2 6.0 copy-start.40
  539.2 105.7 %all-to-all-start.1 = ((bf16[8,4,2,16,2048]{4,3,2,1,0:T(8,128)(2,1)}), bf16[8,4,2,16,2048]{4,3,2,1,0:T(8,128)(2,1)}, u32[]{:S(2)}, u32[]{:S(2)}) async-start(bf16[8,4,2,16,2048]{4,3,2,1,0:T(8,128)(2,1)} %get-tuple-element.116), calls=%async_computation.2 | async-start | bytes 8388608 | tf_op jit(solution)/shard_map/all_to_all | solution.py:1762
  544.1 89.0 %reduce-scatter.5.cloned.1.call-start = ((), (), s32[]{:S(2)}) async-start(), calls=%async_computation.8 | async-start | bytes 3244032 | tf_op jit(solution)/shard_map/reduce_scatter | solution.py:1800
  545.2 2.6 copy-start.17
  580.7 5.7 copy-start.41
  584.8 1.6 copy-start.20
  586.0 18.6 %collective-permute-start = (bf16[2,2,64,2048]{3,2,0,1:T(8,128)(2,1)}, bf16[2,2,64,2048]{3,2,0,1:T(8,128)(2,1)S(1)}, u32[]{:S(2)}, u32[]{:S(2)}) collective-permute-start(bf16[2,2,64,2048]{3,2,0,1:T(8,128)(2,1)} %bitcast.97), channel_id=1, source_target_pairs={{0,1},{1,0},{2,3},{3,2},{4,5},{5,4},{6,7},{7,6},{8,9},{9,8},{10,11... | collective-permute-start | bytes 3145736 | tf_op jit(solution)/shard_map/ppermute | solution.py:79
  586.4 9.4 %copy-start.30 = (f32[2,2048,128]{2,1,0:T(8,128)S(1)}, f32[2,2048,128]{2,1,0:T(8,128)}, u32[]{:S(2)}) copy-start(f32[2,2048,128]{2,1,0:T(8,128)} %get-tuple-element.114) | copy-start | bytes 6291460
  602.5 6.1 slice-start.2
  602.5 6.1 slice-start.3
  604.3 36.4 %collective-permute-start.2 = (bf16[2,2,2,4,64,640]{5,4,3,2,0,1:T(8,128)(2,1)}, bf16[2,2,2,4,64,640]{5,4,3,2,0,1:T(8,128)(2,1)}, u32[]{:S(2)}, u32[]{:S(2)}) collective-permute-start(bf16[2,2,2,4,64,640]{5,4,3,2,0,1:T(8,128)(2,1)} %bitcast.96), channel_id=1, source_target_pairs={{0,1},{1,0},{2,3},{3,2},{4,5},{5,4},{6,7},{7,6},{8,9},{9,8},{10,11... | collective-permute-start | bytes 7864328 | tf_op jit(solution)/shard_map/ppermute | solution.py:79
  605.0 1.0 copy-start.27
  606.9 28.1 %copy-start.1 = (bf16[2,2,2,64,2048]{4,3,2,1,0:T(8,128)(2,1)S(1)}, bf16[2,2,2,64,2048]{4,3,2,1,0:T(8,128)(2,1)}, u32[]{:S(2)}) copy-start(bf16[2,2,2,64,2048]{4,3,2,1,0:T(8,128)(2,1)} %copy-done) | copy-start | bytes 6291460
  606.9 32.9 %collective-permute-start.1 = (bf16[2,64,2048]{2,1,0:T(8,128)(2,1)}, bf16[2,64,2048]{2,1,0:T(8,128)(2,1)S(1)}, u32[]{:S(2)}, u32[]{:S(2)}) collective-permute-start(bf16[2,64,2048]{2,1,0:T(8,128)(2,1)} %slice_bitcast_fusion.2), channel_id=1, source_target_pairs={{0,2},{2,0},{1,3},{3,1},{4,6},{6,4},{5,7},{7,5},{8,10},{10,8},{9,1... | collective-permute-start | bytes 1572872 | tf_op jit(solution)/shard_map/ppermute | solution.py:79
  635.0 4.8 copy-start.28
  635.0 5.7 copy-start.25
  647.5 43.2 %collective-permute-start.3 = (bf16[2,2,4,64,640]{4,3,2,1,0:T(8,128)(2,1)}, bf16[2,2,4,64,640]{4,3,2,1,0:T(8,128)(2,1)}, u32[]{:S(2)}, u32[]{:S(2)}) collective-permute-start(bf16[2,2,4,64,640]{4,3,2,1,0:T(8,128)(2,1)} %slice_bitcast_fusion), channel_id=1, source_target_pairs={{0,2},{2,0},{1,3},{3,1},{4,6},{6,4},{5,7},{7,5},{8,10},{10,8},{9,1... | collective-permute-start | bytes 3932168 | tf_op jit(solution)/shard_map/ppermute | solution.py:79
  682.9 7.8 copy-start.26
  829.6 9.3 %copy-start.34 = (bf16[2,64,2048]{2,1,0:T(8,128)(2,1)S(1)}, bf16[2,64,2048]{2,1,0:T(8,128)(2,1)}, u32[]{:S(2)}) copy-start(bf16[2,64,2048]{2,1,0:T(8,128)(2,1)} %get-tuple-element.252) | copy-start | bytes 1572868
  829.6 10.1 %copy-start.31 = (f32[256,768]{1,0:T(8,128)S(1)}, f32[256,768]{1,0:T(8,128)}, u32[]{:S(2)}) copy-start(f32[256,768]{1,0:T(8,128)} %get-tuple-element.254) | copy-start | bytes 2359300
  834.2 6.5 copy-start.35
  834.9 6.4 copy-start.33
Sparse Core Ops, SparseCore 0:
  155.9 88.4 all-gather.3
  246.4 76.4 all-gather.7
  324.9 57.8 all-gather.5
  400.8 95.6 reduce-scatter.2
  550.1 82.9 reduce-scatter.4

commit v5 on v4

--- a/solution.py
+++ b/solution.py
@@ -1830,9 +1830,9 @@
     )
     hidden_partial = dot_nt(query_lin_grad, query_w, narrow)
     latent_partial = (
-        dot_nt(expand_grad, expand_w).reshape(seqs, length, KVR + NOPE)
-        + jnp.pad(rope_partial, ((0, 0), (0, 0), (KVR, 0)))
-    ).astype(narrow)
+        dot_nt(expand_grad, expand_w, narrow).reshape(seqs, length, KVR + NOPE)
+        + jnp.pad(rope_partial.astype(narrow), ((0, 0), (0, 0), (KVR, 0)))
+    )
     latent_blocks = latent_partial.reshape(seqs, nc, ny, nx, nz, local_len, KVR + NOPE)
     latent_blocks = ring_sum([latent_blocks[:, i] for i in range(nc)], "core").astype(narrow)
     latent_blocks, gated, outputs, late_hidden, late_mid = lax.optimization_barrier(

time: 857 us -> 857 us (level)
  transfers between devices with their start and end apart: 11 -> 11, of which waited for: 1 -> 2; matrix products, arithmetic and copies ran while one was open for 13% -> 12% of each run, Pallas kernels for 44% -> 44%
where the time goes in v5:
time: 857 us; the launch traced here: 849 us
  Pallas kernels  639 us (75%)
  matrix products  84.2 us (10%)
  local copies, waits for them, and re-layouts  53.3 us (6%)
  waiting for transfers between devices  21.9 us (3%)
  other arithmetic  21.2 us (2%)
  between operations  15.7 us (2%)
  starting transfers between devices  13.5 us (2%)
    pallas_call x1, Pallas kernels, finish(): pl.pallas_call(functools.partial(finish_kernel, modes=modes), out_shape=[...  136 us
    pallas_call x1, Pallas kernels, start(): pl.pallas_call(functools.partial(start_kernel, units=units, split=split),...  133 us
    pallas_call x1, Pallas kernels, come_back(): pl.pallas_call(functools.partial(return_kernel, modes=modes), out_shape=[...  127 us
    pallas_call x1, Pallas kernels, dispatch(): pl.pallas_call(functools.partial(dispatch_kernel, plan=plan), out_shape=[...  108 us
    pallas_call x1, Pallas kernels, run_experts(): pl.pallas_call(functools.partial(expert_kernel, split=split, plan=plan),...  57.3 us
    dot_general x6, matrix products, dot(): return jnp.dot(a, b, preferred_element_type=out)  33.3 us
    pallas_call x1, Pallas kernels, unit_grads(): pl.pallas_call(unit_grads_kernel, grid=(units, features // step), in_spec...  31.5 us
    unnamed x104, local copies, waits for them, and re-layouts  29.2 us
  transfers between devices with their start and end apart: 11, of which 2 were waited for; matrix products, arithmetic and copies ran while one was open for 12% of the time, Pallas kernels for 44%

profile of v5, /device:TPU:0, one launch (start us, length us, event | category | flops | bytes accessed | tf_op | source)
XLA Modules:
  0.0 849.2 jit_solution(14333595145012492740)
XLA Ops:
  10.1 1.0 pad_maximum_fusion
  12.0 1.0 copy-done.8
  13.1 1.0 copy-done.9
  14.1 1.0 copy-done.11
  15.1 0.9 copy-done.12
  17.0 132.9 %shard_map.305 = (f32[8,8,512]{2,1,0:T(8,128)S(1)}, bf16[8,4,64,640]{3,2,1,0:T(8,128)(2,1)S(1)}, bf16[2048,768]{1,0:T(8,128)(2,1)}, bf16[512,1024]{1,0:T(8,128)(...) custom-call(bf16[2,64,2048]{2,1,0:T(8,128)(2,1)S(1)} %copy-done.9, ...), custom_call_target="tpu_custom_call" | custom-call | flops 120000004096 | bytes 120000000 | tf_op jit(solution)/shard_map/pallas_call | solution.py:448
  149.9 1.4 copy-done.4
  151.3 1.3 copy-done.14
  152.6 1.3 copy-done.16
  153.9 1.0 copy-done.18
  156.4 4.6 all-to-all-start
  162.8 1.2 multiply_sine_fusion
  164.7 1.4 slice.81.router
  166.3 5.0 fusion.21.query
  171.3 8.2 fusion.8.keys
  180.2 17.8 %shard_map.306 = (bf16[512,1024]{1,0:T(8,128)(2,1)}, bf16[512,512]{1,0:T(8,128)(2,1)}, f32[2,4,256,2]{3,2,1,0:T(8,128)}) custom-call(f32[512,768]{1,0:T(8,128)} %fusion.21.query, f32[256,32]{1,0:T(8,128)} %get-tuple-element.195.cosine, f32[256,32]{1,0:T(8,128)} %get-tuple-element.194.sine, bf16[4096,1024]{1,0:T(8,128)(2,1)} %fusion.8.keys, ...), custom_call_target="tpu_custom_call" | custom-call | flops 16000000000 | bytes 16000000 | tf_op jit(solution)/shard_map/pallas_call | solution.py:573
  198.0 1.4 slice_reduce_fusion
  199.5 4.4 fusion.22
  203.9 108.1 %shard_map.307 = (f32[128,2048]{1,0:T(8,128)S(1)}, f32[128,64]{1,0:T(8,128)S(1)}, bf16[128,2048]{1,0:T(8,128)(2,1)}, bf16[2,2,2,64,2048]{4,3,2,1,0:T(8,128)(2,1)...) custom-call(bf16[2,2,2,64,2048]{4,3,2,1,0:T(8,128)(2,1)} %bitcast.145, ...), custom_call_target="tpu_custom_call" | custom-call | flops 80000000000 | bytes 80000000 | tf_op jit(solution)/shard_map/pallas_call | solution.py:1177
  312.0 1.0 copy-done.21
  315.4 57.3 %shard_map.308 = (bf16[8,4,2,16,2176]{4,3,2,1,0:T(8,128)(2,1)}, bf16[8,4,2,16,2048]{4,3,2,1,0:T(8,128)(2,1)}, bf16[2,512,1408]{2,1,0:T(8,128)(2,1)}, bf16[2,512,1408]{2,1,0:T(8,128)(2,1)}, bf16[2,512,1408]{2,1,0:T(8,128)(2,1)}) custom-call(bf16[8,4,2,16,2176]{4,3,2,1,0:T(8,128)(2,1)} %get-tuple-element.95.rows_in.rows, ...), custom_call_target="tpu_custom_call" | custom-call | flops 80000000000 | bytes 80000000 | tf_op jit(solution)/shard_map/pallas_call | solution.py:1575
  372.8 5.3 fusion.23
  378.1 4.6 fusion.24
  382.8 6.0 multiply_convert_fusion
  389.6 3.2 fusion.25
  392.9 4.3 fusion.33
  397.2 3.5 fusion.28.rest_0_
  400.7 1.1 copy-done.39
  401.8 5.1 fusion.27
  406.9 2.1 fusion.26
  409.0 3.3 add_convert_fusion
  412.3 127.0 %shard_map.309 = (f32[128,2048]{1,0:T(8,128)}, bf16[2,2,2,64,2048]{4,3,2,1,0:T(8,128)(2,1)}, bf16[128,64]{1,0:T(8,128)(2,1)}, f32[1,2048]{1,0:T(1,128)}, bf16[2,...) custom-call(bf16[8,4,2,16,2176]{4,3,2,1,0:T(8,128)(2,1)} %get-tuple-element.105.returned, ...), custom_call_target="tpu_custom_call" | custom-call | flops 99999997952 | bytes 100000000 | tf_op jit(solution)/shard_map/pallas_call | solution.py:1336
  539.4 4.8 all-to-all-start.1
  544.2 1.1 copy.54
  545.4 2.6 fusion.32.rest_2_
  548.0 2.1 fusion.29.grads
  550.1 1.9 convert_element_type.115
  552.0 28.8 %shard_map.310 = (bf16[512,768]{1,0:T(8,128)(2,1)}, bf16[4096,1024]{1,0:T(8,128)(2,1)}, f32[2,2048,128]{2,1,0:T(8,128)}) custom-call(bf16[512,1024]{1,0:T(8,128)(2,1)} %get-tuple-element.87.query, f32[256,32]{1,0:T(8,128)} %get-tuple-element.195.cosine, f32[256,32]{1,0:T(8,128)} %get-tuple-element.194.sine, bf16[4096,1024]{1,0:T(8,128)(2,1)} %fusion.8.keys, ...), custom_call_target="tpu_custom_call" | custom-call | flops 24999999488 | bytes 25000000 | tf_op jit(solution)/shard_map/pallas_call | solution.py:594
  580.8 4.1 fusion.30
  585.7 2.6 copy-done.41
  588.6 7.0 fusion.6
  596.3 2.0 fusion.18
  598.3 1.8 copy.70
  600.9 1.0 copy-done.27
  602.7 1.7 collective-permute-start.1
  604.4 8.5 fusion.1.rest_1_
  612.8 20.4 %reduce-scatter.5.cloned.1.call-done = bf16[704,256]{1,0:T(8,128)(2,1)} async-done(((bf16[704,2048]{1,0:T(8,128)(2,1)}), bf16[704,256]{1,0:T(8,128)(2,1)}) %reduce-scatter.5.cloned.1.call-update) | async-done | bytes 360464 | tf_op jit(solution)/shard_map/reduce_scatter | solution.py:1800
  633.2 1.9 convert_element_type.129
  635.1 4.9 fusion.31.rest_0_
  640.0 0.9 fusion.10.hidden_sum
  640.9 4.2 fusion
  645.1 2.5 slice_bitcast_fusion
  647.6 1.5 collective-permute-start.3
  649.1 31.5 %shard_map.311 = (f32[2,2048,1408]{2,1,0:T(8,128)}, f32[2,2048,1408]{2,1,0:T(8,128)}, f32[2,1408,2048]{2,1,0:T(8,128)}) custom-call(bf16[8,4,2,16,2176]{4,3,2,1,0:T(8,128)(2,1)} %get-tuple-element.95.rows_in.rows, bf16[8,4,2,16,2048]{4,3,2,1,0:T(8,128)(2,1)} %all-to-all-done.grads_in.grads, bf16[2,512,1408]{2,1,0:T(8,128)(2,1)} %get-tuple-element.119.gated, ...), custom_call_target="tpu_custom_call" | custom-call | flops 35000000512 | bytes 35000000 | tf_op jit(solution)/shard_map/pallas_call | solution.py:1627
  680.6 2.5 copy.50
  683.1 4.1 copy.51
  687.2 1.9 constant_dynamic-slice_fusion.1
  689.1 1.9 constant_dynamic-slice_fusion
  691.0 2.8 fusion.3.latent_partial
  693.7 136.0 %shard_map.312 = (bf16[2,64,2048]{2,1,0:T(8,128)(2,1)}, bf16[2,64,2048]{2,1,0:T(8,128)(2,1)}, f32[4,64,640]{2,1,0:T(8,128)}, f32[4,8,768]{2,1,0:T(8,128)}, f32[2...) custom-call(bf16[2,64,2048]{2,1,0:T(8,128)(2,1)} %fusion.10.hidden_sum, ...), custom_call_target="tpu_custom_call" | custom-call | flops 190000005120 | bytes 190000000 | tf_op jit(solution)/shard_map/pallas_call | solution.py:998
  829.8 1.4 slice_reduce_fusion.3
  833.3 1.0 slice.90
  835.0 2.2 copy.60
  837.2 1.9 copy.79
  (163 shorter events, 21.3 us)
Async XLA Ops:
  7.2 365.6 %all-gather.4.cloned.1.call-start = ((), (), s32[]{:S(2)}) async-start(), calls=%async_computation.4 | async-start | bytes 3244032 | tf_op jit(solution)/shard_map/all_gather | solution.py:1742
  11.8 138.1 %copy-start.5 = (f32[128,32]{1,0:T(8,128)}, f32[128,32]{1,0:T(8,128)S(1)}, u32[]{:S(2)}) copy-start(f32[128,32]{1,0:T(8,128)S(1)} %get-tuple-element.196.sine) | copy-start | bytes 49156
  11.8 138.1 %copy-start.6 = (f32[128,32]{1,0:T(8,128)}, f32[128,32]{1,0:T(8,128)S(1)}, u32[]{:S(2)}) copy-start(f32[128,32]{1,0:T(8,128)S(1)} %get-tuple-element.197.cosine) | copy-start | bytes 49156
  12.0 1.0 copy-start.8
  13.1 1.0 copy-start.9
  14.1 1.0 copy-start.11
  15.1 0.9 copy-start.12
  16.1 0.9 copy-start.13
  149.9 1.5 copy-start.4
  151.3 1.3 copy-start.14
  152.6 1.3 copy-start.16
  153.9 1.0 copy-start.18
  154.9 0.7 copy-start.23
  155.6 10.6 %copy-start = (bf16[2,2,2,64,2048]{4,3,2,1,0:T(8,128)(2,1)}, bf16[2,2,2,64,2048]{4,3,2,1,0:T(8,128)(2,1)S(1)}, u32[]{:S(2)}) copy-start(bf16[2,2,2,64,2048]{4,3,2,1,0:T(8,128)(2,1)S(1)} %get-tuple-element.83) | copy-start | bytes 6291460
  155.6 48.3 %copy-start.22 = (bf16[4,128,256]{2,1,0:T(8,128)(2,1)}, bf16[4,128,256]{2,1,0:T(8,128)(2,1)S(1)}, u32[]{:S(2)}) copy-start(bf16[4,128,256]{2,1,0:T(8,128)(2,1)S(1)} %get-tuple-element.94.picks) | copy-start | bytes 786436
  155.7 222.4 %all-gather.8.cloned.1.call-start = ((), (), s32[]{:S(2)}) async-start(), calls=%async_computation.6 | async-start | bytes 3244032 | tf_op jit(solution)/shard_map/all_gather | solution.py:1741
  156.4 159.0 %all-to-all-start = ((bf16[8,4,2,16,2048]{4,3,2,1,0:T(8,128)(2,1)}), bf16[8,4,2,16,2048]{4,3,2,1,0:T(8,128)(2,1)}, u32[]{:S(2)}, u32[]{:S(2)}) async-start(bf16[8,4,2,16,2048]{4,3,2,1,0:T(8,128)(2,1)} %get-tuple-element.97), calls=%async_computation | async-start | bytes 8388608 | tf_op jit(solution)/shard_map/all_to_all | solution.py:1762
  161.0 221.8 %all-gather.6.cloned.1.call-start = ((), (), s32[]{:S(2)}) async-start(), calls=%async_computation.5 | async-start | bytes 3244032 | tf_op jit(solution)/shard_map/all_gather | solution.py:1740
  161.7 388.4 %reduce-scatter.3.cloned.1.call-start = ((), (), s32[]{:S(2)}) async-start(), calls=%async_computation.7 | async-start | bytes 3244032 | tf_op jit(solution)/shard_map/reduce_scatter | solution.py:1800
  164.7 39.2 %copy-start.7 = (f32[8,1,256]{2,1,0:T(1,128)}, f32[8,1,256]{2,1,0:T(1,128)S(1)}, u32[]{:S(2)}) copy-start(f32[8,1,256]{2,1,0:T(1,128)S(1)} %get-tuple-element.193) | copy-start | bytes 24580
  164.7 6.6 slice-start
  166.1 37.8 %copy-start.3 = (bf16[2048,64]{1,0:T(8,128)(2,1)}, bf16[2048,64]{1,0:T(8,128)(2,1)S(1)}, u32[]{:S(2)}) copy-start(bf16[2048,64]{1,0:T(8,128)(2,1)S(1)} %slice.81.router) | copy-start | bytes 786436
  166.3 5.0 copy-start.19
  166.3 5.0 slice-start.1
  199.5 4.4 copy-start.10
  312.0 1.0 copy-start.21
  313.0 0.6 copy-start.24
  313.6 83.6 %copy-start.2 = (bf16[2,2,2,64,2048]{4,3,2,1,0:T(8,128)(2,1)}, bf16[2,2,2,64,2048]{4,3,2,1,0:T(8,128)(2,1)S(1)}, u32[]{:S(2)}) copy-start(bf16[2,2,2,64,2048]{4,3,2,1,0:T(8,128)(2,1)S(1)} %get-tuple-element.99) | copy-start | bytes 6291460
  382.8 6.8 copy-start.15
  388.8 0.9 copy-start.38
  400.7 1.1 copy-start.39
  401.8 5.1 copy-start.29
  406.9 2.1 copy-start.36
  406.9 2.1 copy-start.42
  539.3 4.9 copy-start.32
  539.3 6.0 copy-start.37
  539.3 6.0 copy-start.40
  539.4 105.7 %all-to-all-start.1 = ((bf16[8,4,2,16,2048]{4,3,2,1,0:T(8,128)(2,1)}), bf16[8,4,2,16,2048]{4,3,2,1,0:T(8,128)(2,1)}, u32[]{:S(2)}, u32[]{:S(2)}) async-start(bf16[8,4,2,16,2048]{4,3,2,1,0:T(8,128)(2,1)} %get-tuple-element.116), calls=%async_computation.2 | async-start | bytes 8388608 | tf_op jit(solution)/shard_map/all_to_all | solution.py:1762
  544.2 89.0 %reduce-scatter.5.cloned.1.call-start = ((), (), s32[]{:S(2)}) async-start(), calls=%async_computation.8 | async-start | bytes 3244032 | tf_op jit(solution)/shard_map/reduce_scatter | solution.py:1800
  545.4 2.6 copy-start.17
  580.8 4.1 copy-start.30
  584.9 3.5 copy-start.41
  585.1 3.6 copy-start.20
  585.3 15.1 %collective-permute-start = (bf16[2,2,64,2048]{3,2,0,1:T(8,128)(2,1)S(1)}, bf16[2,2,64,2048]{3,2,0,1:T(8,128)(2,1)S(1)}, u32[]{:S(2)}, u32[]{:S(2)}) collective-permute-start(bf16[2,2,64,2048]{3,2,0,1:T(8,128)(2,1)S(1)} %bitcast.120), channel_id=1, source_target_pairs={{0,1},{1,0},{2,3},{3,2},{4,5},{5,4},{6,7},{7,6},{8,9},{9,8},{10,11... | collective-permute-start | bytes 3145736 | tf_op jit(solution)/shard_map/ppermute | solution.py:79
  598.3 6.0 slice-start.2
  598.3 6.0 slice-start.3
  600.1 40.8 %collective-permute-start.2 = (bf16[2,2,2,4,64,640]{5,4,3,2,0,1:T(8,128)(2,1)}, bf16[2,2,2,4,64,640]{5,4,3,2,0,1:T(8,128)(2,1)}, u32[]{:S(2)}, u32[]{:S(2)}) collective-permute-start(bf16[2,2,2,4,64,640]{5,4,3,2,0,1:T(8,128)(2,1)} %bitcast.96), channel_id=1, source_target_pairs={{0,1},{1,0},{2,3},{3,2},{4,5},{5,4},{6,7},{7,6},{8,9},{9,8},{10,11... | collective-permute-start | bytes 7864328 | tf_op jit(solution)/shard_map/ppermute | solution.py:79
  600.9 1.0 copy-start.27
  602.7 32.4 %copy-start.1 = (bf16[2,2,2,64,2048]{4,3,2,1,0:T(8,128)(2,1)S(1)}, bf16[2,2,2,64,2048]{4,3,2,1,0:T(8,128)(2,1)}, u32[]{:S(2)}) copy-start(bf16[2,2,2,64,2048]{4,3,2,1,0:T(8,128)(2,1)} %copy-done) | copy-start | bytes 6291460
  602.7 37.3 %collective-permute-start.1 = (bf16[2,64,2048]{2,1,0:T(8,128)(2,1)}, bf16[2,64,2048]{2,1,0:T(8,128)(2,1)S(1)}, u32[]{:S(2)}, u32[]{:S(2)}) collective-permute-start(bf16[2,64,2048]{2,1,0:T(8,128)(2,1)} %slice_bitcast_fusion.2), channel_id=1, source_target_pairs={{0,2},{2,0},{1,3},{3,1},{4,6},{6,4},{5,7},{7,5},{8,10},{10,8},{9,1... | collective-permute-start | bytes 1572872 | tf_op jit(solution)/shard_map/ppermute | solution.py:79
  635.1 4.9 copy-start.28
  635.1 5.8 copy-start.25
  647.6 43.4 %collective-permute-start.3 = (bf16[2,2,4,64,640]{4,3,2,1,0:T(8,128)(2,1)}, bf16[2,2,4,64,640]{4,3,2,1,0:T(8,128)(2,1)}, u32[]{:S(2)}, u32[]{:S(2)}) collective-permute-start(bf16[2,2,4,64,640]{4,3,2,1,0:T(8,128)(2,1)} %slice_bitcast_fusion), channel_id=1, source_target_pairs={{0,2},{2,0},{1,3},{3,1},{4,6},{6,4},{5,7},{7,5},{8,10},{10,8},{9,1... | collective-permute-start | bytes 3932168 | tf_op jit(solution)/shard_map/ppermute | solution.py:79
  683.1 7.8 copy-start.26
  829.8 9.3 %copy-start.34 = (bf16[2,64,2048]{2,1,0:T(8,128)(2,1)S(1)}, bf16[2,64,2048]{2,1,0:T(8,128)(2,1)}, u32[]{:S(2)}) copy-start(bf16[2,64,2048]{2,1,0:T(8,128)(2,1)} %get-tuple-element.252) | copy-start | bytes 1572868
  829.8 10.1 %copy-start.31 = (f32[256,768]{1,0:T(8,128)S(1)}, f32[256,768]{1,0:T(8,128)}, u32[]{:S(2)}) copy-start(f32[256,768]{1,0:T(8,128)} %get-tuple-element.254) | copy-start | bytes 2359300
  834.3 6.5 copy-start.35
  835.0 6.4 copy-start.33
Sparse Core Ops, SparseCore 0:
  155.8 88.4 all-gather.3
  246.3 76.5 all-gather.7
  324.9 57.8 all-gather.5
  400.8 95.6 reduce-scatter.2
  550.2 82.9 reduce-scatter.4
